TPU v7x, 128 devices: a whole 4x4x4 slice. The times are simulated.
128 devices in a mesh: feat: 32 (over z, x, core), conf: 4 (over y).
Axes of the slice: x: 4, y: 4, z: 4, core: 2. Of those that a mesh axis runs over, the one named last changes fastest.
Arguments:
- matrix: float32 [32768, 20480], P('conf', 'feat'), may hold values from -3 to 3
- targets: float32 [32, 32768], P(None, 'conf'), may hold values from -40 to 40
Outputs:
- solution: float32 [32, 20480], P(None, 'feat')
- residual: float32 [32, 32768], P(None, 'conf')
All inputs are finite; a program needn't handle non-finite values.
Results may differ from a plain program's by a relative error of at most 0.00016.
Values sent between devices are 32-bit elements; how exact they have to be, the bound alone decides.
No kernel may reach another device: no remote copies, remote signals or barrier semaphores. Data moves between devices by JAX's collectives and lax.ppermute only.
A program may use at most 128 MiB of HBM per device.

v0:
```python
import functools

import jax
import jax.numpy as jnp
from jax import lax
from jax.experimental import pallas as pl
from jax.experimental.pallas import tpu as pltpu
from jax.sharding import PartitionSpec as P

BF, F32 = jnp.bfloat16, jnp.float32
MEMBERS = 32
PIECES = 4
PAD = 128
VMEM = pl.BlockSpec(memory_space=pltpu.VMEM)
ANY = pl.BlockSpec(memory_space=pl.ANY)


def params(mib):
    return pltpu.CompilerParams(vmem_limit_bytes=mib << 20)


def pin(x):
    return pltpu.with_memory_space_constraint(x, pltpu.VMEM)


def far(x):
    return pltpu.with_memory_space_constraint(x, pltpu.HBM)


def place(other):
    f = lax.axis_index("feat")
    z, x, core = f // 8, f // 2 % 4, f % 2
    return core ^ other, jnp.where((core ^ other) == 0, z, x)


def split(x, parts):
    out = []
    for _ in range(parts - 1):
        high = x.astype(BF)
        out.append(high)
        x = x - high.astype(F32)
    return out + [x.astype(BF)]


def fold(product, parts):
    n = product.shape[1] // 2
    rows = sum(product[MEMBERS * j : MEMBERS * (j + 1)] for j in range(parts))
    return rows[:, :n] + rows[:, n:]


def first_kernel(
    blocks, depth, chunk, parts, r_hbm, m_hbm, pair_ref, g_ref, r_ref, m_buf, acc_ref, r_sem, m_sem
):
    rows, n = m_hbm.shape
    block = rows // blocks

    def copy(i):
        slot = lax.rem(i, depth)
        at = pl.ds(pl.multiple_of(i * block, block), block)
        return pltpu.make_async_copy(m_hbm.at[at], m_buf.at[slot], m_sem.at[slot])

    vectors = pltpu.make_async_copy(r_hbm, r_ref, r_sem)
    copy(0).start()
    vectors.start()
    for i in range(1, depth):
        copy(i).start()
    acc_ref[...] = jnp.zeros_like(acc_ref)
    vectors.wait()

    def step(i, carry):
        copy(i).wait()
        slot = lax.rem(i, depth)
        for k in range(0, block, chunk):
            at = pl.ds(pl.multiple_of(i * block + k, chunk), chunk)
            pair = jnp.concatenate(split(m_buf[slot, k : k + chunk, :], 2), axis=1)
            pair_ref[at, :] = pair
            r = jnp.concatenate(split(r_ref[:, at], parts), axis=0)
            acc_ref[...] += jnp.dot(r, pair, preferred_element_type=F32)

        @pl.when(i + depth < blocks)
        def _():
            copy(i + depth).start()

        return carry

    lax.fori_loop(0, blocks, step, 0)
    g_ref[...] = fold(acc_ref[...], parts)


def first(residual, matrix, blocks=8, depth=3, chunk=512, parts=3):
    rows, n = matrix.shape
    return pl.pallas_call(
        functools.partial(first_kernel, blocks, depth, chunk, parts),
        in_specs=[ANY, ANY],
        out_specs=[VMEM, VMEM],
        out_shape=[pltpu.VMEM((rows, 2 * n), BF), pltpu.VMEM((MEMBERS, n), F32)],
        scratch_shapes=[
            pltpu.VMEM(residual.shape, F32),
            pltpu.VMEM((depth, rows // blocks, n), F32),
            pltpu.VMEM((MEMBERS * parts, 2 * n), F32),
            pltpu.SemaphoreType.DMA,
            pltpu.SemaphoreType.DMA((depth,)),
        ],
        compiler_params=params(20),
    )(far(residual), far(matrix))


def rows_body(half, start, d, pair_ref, out_ref, w_ref):
    n = d.shape[1]
    piece = out_ref.shape[2] - PAD
    t = jnp.concatenate([x.astype(F32) for x in split(d, 2)], axis=0).T.astype(BF)
    w_ref[:n, :] = t
    w_ref[n:, :] = t
    chunk = 512
    norm = jnp.broadcast_to(jnp.sum(d * d, axis=1, keepdims=True), (MEMBERS, PAD))
    for q in range(PIECES):
        slot = lax.rem(q - start + PIECES, PIECES)
        for r in range(0, piece, chunk):
            at = pl.multiple_of((half * PIECES + q) * piece + r, chunk)
            o = jnp.dot(
                pair_ref[pl.ds(at, chunk), :], w_ref[...], preferred_element_type=F32
            ).T
            out_ref[slot, :, r : r + chunk] = o[:MEMBERS] + o[MEMBERS:]
        out_ref[slot, :, piece:] = norm


def rows_kernel(other, d_ref, pair_ref, out_ref, w_ref):
    rows_body(*place(other), d_ref[...], pair_ref, out_ref, w_ref)


def rows_first_kernel(other, a, b, c, d, pair_ref, out_ref, g_ref, w_ref):
    g = (a[...] + d[...]) + (b[...] + c[...])
    g_ref[...] = g
    rows_body(*place(other), g, pair_ref, out_ref, w_ref)


def rows_second_kernel(
    other, a, b, c, d, g0_ref, gamma_ref, pair_ref, out_ref, g_ref, alpha_ref, w_ref
):
    w = (a[...] + d[...]) + (b[...] + c[...])
    n = g0_ref.shape[1]
    alpha = gamma_ref[...] / w[:, n:]
    alpha_ref[...] = alpha
    g = g0_ref[...] - alpha[:, :1] * w[:, :n]
    g_ref[...] = g
    rows_body(*place(other), g, pair_ref, out_ref, w_ref)


def by_rows(kernel, other, operands, pair, more):
    rows, n2 = pair.shape
    piece = rows // (2 * PIECES)
    return pl.pallas_call(
        functools.partial(kernel, other),
        in_specs=[VMEM] * (len(operands) + 1),
        out_specs=[VMEM] * (1 + len(more)),
        out_shape=[pltpu.VMEM((PIECES, MEMBERS, piece + PAD), F32)]
        + [pltpu.VMEM(s, F32) for s in more],
        scratch_shapes=[pltpu.VMEM((n2, 2 * MEMBERS), BF)],
        compiler_params=params(16),
    )(*map(pin, operands), pin(pair))


def cols_body(half, start, pieces, pair_ref, parts):
    piece = pieces[0].shape[1]
    acc = jnp.zeros((MEMBERS * parts, pair_ref.shape[1]), F32)
    norm = jnp.zeros((MEMBERS, 1), F32)
    for i, p in enumerate(pieces):
        q = lax.rem(start - ORDER[i] + PIECES, PIECES)
        at = pl.multiple_of((half * PIECES + q) * piece, piece)
        vectors = jnp.concatenate(split(p, parts), axis=0)
        acc += jnp.dot(vectors, pair_ref[pl.ds(at, piece), :], preferred_element_type=F32)
        norm += jnp.sum(p * p, axis=1, keepdims=True)
    return fold(acc, parts), norm


def cols_own_kernel(parts, a, b, c, d, pair_ref, w_ref):
    w, norm = cols_body(*place(0), [a[...], b[...], c[...], d[...]], pair_ref, parts)
    n = w.shape[1]
    w_ref[:, :n] = w
    w_ref[:, n:] = jnp.broadcast_to(norm, (MEMBERS, PAD))


def cols_other_kernel(parts, p_ref, before_ref, pair_ref, w_ref):
    w, norm = cols_body(*place(1), [p_ref[i] for i in range(PIECES)], pair_ref, parts)
    n = w.shape[1]
    w_ref[:, :n] = before_ref[:, :n] + w
    w_ref[:, n:] = before_ref[:, n:] + norm


def by_cols(kernel, operands, pair, parts=3):
    n = pair.shape[1] // 2
    return pl.pallas_call(
        functools.partial(kernel, parts),
        in_specs=[VMEM] * (len(operands) + 1),
        out_specs=VMEM,
        out_shape=pltpu.VMEM((MEMBERS, n + PAD), F32),
        compiler_params=params(16),
    )(*map(pin, operands), pin(pair))


def ring(stage):
    def moved(f, k):
        z, x, core = f // 8, f // 2 % 4, f % 2
        if core == stage:
            z = (z + k) % 4
        else:
            x = (x + k) % 4
        return z * 8 + x * 2 + core

    return [[(f, moved(f, k)) for f in range(32)] for k in (1, 2, 3)]


CORE = [(f, f ^ 1) for f in range(32)]
CONF = [[(c, (c + k) % 4) for c in range(4)] for k in (1, 2, 3)]


def three(xs, axis, perms):
    return [lax.ppermute(x, axis, perm) for x, perm in zip(xs, perms)]


ORDER = (0, 1, 3, 2)


def opposite_last(x):
    return [x[k] for k in ORDER]


def total(own, others):
    return (others[0] + others[2]) + (own + others[1])


def reduce_pieces(keep, send):
    got = lax.ppermute(send, "feat", CORE)
    mine = [keep[i] + got[i] for i in range(PIECES)]
    a, b, c, d = [mine[0]] + three(mine[1:], "feat", ring(0))
    piece = (b + d) + (a + c)
    return total(piece, three([piece] * 3, "feat", ring(1)))


def gather_pieces(piece):
    own = opposite_last([piece] + three([piece] * 3, "feat", ring(0)))
    return own, jnp.stack(own)


def finish_kernel(*refs):
    r0_ref, alpha0_ref, gamma0_ref, gamma1_ref, own_ref, other_ref = refs[:6]
    p_own, p_other, i_own, i_other = refs[6:10], refs[10], refs[11:15], refs[15]
    g0_ref, g1_ref, sol_ref, res_ref = refs[16:]
    gamma1 = gamma1_ref[:, :1]
    a0 = alpha0_ref[:, :1]
    a1 = gamma1 / (own_ref[:, :1] + other_ref[:, :1])
    b0 = gamma1 / gamma0_ref[:, :1]
    g0 = g0_ref[...]
    sol_ref[...] = a0 * g0 + a1 * (g1_ref[...] + b0 * g0)
    piece = p_own[0].shape[1]
    for far_half in range(2):
        half, start = place(far_half)
        for i in range(PIECES):
            q = lax.rem(start - ORDER[i] + PIECES, PIECES)
            at = pl.ds(pl.multiple_of((half * PIECES + q) * piece, piece), piece)
            p = p_other[i] if far_half else p_own[i][...]
            image = i_other[i] if far_half else i_own[i][...]
            res_ref[:, at] = r0_ref[:, at] - a0 * p - a1 * image


def body(matrix, targets):
    rows, n = matrix.shape
    piece = rows // (2 * PIECES)

    pair, part = first(targets, matrix)
    parts = opposite_last([part] + three([part] * 3, "conf", CONF))

    send, g0 = by_rows(rows_first_kernel, 1, parts, pair, [(MEMBERS, n)])
    (keep,) = by_rows(rows_kernel, 0, [g0], pair, [])
    p = reduce_pieces(keep, send)
    gamma0 = p[:, piece:]
    p = p[:, :piece]
    p_own, stacked = gather_pieces(p)
    p_other = lax.ppermute(stacked, "feat", CORE)

    w = by_cols(cols_own_kernel, p_own, pair)
    w = by_cols(cols_other_kernel, [p_other, w], pair)
    parts = opposite_last([w] + three([w] * 3, "conf", CONF))

    send, g1, alpha0 = by_rows(
        rows_second_kernel, 1, parts + [g0, gamma0], pair, [(MEMBERS, n), (MEMBERS, PAD)]
    )
    (keep,) = by_rows(rows_kernel, 0, [g1], pair, [])
    image = reduce_pieces(keep, send)
    gamma1 = image[:, piece:]
    beta = gamma1 / gamma0
    image = image[:, :piece] + beta[:, :1] * p
    i_own, stacked = gather_pieces(image)
    i_other = lax.ppermute(stacked, "feat", CORE)

    curve = sum(jnp.sum(v * v, axis=1, keepdims=True) for v in i_own)
    curve = jnp.broadcast_to(curve, (MEMBERS, PAD))
    curve = total(curve, three([curve] * 3, "conf", CONF))
    curve_other = lax.ppermute(curve, "feat", CORE)

    return pl.pallas_call(
        finish_kernel,
        in_specs=[VMEM] * 18,
        out_specs=[VMEM, VMEM],
        out_shape=[
            jax.ShapeDtypeStruct((MEMBERS, n), F32),
            jax.ShapeDtypeStruct((MEMBERS, rows), F32),
        ],
        compiler_params=params(16),
    )(
        targets,
        alpha0,
        gamma0,
        gamma1,
        curve,
        curve_other,
        *p_own,
        p_other,
        *i_own,
        i_other,
        g0,
        g1,
    )


def solution(mesh):
    placed = (P("conf", "feat"), P(None, "conf"))
    return jax.shard_map(
        body,
        mesh=mesh,
        in_specs=placed,
        out_specs=(P(None, "feat"), P(None, "conf")),
        check_vma=False,
    )
```

profile of v0, /device:TPU:0, one launch (start us, length us, event | category | flops | bytes accessed | tf_op | source)
XLA Modules:
  0.0 113.5 jit_solution(17281440137078502681)
XLA Ops:
  0.6 9.1 %shard_map.41 = (bf16[8192,1280]{1,0:T(8,128)(2,1)S(1)}, f32[32,640]{1,0:T(8,128)S(1)}) custom-call(f32[32,8192]{1,0:T(8,128)} %refs_0_.1, f32[8192,640]{1,0:T(8,128)} %m_hbm.1), custom_call_target="tpu_custom_call" | custom-call | tf_op jit(solution)/shard_map/pallas_call | solution.py:92
  9.7 3.4 %collective-permute-start.2 = (f32[32,640]{1,0:T(8,128)S(1)}, f32[32,640]{1,0:T(8,128)S(1)}, u32[]{:S(2)}, u32[]{:S(2)}) collective-permute-start(f32[32,640]{1,0:T(8,128)S(1)} %get-tuple-element.9.a), channel_id=1, source_target_pairs={{0,2},{1,3},{2,0},{3,1},{4,6},{5,7},{6,4},{7,5},{8,10},{9,11},{10,... | collective-permute-start | bytes 245768 | tf_op jit(solution)/shard_map/ppermute | solution.py:218
  13.1 1.1 collective-permute-start.1
  14.1 1.0 collective-permute-start
  15.8 2.1 %collective-permute-done.1.c = f32[32,640]{1,0:T(8,128)S(1)} collective-permute-done((f32[32,640]{1,0:T(8,128)S(1)}, f32[32,640]{1,0:T(8,128)S(1)}, u32[]{:S(2)}, u32[]{:S(2)}) %collective-permute-start.1) | collective-permute-done | bytes 81952 | tf_op jit(solution)/shard_map/ppermute | solution.py:218
  17.9 1.9 %collective-permute-done.b = f32[32,640]{1,0:T(8,128)S(1)} collective-permute-done((f32[32,640]{1,0:T(8,128)S(1)}, f32[32,640]{1,0:T(8,128)S(1)}, u32[]{:S(2)}, u32[]{:S(2)}) %collective-permute-start) | collective-permute-done | bytes 81952 | tf_op jit(solution)/shard_map/ppermute | solution.py:218
  19.8 3.1 %shard_map.42 = (f32[4,32,1152]{2,1,0:T(8,128)S(1)}, f32[32,640]{1,0:T(8,128)S(1)}) custom-call(f32[32,640]{1,0:T(8,128)S(1)} %get-tuple-element.9.a, f32[32,640]{1,0:T(8,128)S(1)} %collective-permute-done.b, f32[32,640]{1,0:T(8,128)S(1)} %collective-permute-done.1.c, f32[32,640]{1,0:T(8,128)S(1)} %collective-permute-done.2.d, ...), custom_call_target="tpu_custom_call" | custom-call | tf_op jit(solution)/shard_map/pallas_call | solution.py:152
  23.0 3.1 %shard_map.43 = f32[4,32,1152]{2,1,0:T(8,128)S(1)} custom-call(f32[32,640]{1,0:T(8,128)S(1)} %get-tuple-element.11.d_ref.g0_ref.refs_16_, bf16[8192,1280]{1,0:T(8,128)(2,1)S(1)} %get-tuple-element.10.pair_ref), custom_call_target="tpu_custom_call" | custom-call | tf_op jit(solution)/shard_map/pallas_call | solution.py:152
  26.1 4.1 %collective-permute-start.5 = (f32[32,1152]{1,0:T(8,128)S(1)}, f32[32,1152]{1,0:T(8,128)S(1)}, u32[]{:S(2)}, u32[]{:S(2)}) collective-permute-start(f32[32,1152]{1,0:T(8,128)S(1)} %get-tuple-element.21), channel_id=1, source_target_pairs={{0,96},{4,28},{8,104},{12,4},{16,112},{20,12},{24,120},{28,20},{32... | collective-permute-start | bytes 442376 | tf_op jit(solution)/shard_map/ppermute | solution.py:218
  30.2 1.3 %collective-permute-start.4 = (f32[32,1152]{1,0:T(8,128)S(1)}, f32[32,1152]{1,0:T(8,128)S(1)}, u32[]{:S(2)}, u32[]{:S(2)}) collective-permute-start(f32[32,1152]{1,0:T(8,128)S(1)} %get-tuple-element.23), channel_id=1, source_target_pairs={{0,32},{4,12},{8,40},{12,20},{16,48},{20,28},{24,56},{28,4},{32,64... | collective-permute-start | bytes 442376 | tf_op jit(solution)/shard_map/ppermute | solution.py:218
  31.4 3.0 %collective-permute-done.5 = f32[32,1152]{1,0:T(8,128)S(1)} collective-permute-done((f32[32,1152]{1,0:T(8,128)S(1)}, f32[32,1152]{1,0:T(8,128)S(1)}, u32[]{:S(2)}, u32[]{:S(2)}) %collective-permute-start.5) | collective-permute-done | bytes 147488 | tf_op jit(solution)/shard_map/ppermute | solution.py:218
  34.5 2.5 %collective-permute-done.6 = f32[32,1152]{1,0:T(8,128)S(1)} collective-permute-done((f32[32,1152]{1,0:T(8,128)S(1)}, f32[32,1152]{1,0:T(8,128)S(1)}, u32[]{:S(2)}, u32[]{:S(2)}) %collective-permute-start.6) | collective-permute-done | bytes 147488 | tf_op jit(solution)/shard_map/ppermute | solution.py:218
  36.9 1.2 %collective-permute-done.4 = f32[32,1152]{1,0:T(8,128)S(1)} collective-permute-done((f32[32,1152]{1,0:T(8,128)S(1)}, f32[32,1152]{1,0:T(8,128)S(1)}, u32[]{:S(2)}, u32[]{:S(2)}) %collective-permute-start.4) | collective-permute-done | bytes 147488 | tf_op jit(solution)/shard_map/ppermute | solution.py:218
  38.2 3.1 %collective-permute-start.9 = (f32[32,1152]{1,0:T(8,128)S(1)}, f32[32,1152]{1,0:T(8,128)S(1)}, u32[]{:S(2)}, u32[]{:S(2)}) collective-permute-start(f32[32,1152]{1,0:T(8,128)S(1)} %fusion.9), channel_id=1, source_target_pairs={{0,16},{4,68},{8,24},{12,76},{16,0},{20,84},{24,8},{28,92},{32,48}... | collective-permute-start | bytes 442376 | tf_op jit(solution)/shard_map/ppermute | solution.py:218
  41.3 1.2 %collective-permute-start.8 = (f32[32,1152]{1,0:T(8,128)S(1)}, f32[32,1152]{1,0:T(8,128)S(1)}, u32[]{:S(2)}, u32[]{:S(2)}) collective-permute-start(f32[32,1152]{1,0:T(8,128)S(1)} %fusion.9), channel_id=1, source_target_pairs={{0,24},{4,100},{8,0},{12,108},{16,8},{20,116},{24,16},{28,124},{32... | collective-permute-start | bytes 442376 | tf_op jit(solution)/shard_map/ppermute | solution.py:218
  42.4 0.9 collective-permute-start.7
  43.3 1.6 %collective-permute-done.9 = f32[32,1152]{1,0:T(8,128)S(1)} collective-permute-done((f32[32,1152]{1,0:T(8,128)S(1)}, f32[32,1152]{1,0:T(8,128)S(1)}, u32[]{:S(2)}, u32[]{:S(2)}) %collective-permute-start.9) | collective-permute-done | bytes 147488 | tf_op jit(solution)/shard_map/ppermute | solution.py:218
  44.9 1.7 %collective-permute-done.8 = f32[32,1152]{1,0:T(8,128)S(1)} collective-permute-done((f32[32,1152]{1,0:T(8,128)S(1)}, f32[32,1152]{1,0:T(8,128)S(1)}, u32[]{:S(2)}, u32[]{:S(2)}) %collective-permute-start.8) | collective-permute-done | bytes 147488 | tf_op jit(solution)/shard_map/ppermute | solution.py:218
  46.6 2.2 %collective-permute-done.7 = f32[32,1152]{1,0:T(8,128)S(1)} collective-permute-done((f32[32,1152]{1,0:T(8,128)S(1)}, f32[32,1152]{1,0:T(8,128)S(1)}, u32[]{:S(2)}, u32[]{:S(2)}) %collective-permute-start.7) | collective-permute-done | bytes 147488 | tf_op jit(solution)/shard_map/ppermute | solution.py:218
  48.8 0.8 collective-permute-start.12
  50.4 1.3 %collective-permute-start.10 = (f32[32,1024]{1,0:T(8,128)S(1)}, f32[32,1024]{1,0:T(8,128)S(1)}, u32[]{:S(2)}, u32[]{:S(2)}) collective-permute-start(f32[32,1024]{1,0:T(8,128)S(1)} %get-tuple-element.25.a.refs_6_), channel_id=1, source_target_pairs={{0,32},{4,12},{8,40},{12,20},{16,48},{20,28},{24,56},{28,4},{32,64... | collective-permute-start | bytes 393224 | tf_op jit(solution)/shard_map/ppermute | solution.py:218
  51.7 3.7 %collective-permute-done.12.d.refs_9_ = f32[32,1024]{1,0:T(8,128)S(1)} collective-permute-done((f32[32,1024]{1,0:T(8,128)S(1)}, f32[32,1024]{1,0:T(8,128)S(1)}, u32[]{:S(2)}, u32[]{:S(2)}) %collective-permute-start.12) | collective-permute-done | bytes 131104 | tf_op jit(solution)/shard_map/ppermute | solution.py:218
  55.4 1.4 %collective-permute-done.10.b.refs_7_ = f32[32,1024]{1,0:T(8,128)S(1)} collective-permute-done((f32[32,1024]{1,0:T(8,128)S(1)}, f32[32,1024]{1,0:T(8,128)S(1)}, u32[]{:S(2)}, u32[]{:S(2)}) %collective-permute-start.10) | collective-permute-done | bytes 131104 | tf_op jit(solution)/shard_map/ppermute | solution.py:218
  57.1 1.8 %shard_map.44.before_ref = f32[32,768]{1,0:T(8,128)S(1)} custom-call(f32[32,1024]{1,0:T(8,128)S(1)} %get-tuple-element.25.a.refs_6_, f32[32,1024]{1,0:T(8,128)S(1)} %collective-permute-done.10.b.refs_7_, f32[32,1024]{1,0:T(8,128)S(1)} %collective-permute-done.11.c.refs_8_, f32[32,1024]{1,0:T(8,128)S(1)} %collective-permute-done.12.d.refs_9_, ...), custom_call_target="tpu_custom_call" | custom-call | tf_op jit(solution)/shard_map/pallas_call | solution.py:192
  59.0 1.8 %shard_map.45.a = f32[32,768]{1,0:T(8,128)S(1)} custom-call(f32[4,32,1024]{2,1,0:T(8,128)S(1)} %collective-permute-done.13.p_ref.refs_10_, f32[32,768]{1,0:T(8,128)S(1)} %shard_map.44.before_ref, bf16[8192,1280]{1,0:T(8,128)(2,1)S(1)} %get-tuple-element.10.pair_ref), custom_call_target="tpu_custom_call" | custom-call | tf_op jit(solution)/shard_map/pallas_call | solution.py:192
  60.8 0.8 collective-permute-start.16
  61.6 1.7 %collective-permute-start.15 = (f32[32,768]{1,0:T(8,128)S(1)}, f32[32,768]{1,0:T(8,128)S(1)}, u32[]{:S(2)}, u32[]{:S(2)}) collective-permute-start(f32[32,768]{1,0:T(8,128)S(1)} %shard_map.45.a), channel_id=1, source_target_pairs={{0,3},{1,0},{2,1},{3,2},{4,7},{5,4},{6,5},{7,6},{8,11},{9,8},{10,9... | collective-permute-start | bytes 294920 | tf_op jit(solution)/shard_map/ppermute | solution.py:218
  63.6 4.3 %collective-permute-done.16.d = f32[32,768]{1,0:T(8,128)S(1)} collective-permute-done((f32[32,768]{1,0:T(8,128)S(1)}, f32[32,768]{1,0:T(8,128)S(1)}, u32[]{:S(2)}, u32[]{:S(2)}) %collective-permute-start.16) | collective-permute-done | bytes 98336 | tf_op jit(solution)/shard_map/ppermute | solution.py:218
  68.0 1.6 %collective-permute-done.14.b = f32[32,768]{1,0:T(8,128)S(1)} collective-permute-done((f32[32,768]{1,0:T(8,128)S(1)}, f32[32,768]{1,0:T(8,128)S(1)}, u32[]{:S(2)}, u32[]{:S(2)}) %collective-permute-start.14) | collective-permute-done | bytes 98336 | tf_op jit(solution)/shard_map/ppermute | solution.py:218
  69.6 3.1 %shard_map.46 = (f32[4,32,1152]{2,1,0:T(8,128)S(1)}, f32[32,640]{1,0:T(8,128)S(1)}, f32[32,128]{1,0:T(8,128)S(1)}) custom-call(f32[32,768]{1,0:T(8,128)S(1)} %shard_map.45.a, f32[32,768]{1,0:T(8,128)S(1)} %collective-permute-done.14.b, f32[32,768]{1,0:T(8,128)S(1)} %collective-permute-done.15.c, f32[32,768]{1,0:T(8,128)S(1)} %collective-permute-done.16.d, ...), custom_call_target="tpu_custom_call" | custom-call | tf_op jit(solution)/shard_map/pallas_call | solution.py:152
  72.8 3.1 %shard_map.47 = f32[4,32,1152]{2,1,0:T(8,128)S(1)} custom-call(f32[32,640]{1,0:T(8,128)S(1)} %get-tuple-element.14.d_ref.refs_17_, bf16[8192,1280]{1,0:T(8,128)(2,1)S(1)} %get-tuple-element.10.pair_ref), custom_call_target="tpu_custom_call" | custom-call | tf_op jit(solution)/shard_map/pallas_call | solution.py:152
  76.0 1.3 %collective-permute-start.19 = (f32[32,1152]{1,0:T(8,128)S(1)}, f32[32,1152]{1,0:T(8,128)S(1)}, u32[]{:S(2)}, u32[]{:S(2)}) collective-permute-start(f32[32,1152]{1,0:T(8,128)S(1)} %get-tuple-element.18), channel_id=1, source_target_pairs={{0,96},{4,28},{8,104},{12,4},{16,112},{20,12},{24,120},{28,20},{32... | collective-permute-start | bytes 442376 | tf_op jit(solution)/shard_map/ppermute | solution.py:218
  78.4 2.8 %collective-permute-done.19 = f32[32,1152]{1,0:T(8,128)S(1)} collective-permute-done((f32[32,1152]{1,0:T(8,128)S(1)}, f32[32,1152]{1,0:T(8,128)S(1)}, u32[]{:S(2)}, u32[]{:S(2)}) %collective-permute-start.19) | collective-permute-done | bytes 147488 | tf_op jit(solution)/shard_map/ppermute | solution.py:218
  81.2 2.8 %collective-permute-done.20 = f32[32,1152]{1,0:T(8,128)S(1)} collective-permute-done((f32[32,1152]{1,0:T(8,128)S(1)}, f32[32,1152]{1,0:T(8,128)S(1)}, u32[]{:S(2)}, u32[]{:S(2)}) %collective-permute-start.20) | collective-permute-done | bytes 147488 | tf_op jit(solution)/shard_map/ppermute | solution.py:218
  84.0 1.5 %collective-permute-done.18 = f32[32,1152]{1,0:T(8,128)S(1)} collective-permute-done((f32[32,1152]{1,0:T(8,128)S(1)}, f32[32,1152]{1,0:T(8,128)S(1)}, u32[]{:S(2)}, u32[]{:S(2)}) %collective-permute-start.18) | collective-permute-done | bytes 147488 | tf_op jit(solution)/shard_map/ppermute | solution.py:218
  86.3 1.6 %collective-permute-start.22 = (f32[32,1152]{1,0:T(8,128)S(1)}, f32[32,1152]{1,0:T(8,128)S(1)}, u32[]{:S(2)}, u32[]{:S(2)}) collective-permute-start(f32[32,1152]{1,0:T(8,128)S(1)} %fusion.3), channel_id=1, source_target_pairs={{0,24},{4,100},{8,0},{12,108},{16,8},{20,116},{24,16},{28,124},{32... | collective-permute-start | bytes 442376 | tf_op jit(solution)/shard_map/ppermute | solution.py:218
  88.3 3.9 %collective-permute-done.23 = f32[32,1152]{1,0:T(8,128)S(1)} collective-permute-done((f32[32,1152]{1,0:T(8,128)S(1)}, f32[32,1152]{1,0:T(8,128)S(1)}, u32[]{:S(2)}, u32[]{:S(2)}) %collective-permute-start.23) | collective-permute-done | bytes 147488 | tf_op jit(solution)/shard_map/ppermute | solution.py:218
  92.2 2.0 %collective-permute-done.21 = f32[32,1152]{1,0:T(8,128)S(1)} collective-permute-done((f32[32,1152]{1,0:T(8,128)S(1)}, f32[32,1152]{1,0:T(8,128)S(1)}, u32[]{:S(2)}, u32[]{:S(2)}) %collective-permute-start.21) | collective-permute-done | bytes 147488 | tf_op jit(solution)/shard_map/ppermute | solution.py:218
  94.6 0.8 collective-permute-start.26
  95.4 1.2 %collective-permute-start.25 = (f32[32,1024]{1,0:T(8,128)S(1)}, f32[32,1024]{1,0:T(8,128)S(1)}, u32[]{:S(2)}, u32[]{:S(2)}) collective-permute-start(f32[32,1024]{1,0:T(8,128)S(1)} %get-tuple-element.17.refs_11_), channel_id=1, source_target_pairs={{0,96},{4,28},{8,104},{12,4},{16,112},{20,12},{24,120},{28,20},{32... | collective-permute-start | bytes 393224 | tf_op jit(solution)/shard_map/ppermute | solution.py:218
  96.7 0.8 collective-permute-start.24
  97.5 3.7 %collective-permute-done.26.refs_14_ = f32[32,1024]{1,0:T(8,128)S(1)} collective-permute-done((f32[32,1024]{1,0:T(8,128)S(1)}, f32[32,1024]{1,0:T(8,128)S(1)}, u32[]{:S(2)}, u32[]{:S(2)}) %collective-permute-start.26) | collective-permute-done | bytes 131104 | tf_op jit(solution)/shard_map/ppermute | solution.py:218
  101.2 1.6 %collective-permute-done.24.refs_12_ = f32[32,1024]{1,0:T(8,128)S(1)} collective-permute-done((f32[32,1024]{1,0:T(8,128)S(1)}, f32[32,1024]{1,0:T(8,128)S(1)}, u32[]{:S(2)}, u32[]{:S(2)}) %collective-permute-start.24) | collective-permute-done | bytes 131104 | tf_op jit(solution)/shard_map/ppermute | solution.py:218
  104.2 1.7 %collective-permute-start.28 = (f32[32,128]{1,0:T(8,128)S(1)}, f32[32,128]{1,0:T(8,128)S(1)}, u32[]{:S(2)}, u32[]{:S(2)}) collective-permute-start(f32[32,128]{1,0:T(8,128)S(1)} %broadcast_in_dim.2), channel_id=1, source_target_pairs={{0,3},{1,0},{2,1},{3,2},{4,7},{5,4},{6,5},{7,6},{8,11},{9,8},{10,9... | collective-permute-start | bytes 49160 | tf_op jit(solution)/shard_map/ppermute | solution.py:218
  106.2 2.5 %collective-permute-done.29 = f32[32,128]{1,0:T(8,128)S(1)} collective-permute-done((f32[32,128]{1,0:T(8,128)S(1)}, f32[32,128]{1,0:T(8,128)S(1)}, u32[]{:S(2)}, u32[]{:S(2)}) %collective-permute-start.29) | collective-permute-done | bytes 16416 | tf_op jit(solution)/shard_map/ppermute | solution.py:218
  108.7 2.2 %collective-permute-done.27 = f32[32,128]{1,0:T(8,128)S(1)} collective-permute-done((f32[32,128]{1,0:T(8,128)S(1)}, f32[32,128]{1,0:T(8,128)S(1)}, u32[]{:S(2)}, u32[]{:S(2)}) %collective-permute-start.27) | collective-permute-done | bytes 16416 | tf_op jit(solution)/shard_map/ppermute | solution.py:218
  111.0 1.2 %collective-permute-done.30.refs_5_ = f32[32,128]{1,0:T(8,128)S(1)} collective-permute-done((f32[32,128]{1,0:T(8,128)S(1)}, f32[32,128]{1,0:T(8,128)S(1)}, u32[]{:S(2)}, u32[]{:S(2)}) %collective-permute-start.30) | collective-permute-done | bytes 16416 | tf_op jit(solution)/shard_map/ppermute | solution.py:299
  112.2 1.3 %shard_map.48 = (f32[32,640]{1,0:T(8,128)}, f32[32,8192]{1,0:T(8,128)}) custom-call(f32[32,8192]{1,0:T(8,128)S(1)} %copy-done, f32[32,128]{1,0:T(8,128)S(1)} %get-tuple-element.13.refs_1_, f32[32,128]{1,0:T(8,128)S(1)} %slice.93.gamma_ref.refs_2_, f32[32,128]{1,0:T(8,128)S(1)} %slice.102.refs_3_, f32[32,128]{1,0:T(8,128)S(1)} %add_add_fusion.2.refs_4_, ...), custom_call_target="tpu_custom_call" | custom-call | tf_op jit(solution)/shard_map/pallas_call | solution.py:301
  (45 shorter events, 7.0 us)
Async XLA Ops:
  9.7 6.0 %collective-permute-start.2 = (f32[32,640]{1,0:T(8,128)S(1)}, f32[32,640]{1,0:T(8,128)S(1)}, u32[]{:S(2)}, u32[]{:S(2)}) collective-permute-start(f32[32,640]{1,0:T(8,128)S(1)} %get-tuple-element.9.a), channel_id=1, source_target_pairs={{0,2},{1,3},{2,0},{3,1},{4,6},{5,7},{6,4},{7,5},{8,10},{9,11},{10,... | collective-permute-start | bytes 245768 | tf_op jit(solution)/shard_map/ppermute | solution.py:218
  13.1 4.8 %collective-permute-start.1 = (f32[32,640]{1,0:T(8,128)S(1)}, f32[32,640]{1,0:T(8,128)S(1)}, u32[]{:S(2)}, u32[]{:S(2)}) collective-permute-start(f32[32,640]{1,0:T(8,128)S(1)} %get-tuple-element.9.a), channel_id=1, source_target_pairs={{0,3},{1,0},{2,1},{3,2},{4,7},{5,4},{6,5},{7,6},{8,11},{9,8},{10,9... | collective-permute-start | bytes 245768 | tf_op jit(solution)/shard_map/ppermute | solution.py:218
  14.1 5.7 %collective-permute-start = (f32[32,640]{1,0:T(8,128)S(1)}, f32[32,640]{1,0:T(8,128)S(1)}, u32[]{:S(2)}, u32[]{:S(2)}) collective-permute-start(f32[32,640]{1,0:T(8,128)S(1)} %get-tuple-element.9.a), channel_id=1, source_target_pairs={{0,1},{1,2},{2,3},{3,0},{4,5},{5,6},{6,7},{7,4},{8,9},{9,10},{10,1... | collective-permute-start | bytes 245768 | tf_op jit(solution)/shard_map/ppermute | solution.py:218
  22.9 3.2 %collective-permute-start.3 = (f32[4,32,1152]{2,1,0:T(8,128)S(1)}, f32[4,32,1152]{2,1,0:T(8,128)S(1)}, u32[]{:S(2)}, u32[]{:S(2)}) collective-permute-start(f32[4,32,1152]{2,1,0:T(8,128)S(1)} %get-tuple-element.12), channel_id=1, source_target_pairs={{0,4},{4,0},{8,12},{12,8},{16,20},{20,16},{24,28},{28,24},{32,36},... | collective-permute-start | bytes 1769480 | tf_op jit(solution)/shard_map/ppermute | solution.py:233
  26.1 8.4 %collective-permute-start.5 = (f32[32,1152]{1,0:T(8,128)S(1)}, f32[32,1152]{1,0:T(8,128)S(1)}, u32[]{:S(2)}, u32[]{:S(2)}) collective-permute-start(f32[32,1152]{1,0:T(8,128)S(1)} %get-tuple-element.21), channel_id=1, source_target_pairs={{0,96},{4,28},{8,104},{12,4},{16,112},{20,12},{24,120},{28,20},{32... | collective-permute-start | bytes 442376 | tf_op jit(solution)/shard_map/ppermute | solution.py:218
  30.2 6.8 %collective-permute-start.6 = (f32[32,1152]{1,0:T(8,128)S(1)}, f32[32,1152]{1,0:T(8,128)S(1)}, u32[]{:S(2)}, u32[]{:S(2)}) collective-permute-start(f32[32,1152]{1,0:T(8,128)S(1)} %get-tuple-element.22), channel_id=1, source_target_pairs={{0,64},{4,20},{8,72},{12,28},{16,80},{20,4},{24,88},{28,12},{32,96... | collective-permute-start | bytes 442376 | tf_op jit(solution)/shard_map/ppermute | solution.py:218
  30.2 7.9 %collective-permute-start.4 = (f32[32,1152]{1,0:T(8,128)S(1)}, f32[32,1152]{1,0:T(8,128)S(1)}, u32[]{:S(2)}, u32[]{:S(2)}) collective-permute-start(f32[32,1152]{1,0:T(8,128)S(1)} %get-tuple-element.23), channel_id=1, source_target_pairs={{0,32},{4,12},{8,40},{12,20},{16,48},{20,28},{24,56},{28,4},{32,64... | collective-permute-start | bytes 442376 | tf_op jit(solution)/shard_map/ppermute | solution.py:218
  38.2 6.7 %collective-permute-start.9 = (f32[32,1152]{1,0:T(8,128)S(1)}, f32[32,1152]{1,0:T(8,128)S(1)}, u32[]{:S(2)}, u32[]{:S(2)}) collective-permute-start(f32[32,1152]{1,0:T(8,128)S(1)} %fusion.9), channel_id=1, source_target_pairs={{0,16},{4,68},{8,24},{12,76},{16,0},{20,84},{24,8},{28,92},{32,48}... | collective-permute-start | bytes 442376 | tf_op jit(solution)/shard_map/ppermute | solution.py:218
  41.3 5.3 %collective-permute-start.8 = (f32[32,1152]{1,0:T(8,128)S(1)}, f32[32,1152]{1,0:T(8,128)S(1)}, u32[]{:S(2)}, u32[]{:S(2)}) collective-permute-start(f32[32,1152]{1,0:T(8,128)S(1)} %fusion.9), channel_id=1, source_target_pairs={{0,24},{4,100},{8,0},{12,108},{16,8},{20,116},{24,16},{28,124},{32... | collective-permute-start | bytes 442376 | tf_op jit(solution)/shard_map/ppermute | solution.py:218
  42.4 6.4 %collective-permute-start.7 = (f32[32,1152]{1,0:T(8,128)S(1)}, f32[32,1152]{1,0:T(8,128)S(1)}, u32[]{:S(2)}, u32[]{:S(2)}) collective-permute-start(f32[32,1152]{1,0:T(8,128)S(1)} %fusion.9), channel_id=1, source_target_pairs={{0,8},{4,36},{8,16},{12,44},{16,24},{20,52},{24,0},{28,60},{32,40}... | collective-permute-start | bytes 442376 | tf_op jit(solution)/shard_map/ppermute | solution.py:218
  48.8 6.6 %collective-permute-start.12 = (f32[32,1024]{1,0:T(8,128)S(1)}, f32[32,1024]{1,0:T(8,128)S(1)}, u32[]{:S(2)}, u32[]{:S(2)}) collective-permute-start(f32[32,1024]{1,0:T(8,128)S(1)} %get-tuple-element.25.a.refs_6_), channel_id=1, source_target_pairs={{0,64},{4,20},{8,72},{12,28},{16,80},{20,4},{24,88},{28,12},{32,96... | collective-permute-start | bytes 393224 | tf_op jit(solution)/shard_map/ppermute | solution.py:218
  49.7 5.8 %collective-permute-start.11 = (f32[32,1024]{1,0:T(8,128)S(1)}, f32[32,1024]{1,0:T(8,128)S(1)}, u32[]{:S(2)}, u32[]{:S(2)}) collective-permute-start(f32[32,1024]{1,0:T(8,128)S(1)} %get-tuple-element.25.a.refs_6_), channel_id=1, source_target_pairs={{0,96},{4,28},{8,104},{12,4},{16,112},{20,12},{24,120},{28,20},{32... | collective-permute-start | bytes 393224 | tf_op jit(solution)/shard_map/ppermute | solution.py:218
  50.4 6.4 %collective-permute-start.10 = (f32[32,1024]{1,0:T(8,128)S(1)}, f32[32,1024]{1,0:T(8,128)S(1)}, u32[]{:S(2)}, u32[]{:S(2)}) collective-permute-start(f32[32,1024]{1,0:T(8,128)S(1)} %get-tuple-element.25.a.refs_6_), channel_id=1, source_target_pairs={{0,32},{4,12},{8,40},{12,20},{16,48},{20,28},{24,56},{28,4},{32,64... | collective-permute-start | bytes 393224 | tf_op jit(solution)/shard_map/ppermute | solution.py:218
  56.8 2.2 %collective-permute-start.13 = (f32[4,32,1024]{2,1,0:T(8,128)S(1)}, f32[4,32,1024]{2,1,0:T(8,128)S(1)}, u32[]{:S(2)}, u32[]{:S(2)}) collective-permute-start(f32[4,32,1024]{2,1,0:T(8,128)S(1)} %pad_maximum_fusion), channel_id=1, source_target_pairs={{0,4},{4,0},{8,12},{12,8},{16,20},{20,16},{24,28},{28,24},{32,36},... | collective-permute-start | bytes 1572872 | tf_op jit(solution)/shard_map/ppermute | solution.py:279
  60.8 7.2 %collective-permute-start.16 = (f32[32,768]{1,0:T(8,128)S(1)}, f32[32,768]{1,0:T(8,128)S(1)}, u32[]{:S(2)}, u32[]{:S(2)}) collective-permute-start(f32[32,768]{1,0:T(8,128)S(1)} %shard_map.45.a), channel_id=1, source_target_pairs={{0,2},{1,3},{2,0},{3,1},{4,6},{5,7},{6,4},{7,5},{8,10},{9,11},{10,... | collective-permute-start | bytes 294920 | tf_op jit(solution)/shard_map/ppermute | solution.py:218
  61.6 6.4 %collective-permute-start.15 = (f32[32,768]{1,0:T(8,128)S(1)}, f32[32,768]{1,0:T(8,128)S(1)}, u32[]{:S(2)}, u32[]{:S(2)}) collective-permute-start(f32[32,768]{1,0:T(8,128)S(1)} %shard_map.45.a), channel_id=1, source_target_pairs={{0,3},{1,0},{2,1},{3,2},{4,7},{5,4},{6,5},{7,6},{8,11},{9,8},{10,9... | collective-permute-start | bytes 294920 | tf_op jit(solution)/shard_map/ppermute | solution.py:218
  63.3 6.3 %collective-permute-start.14 = (f32[32,768]{1,0:T(8,128)S(1)}, f32[32,768]{1,0:T(8,128)S(1)}, u32[]{:S(2)}, u32[]{:S(2)}) collective-permute-start(f32[32,768]{1,0:T(8,128)S(1)} %shard_map.45.a), channel_id=1, source_target_pairs={{0,1},{1,2},{2,3},{3,0},{4,5},{5,6},{6,7},{7,4},{8,9},{9,10},{10,1... | collective-permute-start | bytes 294920 | tf_op jit(solution)/shard_map/ppermute | solution.py:218
  63.6 48.5 %copy-start = (f32[32,8192]{1,0:T(8,128)S(1)}, f32[32,8192]{1,0:T(8,128)}, u32[]{:S(2)}) copy-start(f32[32,8192]{1,0:T(8,128)} %refs_0_.1) | copy-start | bytes 3145732
  72.7 3.2 %collective-permute-start.17 = (f32[4,32,1152]{2,1,0:T(8,128)S(1)}, f32[4,32,1152]{2,1,0:T(8,128)S(1)}, u32[]{:S(2)}, u32[]{:S(2)}) collective-permute-start(f32[4,32,1152]{2,1,0:T(8,128)S(1)} %get-tuple-element.15), channel_id=1, source_target_pairs={{0,4},{4,0},{8,12},{12,8},{16,20},{20,16},{24,28},{28,24},{32,36},... | collective-permute-start | bytes 1769480 | tf_op jit(solution)/shard_map/ppermute | solution.py:233
  76.0 5.2 %collective-permute-start.19 = (f32[32,1152]{1,0:T(8,128)S(1)}, f32[32,1152]{1,0:T(8,128)S(1)}, u32[]{:S(2)}, u32[]{:S(2)}) collective-permute-start(f32[32,1152]{1,0:T(8,128)S(1)} %get-tuple-element.18), channel_id=1, source_target_pairs={{0,96},{4,28},{8,104},{12,4},{16,112},{20,12},{24,120},{28,20},{32... | collective-permute-start | bytes 442376 | tf_op jit(solution)/shard_map/ppermute | solution.py:218
  77.2 6.8 %collective-permute-start.20 = (f32[32,1152]{1,0:T(8,128)S(1)}, f32[32,1152]{1,0:T(8,128)S(1)}, u32[]{:S(2)}, u32[]{:S(2)}) collective-permute-start(f32[32,1152]{1,0:T(8,128)S(1)} %get-tuple-element.19), channel_id=1, source_target_pairs={{0,64},{4,20},{8,72},{12,28},{16,80},{20,4},{24,88},{28,12},{32,96... | collective-permute-start | bytes 442376 | tf_op jit(solution)/shard_map/ppermute | solution.py:218
  78.0 7.5 %collective-permute-start.18 = (f32[32,1152]{1,0:T(8,128)S(1)}, f32[32,1152]{1,0:T(8,128)S(1)}, u32[]{:S(2)}, u32[]{:S(2)}) collective-permute-start(f32[32,1152]{1,0:T(8,128)S(1)} %get-tuple-element.20), channel_id=1, source_target_pairs={{0,32},{4,12},{8,40},{12,20},{16,48},{20,28},{24,56},{28,4},{32,64... | collective-permute-start | bytes 442376 | tf_op jit(solution)/shard_map/ppermute | solution.py:218
  85.5 6.7 %collective-permute-start.23 = (f32[32,1152]{1,0:T(8,128)S(1)}, f32[32,1152]{1,0:T(8,128)S(1)}, u32[]{:S(2)}, u32[]{:S(2)}) collective-permute-start(f32[32,1152]{1,0:T(8,128)S(1)} %fusion.3), channel_id=1, source_target_pairs={{0,16},{4,68},{8,24},{12,76},{16,0},{20,84},{24,8},{28,92},{32,48}... | collective-permute-start | bytes 442376 | tf_op jit(solution)/shard_map/ppermute | solution.py:218
  86.3 5.9 %collective-permute-start.22 = (f32[32,1152]{1,0:T(8,128)S(1)}, f32[32,1152]{1,0:T(8,128)S(1)}, u32[]{:S(2)}, u32[]{:S(2)}) collective-permute-start(f32[32,1152]{1,0:T(8,128)S(1)} %fusion.3), channel_id=1, source_target_pairs={{0,24},{4,100},{8,0},{12,108},{16,8},{20,116},{24,16},{28,124},{32... | collective-permute-start | bytes 442376 | tf_op jit(solution)/shard_map/ppermute | solution.py:218
  87.9 6.4 %collective-permute-start.21 = (f32[32,1152]{1,0:T(8,128)S(1)}, f32[32,1152]{1,0:T(8,128)S(1)}, u32[]{:S(2)}, u32[]{:S(2)}) collective-permute-start(f32[32,1152]{1,0:T(8,128)S(1)} %fusion.3), channel_id=1, source_target_pairs={{0,8},{4,36},{8,16},{12,44},{16,24},{20,52},{24,0},{28,60},{32,40}... | collective-permute-start | bytes 442376 | tf_op jit(solution)/shard_map/ppermute | solution.py:218
  94.6 6.5 %collective-permute-start.26 = (f32[32,1024]{1,0:T(8,128)S(1)}, f32[32,1024]{1,0:T(8,128)S(1)}, u32[]{:S(2)}, u32[]{:S(2)}) collective-permute-start(f32[32,1024]{1,0:T(8,128)S(1)} %get-tuple-element.17.refs_11_), channel_id=1, source_target_pairs={{0,64},{4,20},{8,72},{12,28},{16,80},{20,4},{24,88},{28,12},{32,96... | collective-permute-start | bytes 393224 | tf_op jit(solution)/shard_map/ppermute | solution.py:218
  95.4 5.7 %collective-permute-start.25 = (f32[32,1024]{1,0:T(8,128)S(1)}, f32[32,1024]{1,0:T(8,128)S(1)}, u32[]{:S(2)}, u32[]{:S(2)}) collective-permute-start(f32[32,1024]{1,0:T(8,128)S(1)} %get-tuple-element.17.refs_11_), channel_id=1, source_target_pairs={{0,96},{4,28},{8,104},{12,4},{16,112},{20,12},{24,120},{28,20},{32... | collective-permute-start | bytes 393224 | tf_op jit(solution)/shard_map/ppermute | solution.py:218
  96.7 6.2 %collective-permute-start.24 = (f32[32,1024]{1,0:T(8,128)S(1)}, f32[32,1024]{1,0:T(8,128)S(1)}, u32[]{:S(2)}, u32[]{:S(2)}) collective-permute-start(f32[32,1024]{1,0:T(8,128)S(1)} %get-tuple-element.17.refs_11_), channel_id=1, source_target_pairs={{0,32},{4,12},{8,40},{12,20},{16,48},{20,28},{24,56},{28,4},{32,64... | collective-permute-start | bytes 393224 | tf_op jit(solution)/shard_map/ppermute | solution.py:218
  102.9 9.3 %collective-permute-start.31 = (f32[4,32,1024]{2,1,0:T(8,128)S(1)}, f32[4,32,1024]{2,1,0:T(8,128)S(1)}, u32[]{:S(2)}, u32[]{:S(2)}) collective-permute-start(f32[4,32,1024]{2,1,0:T(8,128)S(1)} %pad_maximum_fusion.1), channel_id=1, source_target_pairs={{0,4},{4,0},{8,12},{12,8},{16,20},{20,16},{24,28},{28,24},{32,36},... | collective-permute-start | bytes 1572872 | tf_op jit(solution)/shard_map/ppermute | solution.py:294
  103.4 5.3 %collective-permute-start.29 = (f32[32,128]{1,0:T(8,128)S(1)}, f32[32,128]{1,0:T(8,128)S(1)}, u32[]{:S(2)}, u32[]{:S(2)}) collective-permute-start(f32[32,128]{1,0:T(8,128)S(1)} %broadcast_in_dim.2), channel_id=1, source_target_pairs={{0,2},{1,3},{2,0},{3,1},{4,6},{5,7},{6,4},{7,5},{8,10},{9,11},{10,... | collective-permute-start | bytes 49160 | tf_op jit(solution)/shard_map/ppermute | solution.py:218
  104.2 4.5 %collective-permute-start.28 = (f32[32,128]{1,0:T(8,128)S(1)}, f32[32,128]{1,0:T(8,128)S(1)}, u32[]{:S(2)}, u32[]{:S(2)}) collective-permute-start(f32[32,128]{1,0:T(8,128)S(1)} %broadcast_in_dim.2), channel_id=1, source_target_pairs={{0,3},{1,0},{2,1},{3,2},{4,7},{5,4},{6,5},{7,6},{8,11},{9,8},{10,9... | collective-permute-start | bytes 49160 | tf_op jit(solution)/shard_map/ppermute | solution.py:218
  105.9 4.9 %collective-permute-start.27 = (f32[32,128]{1,0:T(8,128)S(1)}, f32[32,128]{1,0:T(8,128)S(1)}, u32[]{:S(2)}, u32[]{:S(2)}) collective-permute-start(f32[32,128]{1,0:T(8,128)S(1)} %broadcast_in_dim.2), channel_id=1, source_target_pairs={{0,1},{1,2},{2,3},{3,0},{4,5},{5,6},{6,7},{7,4},{8,9},{9,10},{10,1... | collective-permute-start | bytes 49160 | tf_op jit(solution)/shard_map/ppermute | solution.py:218
  110.9 1.2 %collective-permute-start.30 = (f32[32,128]{1,0:T(8,128)S(1)}, f32[32,128]{1,0:T(8,128)S(1)}, u32[]{:S(2)}, u32[]{:S(2)}) collective-permute-start(f32[32,128]{1,0:T(8,128)S(1)} %add_add_fusion.2.refs_4_), channel_id=1, source_target_pairs={{0,4},{4,0},{8,12},{12,8},{16,20},{20,16},{24,28},{28,24},{32,36},... | collective-permute-start | bytes 49160 | tf_op jit(solution)/shard_map/ppermute | solution.py:299
where the time goes:
time: 115 us; the launch traced here: 113 us
  waiting for transfers between devices  52.2 us (45%)
  starting transfers between devices  33 us (29%)
  Pallas kernels  26.3 us (23%)
    ppermute x27, waiting for transfers between devices, three(): return [lax.ppermute(x, axis, perm) for x, perm in zip(xs, perms)]  51 us
    ppermute x27, starting transfers between devices, three(): return [lax.ppermute(x, axis, perm) for x, perm in zip(xs, perms)]  32.4 us
    pallas_call x4, Pallas kernels, by_rows(): pl.pallas_call(functools.partial(kernel, other), in_specs=[VMEM] * (len(o...  12.3 us
    pallas_call x1, Pallas kernels, first(): pl.pallas_call(functools.partial(first_kernel, blocks, depth, chunk, part...  9.09 us
    pallas_call x2, Pallas kernels, by_cols(): pl.pallas_call(functools.partial(kernel, parts), in_specs=[VMEM] * (len(o...  3.56 us
  transfers between devices with their start and end apart: 32, of which 24 were waited for; matrix products, arithmetic and copies ran while one was open for 0% of the time, Pallas kernels for 7%

commit v1 on v0

v1 whole, which is shorter than its diff:
```python
import functools

import jax
import jax.numpy as jnp
from jax import lax
from jax.experimental import pallas as pl
from jax.experimental.pallas import tpu as pltpu
from jax.sharding import PartitionSpec as P

BF, F32 = jnp.bfloat16, jnp.float32
MEMBERS = 32
PIECES = 4
LANES = 128
TAIL = 8
VMEM = pl.BlockSpec(memory_space=pltpu.VMEM)
ANY = pl.BlockSpec(memory_space=pl.ANY)


def params(mib):
    return pltpu.CompilerParams(vmem_limit_bytes=mib << 20)


def pin(x):
    return pltpu.with_memory_space_constraint(x, pltpu.VMEM)


def far(x):
    return pltpu.with_memory_space_constraint(x, pltpu.HBM)


def place(other):
    f = lax.axis_index("feat")
    z, x, core = f // 8, f // 2 % 4, f % 2
    return core ^ other, jnp.where((core ^ other) == 0, z, x)


def split(x, parts):
    out = []
    for _ in range(parts - 1):
        high = x.astype(BF)
        out.append(high)
        x = x - high.astype(F32)
    return out + [x.astype(BF)]


def fold(product, parts):
    n = product.shape[1] // 2
    rows = sum(product[MEMBERS * j : MEMBERS * (j + 1)] for j in range(parts))
    return rows[:, :n] + rows[:, n:]


def strips(packed_ref, width):
    at = range(0, width // LANES * MEMBERS, MEMBERS)
    return jnp.concatenate([packed_ref[i : i + MEMBERS, :] for i in at], axis=1)


def put(packed_ref, values, first=0):
    for j in range(values.shape[1] // LANES):
        at = (first + j) * MEMBERS
        packed_ref[at : at + MEMBERS, :] = values[:, j * LANES : (j + 1) * LANES]


def put_sums(packed_ref, column):
    groups = MEMBERS // TAIL
    blocks = [column[TAIL * k : TAIL * (k + 1)] for k in range(groups)]
    blocks = [jnp.broadcast_to(b, (TAIL, LANES // groups)) for b in blocks]
    packed_ref[packed_ref.shape[0] - TAIL :, :] = jnp.concatenate(blocks, axis=1)


def sums_of(packed):
    groups = MEMBERS // TAIL
    block, width = packed[packed.shape[0] - TAIL :, :], LANES // groups
    return jnp.concatenate(
        [block[:, k * width : k * width + 1] for k in range(groups)], axis=0
    )


def wide(column):
    return jnp.broadcast_to(column, (MEMBERS, LANES))


def first_kernel(
    blocks, depth, chunk, parts, r_hbm, m_hbm, pair_ref, g_ref, r_ref, m_buf, acc_ref, r_sem, m_sem
):
    rows, n = m_hbm.shape
    block = rows // blocks

    def copy(i):
        slot = lax.rem(i, depth)
        at = pl.ds(pl.multiple_of(i * block, block), block)
        return pltpu.make_async_copy(m_hbm.at[at], m_buf.at[slot], m_sem.at[slot])

    vectors = pltpu.make_async_copy(r_hbm, r_ref, r_sem)
    copy(0).start()
    vectors.start()
    for i in range(1, depth):
        copy(i).start()
    acc_ref[...] = jnp.zeros_like(acc_ref)
    vectors.wait()

    def step(i, carry):
        copy(i).wait()
        slot = lax.rem(i, depth)
        for k in range(0, block, chunk):
            at = pl.ds(pl.multiple_of(i * block + k, chunk), chunk)
            pair = jnp.concatenate(split(m_buf[slot, k : k + chunk, :], 2), axis=1)
            pair_ref[at, :] = pair
            r = jnp.concatenate(split(r_ref[:, at], parts), axis=0)
            acc_ref[...] += jnp.dot(r, pair, preferred_element_type=F32)

        @pl.when(i + depth < blocks)
        def _():
            copy(i + depth).start()

        return carry

    lax.fori_loop(0, blocks, step, 0)
    g_ref[...] = fold(acc_ref[...], parts)


def first(residual, matrix, blocks=8, depth=3, chunk=512, parts=3):
    rows, n = matrix.shape
    return pl.pallas_call(
        functools.partial(first_kernel, blocks, depth, chunk, parts),
        in_specs=[ANY, ANY],
        out_specs=[VMEM, VMEM],
        out_shape=[pltpu.VMEM((rows, 2 * n), BF), pltpu.VMEM((MEMBERS, n), F32)],
        scratch_shapes=[
            pltpu.VMEM(residual.shape, F32),
            pltpu.VMEM((depth, rows // blocks, n), F32),
            pltpu.VMEM((MEMBERS * parts, 2 * n), F32),
            pltpu.SemaphoreType.DMA,
            pltpu.SemaphoreType.DMA((depth,)),
        ],
        compiler_params=params(16),
    )(far(residual), far(matrix))


def rows_body(slots, half, start, d, pair_ref, outs, w_ref, parts=3, chunk=512):
    rows, n2 = pair_ref.shape
    piece = rows // (2 * PIECES)
    vectors = jnp.concatenate([x.astype(F32) for x in split(d, parts)], axis=0)
    w_ref[: n2 // 2, :] = vectors.T.astype(BF)
    w_ref[n2 // 2 :, :] = w_ref[: n2 // 2, :]
    norm = jnp.sum(d * d, axis=1, keepdims=True)
    for slot, out in zip(slots, outs):
        q = lax.rem(start + slot, PIECES)
        for r in range(0, piece, chunk):
            at = pl.multiple_of((half * PIECES + q) * piece + r, chunk)
            o = jnp.dot(
                pair_ref[pl.ds(at, chunk), :], w_ref[...], preferred_element_type=F32
            ).T
            o = sum(o[MEMBERS * j : MEMBERS * (j + 1)] for j in range(parts))
            put(out, o, r // LANES)
        put_sums(out, norm)


AWAY = (1, 2, 3)


def each(ref):
    return [ref.at[i] for i in range(ref.shape[0])]


def send_first_kernel(order, a, b, c, d, pair_ref, out_ref, g_ref, w_ref):
    g = sum_of_ring(order, (a, b, c, d))
    g_ref[...] = g
    rows_body(range(PIECES), *place(1), g, pair_ref, each(out_ref), w_ref)


def send_second_kernel(
    order, a, b, c, d, g0_ref, gamma_ref, pair_ref, out_ref, g_ref, alpha_ref, w_ref
):
    w = sum_of_ring(order, (a, b, c, d))
    g0 = g0_ref[...]
    alpha = gamma_ref[:, :1] / sums_of(w)
    alpha_ref[...] = wide(alpha)
    g = g0 - alpha * strips(w, g0.shape[1])
    g_ref[...] = g
    rows_body(range(PIECES), *place(1), g, pair_ref, each(out_ref), w_ref)


def keep_kernel(d_ref, pair_ref, out_ref, w_ref):
    rows_body(AWAY, *place(0), d_ref[...], pair_ref, each(out_ref), w_ref)


def near_kernel(d_ref, after_ref, pair_ref, out_ref, w_ref):
    rows_body((0,), *place(0), d_ref[...], pair_ref, [out_ref], w_ref)


def by_rows(kernel, operands, pair, shapes):
    return pl.pallas_call(
        kernel,
        in_specs=[VMEM] * (len(operands) + 1),
        out_specs=[VMEM] * len(shapes),
        out_shape=[pltpu.VMEM(s, F32) for s in shapes],
        scratch_shapes=[pltpu.VMEM((pair.shape[1], 3 * MEMBERS), BF)],
        compiler_params=params(8),
    )(*map(pin, operands), pin(pair))


def cols_body(half, start, order, pieces, pair_ref, parts=3):
    piece = pieces[0].shape[1]
    acc = jnp.zeros((MEMBERS * parts, pair_ref.shape[1]), F32)
    norm = jnp.zeros((MEMBERS, 1), F32)
    for i, p in enumerate(pieces):
        q = lax.rem(start - order[i] + PIECES, PIECES)
        at = pl.multiple_of((half * PIECES + q) * piece, piece)
        vectors = jnp.concatenate(split(p, parts), axis=0)
        acc += jnp.dot(vectors, pair_ref[pl.ds(at, piece), :], preferred_element_type=F32)
        norm += jnp.sum(p * p, axis=1, keepdims=True)
    return fold(acc, parts), norm


def cols_own_kernel(order, a, b, c, d, pair_ref, w_ref):
    piece = pair_ref.shape[0] // (2 * PIECES)
    pieces = [strips(p, piece) for p in (a, b, c, d)]
    w, norm = cols_body(*place(0), order, pieces, pair_ref)
    put(w_ref, w)
    put_sums(w_ref, norm)


def cols_other_kernel(order, p_ref, before_ref, pair_ref, w_ref):
    piece = pair_ref.shape[0] // (2 * PIECES)
    pieces = [strips(p, piece) for p in each(p_ref)]
    w, norm = cols_body(*place(1), order, pieces, pair_ref)
    put(w_ref, w + strips(before_ref, w.shape[1]))
    put_sums(w_ref, norm + sums_of(before_ref))


def on_core(kernel, operands, shapes):
    return pl.pallas_call(
        kernel,
        in_specs=[VMEM] * len(operands),
        out_specs=[VMEM] * len(shapes),
        out_shape=[pltpu.VMEM(s, F32) for s in shapes],
        compiler_params=params(8),
    )(*map(pin, operands))


def ring(stage):
    def moved(f, k):
        z, x, core = f // 8, f // 2 % 4, f % 2
        if core == stage:
            z = (z + k) % 4
        else:
            x = (x + k) % 4
        return z * 8 + x * 2 + core

    return [[(f, moved(f, k)) for f in range(32)] for k in (1, 2, 3)]


CORE = [(f, f ^ 1) for f in range(32)]
CONF = [[(c, (c + k) % 4) for c in range(4)] for k in (1, 2, 3)]


def three(xs, axis, perms):
    return [lax.ppermute(x, axis, perm) for x, perm in zip(xs, perms)]


LAST, SECOND = (0, 1, 3, 2), (0, 2, 1, 3)


def listed(order, x):
    return [x[k] for k in order]


def sum_of_ring(order, refs):
    a, b, c, d = [refs[order.index(k)][...] for k in range(4)]
    return (a + c) + (b + d)


def total(own, others):
    return (others[0] + others[2]) + (own + others[1])


def reduce_pieces(order, d, send, pair):
    shape = send.shape[1:]
    got = lax.ppermute(send, "feat", CORE)
    (keep,) = by_rows(keep_kernel, [d], pair, [(len(AWAY), *shape)])
    away = [keep[i - 1] + got[i] for i in AWAY]
    (near,) = by_rows(near_kernel, [d, away[0]], pair, [shape])
    b, c, d = three(away, "feat", ring(0))
    piece = (d + b) + (c + (near + got[0]))
    return listed(order, [piece] + three([piece] * 3, "feat", ring(1)))


def piece_kernel(order, a, b, c, d, p_ref, gamma_ref):
    p = sum_of_ring(order, (a, b, c, d))
    p_ref[...] = p[: p_ref.shape[0]]
    gamma_ref[...] = wide(sums_of(p))


def image_kernel(order, a, b, c, d, before_ref, gamma0_ref, p_ref, gamma_ref):
    p = sum_of_ring(order, (a, b, c, d))
    gamma = sums_of(p)
    beta = gamma / gamma0_ref[:, :1]
    gamma_ref[...] = wide(gamma)
    for at in range(0, p_ref.shape[0], MEMBERS):
        p_ref[at : at + MEMBERS, :] = (
            p[at : at + MEMBERS] + beta * before_ref[at : at + MEMBERS, :]
        )


def curve_kernel(a, b, c, d, curve_ref):
    norm = sum(jnp.sum(strips(p, p.shape[0] * LANES // MEMBERS) ** 2, axis=1, keepdims=True) for p in (a, b, c, d))
    curve_ref[...] = wide(norm)


def gather_pieces(order, piece):
    own = listed(order, [piece] + three([piece] * 3, "feat", ring(0)))
    return own, jnp.stack(own)


def finish_kernel(p_order, i_order, *refs):
    r0_ref, alpha0_ref, gamma0_ref, gamma1_ref, curve_ref = refs[:5]
    p_own, p_other, i_own, i_other = refs[5:9], refs[9], refs[10:14], refs[14]
    g0_ref, g1_ref, sol_ref, res_ref = refs[15:]
    gamma1 = gamma1_ref[:, :1]
    a0 = alpha0_ref[:, :1]
    a1 = gamma1 / curve_ref[:, :1]
    b0 = gamma1 / gamma0_ref[:, :1]
    g0 = g0_ref[...]
    sol_ref[...] = a0 * g0 + a1 * (g1_ref[...] + b0 * g0)
    piece = p_own[0].shape[0] * LANES // MEMBERS
    for far_half, ps, images in ((0, p_own, i_own), (1, each(p_other), each(i_other))):
        half, start = place(far_half)
        for k in range(PIECES):
            q = lax.rem(start - k + PIECES, PIECES)
            at = pl.ds(pl.multiple_of((half * PIECES + q) * piece, piece), piece)
            p = strips(ps[p_order.index(k)], piece)
            image = strips(images[i_order.index(k)], piece)
            res_ref[:, at] = r0_ref[:, at] - a0 * p - a1 * image


ORDERS = (SECOND, SECOND, LAST, SECOND, SECOND, SECOND)


def body(matrix, targets):
    rows, n = matrix.shape
    size = rows // (2 * PIECES) * MEMBERS // LANES
    column = (MEMBERS, LANES)

    pair, part = first(targets, matrix)
    order = ORDERS[0]
    parts = listed(order, [part] + three([part] * 3, "conf", CONF))

    all_pieces = (PIECES, size + TAIL, LANES)
    send, g0 = by_rows(
        functools.partial(send_first_kernel, order), parts, pair, [all_pieces, (MEMBERS, n)])
    order = ORDERS[1]
    summands = reduce_pieces(order, g0, send, pair)
    p, gamma0 = on_core(
        functools.partial(piece_kernel, order), summands, [(size, LANES), column])
    p_own, stacked = gather_pieces(ORDERS[2], p)
    p_other = lax.ppermute(stacked, "feat", CORE)

    packed = [(MEMBERS * n // LANES + TAIL, LANES)]
    (w,) = on_core(functools.partial(cols_own_kernel, ORDERS[2]), p_own + [pair], packed)
    (w,) = on_core(functools.partial(cols_other_kernel, ORDERS[2]), [p_other, w, pair], packed)
    order = ORDERS[3]
    parts = listed(order, [w] + three([w] * 3, "conf", CONF))

    send, g1, alpha0 = by_rows(
        functools.partial(send_second_kernel, order), parts + [g0, gamma0], pair, [all_pieces, (MEMBERS, n), column]
    )
    order = ORDERS[4]
    summands = reduce_pieces(order, g1, send, pair)
    image, gamma1 = on_core(
        functools.partial(image_kernel, order), summands + [p, gamma0], [(size, LANES), column]
    )
    i_own, stacked = gather_pieces(ORDERS[5], image)

    (curve,) = on_core(curve_kernel, i_own, [column])
    curve = curve + lax.ppermute(curve, "feat", CORE)
    curve = total(curve, three([curve] * 3, "conf", CONF))
    i_other = lax.ppermute(stacked, "feat", CORE)

    return pl.pallas_call(
        functools.partial(finish_kernel, ORDERS[2], ORDERS[5]),
        in_specs=[VMEM] * 17,
        out_specs=[VMEM, VMEM],
        out_shape=[
            jax.ShapeDtypeStruct((MEMBERS, n), F32),
            jax.ShapeDtypeStruct((MEMBERS, rows), F32),
        ],
        compiler_params=params(8),
    )(
        targets,
        alpha0,
        gamma0,
        gamma1,
        curve,
        *p_own,
        p_other,
        *i_own,
        i_other,
        g0,
        g1,
    )


def solution(mesh):
    placed = (P("conf", "feat"), P(None, "conf"))
    return jax.shard_map(
        body,
        mesh=mesh,
        in_specs=placed,
        out_specs=(P(None, "feat"), P(None, "conf")),
        check_vma=False,
    )
```

time: 115 us -> 109 us (0.948); the launches traced: 113 us -> 109 us
  waiting for transfers between devices: 52.2 us -> 37 us
  starting transfers between devices: 33 us -> 42.9 us
  Pallas kernels: 26.3 us -> 27.7 us
    ppermute x27, waiting for transfers between devices: 51 us -> 35.7 us  [three(): return [lax.ppermute(x, axis, perm) for x, perm in zip(xs, perms)]]
    ppermute x27, starting transfers between devices: 32.4 us -> 41.8 us  [three(): return [lax.ppermute(x, axis, perm) for x, perm in zip(xs, perms)]]
    pallas_call x7 -> x12, Pallas kernels: 17.2 us -> 18.7 us  [the longest x6 13.3 us: by_rows(): pl.pallas_call(kernel, in_specs=[VMEM] * (len(operands) + 1), out_specs=[...]
  transfers between devices with their start and end apart: 32 -> 32, of which waited for: 24 -> 22; matrix products, arithmetic and copies ran while one was open for 0% -> 0% of each run, Pallas kernels for 7% -> 8%
where the time goes in v1:
time: 109 us
  starting transfers between devices  42.9 us (39%)
  waiting for transfers between devices  37 us (34%)
  Pallas kernels  27.7 us (25%)
    ppermute x27, starting transfers between devices, three(): return [lax.ppermute(x, axis, perm) for x, perm in zip(xs, perms)]  41.8 us
    ppermute x27, waiting for transfers between devices, three(): return [lax.ppermute(x, axis, perm) for x, perm in zip(xs, perms)]  35.7 us
    pallas_call x6, Pallas kernels, by_rows(): pl.pallas_call(kernel, in_specs=[VMEM] * (len(operands) + 1), out_specs=[...  13.3 us
    pallas_call x1, Pallas kernels, first(): pl.pallas_call(functools.partial(first_kernel, blocks, depth, chunk, part...  9.09 us
    pallas_call x5, Pallas kernels, on_core(): pl.pallas_call(kernel, in_specs=[VMEM] * len(operands), out_specs=[VMEM]...  4.03 us
  transfers between devices with their start and end apart: 32, of which 22 were waited for; matrix products, arithmetic and copies ran while one was open for 0% of the time, Pallas kernels for 8%

profile of v1, /device:TPU:0, one launch (start us, length us, event | category | flops | bytes accessed | tf_op | source)
XLA Modules:
  0.0 108.7 jit_solution(5339444243501507896)
XLA Ops:
  0.6 9.1 %shard_map.41 = (bf16[8192,1280]{1,0:T(8,128)(2,1)S(1)}, f32[32,640]{1,0:T(8,128)S(1)}) custom-call(f32[32,8192]{1,0:T(8,128)} %refs_0_.1, f32[8192,640]{1,0:T(8,128)} %m_hbm.1), custom_call_target="tpu_custom_call" | custom-call | tf_op jit(solution)/shard_map/pallas_call | solution.py:123
  9.7 3.4 %collective-permute-start = (f32[32,640]{1,0:T(8,128)S(1)}, f32[32,640]{1,0:T(8,128)S(1)}, u32[]{:S(2)}, u32[]{:S(2)}) collective-permute-start(f32[32,640]{1,0:T(8,128)S(1)} %get-tuple-element.13.a), channel_id=1, source_target_pairs={{0,2},{1,3},{2,0},{3,1},{4,6},{5,7},{6,4},{7,5},{8,10},{9,11},{10,... | collective-permute-start | bytes 245768 | tf_op jit(solution)/shard_map/ppermute | solution.py:258
  13.1 0.7 collective-permute-start.1
  13.8 2.6 %collective-permute-start.2 = (f32[32,640]{1,0:T(8,128)S(1)}, f32[32,640]{1,0:T(8,128)S(1)}, u32[]{:S(2)}, u32[]{:S(2)}) collective-permute-start(f32[32,640]{1,0:T(8,128)S(1)} %get-tuple-element.13.a), channel_id=1, source_target_pairs={{0,3},{1,0},{2,1},{3,2},{4,7},{5,4},{6,5},{7,6},{8,11},{9,8},{10,9... | collective-permute-start | bytes 245768 | tf_op jit(solution)/shard_map/ppermute | solution.py:258
  16.3 2.4 %collective-permute-done.1.c = f32[32,640]{1,0:T(8,128)S(1)} collective-permute-done((f32[32,640]{1,0:T(8,128)S(1)}, f32[32,640]{1,0:T(8,128)S(1)}, u32[]{:S(2)}, u32[]{:S(2)}) %collective-permute-start.1) | collective-permute-done | bytes 81952 | tf_op jit(solution)/shard_map/ppermute | solution.py:258
  18.7 3.1 %shard_map.42 = (f32[4,264,128]{2,1,0:T(8,128)S(1)}, f32[32,640]{1,0:T(8,128)S(1)}) custom-call(f32[32,640]{1,0:T(8,128)S(1)} %get-tuple-element.13.a, f32[32,640]{1,0:T(8,128)S(1)} %collective-permute-done.b, f32[32,640]{1,0:T(8,128)S(1)} %collective-permute-done.1.c, f32[32,640]{1,0:T(8,128)S(1)} %collective-permute-done.2.d, ...), custom_call_target="tpu_custom_call" | custom-call | tf_op jit(solution)/shard_map/pallas_call | solution.py:192
  21.9 2.4 %shard_map.43 = f32[3,264,128]{2,1,0:T(8,128)S(1)} custom-call(f32[32,640]{1,0:T(8,128)S(1)} %get-tuple-element.15.d_ref.g0_ref.refs_15_, bf16[8192,1280]{1,0:T(8,128)(2,1)S(1)} %get-tuple-element.14.pair_ref), custom_call_target="tpu_custom_call" | custom-call | tf_op jit(solution)/shard_map/pallas_call | solution.py:192
  24.4 4.0 %collective-permute-start.6 = (f32[264,128]{1,0:T(8,128)S(1)}, f32[264,128]{1,0:T(8,128)S(1)}, u32[]{:S(2)}, u32[]{:S(2)}) collective-permute-start(f32[264,128]{1,0:T(8,128)S(1)} %get-tuple-element.28), channel_id=1, source_target_pairs={{0,64},{4,20},{8,72},{12,28},{16,80},{20,4},{24,88},{28,12},{32,96... | collective-permute-start | bytes 405512 | tf_op jit(solution)/shard_map/ppermute | solution.py:258
  28.4 0.7 collective-permute-start.4
  29.1 1.3 %collective-permute-start.5 = (f32[264,128]{1,0:T(8,128)S(1)}, f32[264,128]{1,0:T(8,128)S(1)}, u32[]{:S(2)}, u32[]{:S(2)}) collective-permute-start(f32[264,128]{1,0:T(8,128)S(1)} %get-tuple-element.29.after_ref), channel_id=1, source_target_pairs={{0,32},{4,12},{8,40},{12,20},{16,48},{20,28},{24,56},{28,4},{32,64... | collective-permute-start | bytes 405512 | tf_op jit(solution)/shard_map/ppermute | solution.py:258
  30.4 1.1 shard_map.44
  31.5 2.4 %collective-permute-done.4 = f32[264,128]{1,0:T(8,128)S(1)} collective-permute-done((f32[264,128]{1,0:T(8,128)S(1)}, f32[264,128]{1,0:T(8,128)S(1)}, u32[]{:S(2)}, u32[]{:S(2)}) %collective-permute-start.4) | collective-permute-done | bytes 135200 | tf_op jit(solution)/shard_map/ppermute | solution.py:258
  33.8 1.5 %collective-permute-done.5 = f32[264,128]{1,0:T(8,128)S(1)} collective-permute-done((f32[264,128]{1,0:T(8,128)S(1)}, f32[264,128]{1,0:T(8,128)S(1)}, u32[]{:S(2)}, u32[]{:S(2)}) %collective-permute-start.5) | collective-permute-done | bytes 135200 | tf_op jit(solution)/shard_map/ppermute | solution.py:258
  35.3 3.1 %collective-permute-start.7 = (f32[264,128]{1,0:T(8,128)S(1)}, f32[264,128]{1,0:T(8,128)S(1)}, u32[]{:S(2)}, u32[]{:S(2)}) collective-permute-start(f32[264,128]{1,0:T(8,128)S(1)} %fusion.8.a), channel_id=1, source_target_pairs={{0,16},{4,68},{8,24},{12,76},{16,0},{20,84},{24,8},{28,92},{32,48}... | collective-permute-start | bytes 405512 | tf_op jit(solution)/shard_map/ppermute | solution.py:258
  39.1 2.6 %collective-permute-start.9 = (f32[264,128]{1,0:T(8,128)S(1)}, f32[264,128]{1,0:T(8,128)S(1)}, u32[]{:S(2)}, u32[]{:S(2)}) collective-permute-start(f32[264,128]{1,0:T(8,128)S(1)} %fusion.8.a), channel_id=1, source_target_pairs={{0,24},{4,100},{8,0},{12,108},{16,8},{20,116},{24,16},{28,124},{32... | collective-permute-start | bytes 405512 | tf_op jit(solution)/shard_map/ppermute | solution.py:258
  41.9 2.7 %collective-permute-done.8.c = f32[264,128]{1,0:T(8,128)S(1)} collective-permute-done((f32[264,128]{1,0:T(8,128)S(1)}, f32[264,128]{1,0:T(8,128)S(1)}, u32[]{:S(2)}, u32[]{:S(2)}) %collective-permute-start.8) | collective-permute-done | bytes 135200 | tf_op jit(solution)/shard_map/ppermute | solution.py:258
  44.8 1.2 %collective-permute-start.12 = (f32[256,128]{1,0:T(8,128)S(1)}, f32[256,128]{1,0:T(8,128)S(1)}, u32[]{:S(2)}, u32[]{:S(2)}) collective-permute-start(f32[256,128]{1,0:T(8,128)S(1)} %get-tuple-element.17.a.before_ref.refs_5_), channel_id=1, source_target_pairs={{0,64},{4,20},{8,72},{12,28},{16,80},{20,4},{24,88},{28,12},{32,96... | collective-permute-start | bytes 393224 | tf_op jit(solution)/shard_map/ppermute | solution.py:258
  46.0 1.6 %collective-permute-start.11 = (f32[256,128]{1,0:T(8,128)S(1)}, f32[256,128]{1,0:T(8,128)S(1)}, u32[]{:S(2)}, u32[]{:S(2)}) collective-permute-start(f32[256,128]{1,0:T(8,128)S(1)} %get-tuple-element.17.a.before_ref.refs_5_), channel_id=1, source_target_pairs={{0,96},{4,28},{8,104},{12,4},{16,112},{20,12},{24,120},{28,20},{32... | collective-permute-start | bytes 393224 | tf_op jit(solution)/shard_map/ppermute | solution.py:258
  48.0 3.3 %collective-permute-done.12.d.refs_8_ = f32[256,128]{1,0:T(8,128)S(1)} collective-permute-done((f32[256,128]{1,0:T(8,128)S(1)}, f32[256,128]{1,0:T(8,128)S(1)}, u32[]{:S(2)}, u32[]{:S(2)}) %collective-permute-start.12) | collective-permute-done | bytes 131104 | tf_op jit(solution)/shard_map/ppermute | solution.py:258
  51.3 2.5 %collective-permute-done.10.b.refs_6_ = f32[256,128]{1,0:T(8,128)S(1)} collective-permute-done((f32[256,128]{1,0:T(8,128)S(1)}, f32[256,128]{1,0:T(8,128)S(1)}, u32[]{:S(2)}, u32[]{:S(2)}) %collective-permute-start.10) | collective-permute-done | bytes 131104 | tf_op jit(solution)/shard_map/ppermute | solution.py:258
  54.1 1.8 %shard_map.46.before_ref = f32[168,128]{1,0:T(8,128)S(1)} custom-call(f32[256,128]{1,0:T(8,128)S(1)} %get-tuple-element.17.a.before_ref.refs_5_, f32[256,128]{1,0:T(8,128)S(1)} %collective-permute-done.10.b.refs_6_, f32[256,128]{1,0:T(8,128)S(1)} %collective-permute-done.11.c.refs_7_, f32[256,128]{1,0:T(8,128)S(1)} %collective-permute-done.12.d.refs_8_, ...), custom_call_target="tpu_custom_call" | custom-call | tf_op jit(solution)/shard_map/pallas_call | solution.py:232
  56.0 1.8 %shard_map.47.a = f32[168,128]{1,0:T(8,128)S(1)} custom-call(f32[4,256,128]{2,1,0:T(8,128)S(1)} %collective-permute-done.13.p_ref.refs_9_, f32[168,128]{1,0:T(8,128)S(1)} %shard_map.46.before_ref, bf16[8192,1280]{1,0:T(8,128)(2,1)S(1)} %get-tuple-element.14.pair_ref), custom_call_target="tpu_custom_call" | custom-call | tf_op jit(solution)/shard_map/pallas_call | solution.py:232
  57.8 1.5 %collective-permute-start.14 = (f32[168,128]{1,0:T(8,128)S(1)}, f32[168,128]{1,0:T(8,128)S(1)}, u32[]{:S(2)}, u32[]{:S(2)}) collective-permute-start(f32[168,128]{1,0:T(8,128)S(1)} %shard_map.47.a), channel_id=1, source_target_pairs={{0,2},{1,3},{2,0},{3,1},{4,6},{5,7},{6,4},{7,5},{8,10},{9,11},{10,... | collective-permute-start | bytes 258056 | tf_op jit(solution)/shard_map/ppermute | solution.py:258
  59.4 2.6 %collective-permute-start.15 = (f32[168,128]{1,0:T(8,128)S(1)}, f32[168,128]{1,0:T(8,128)S(1)}, u32[]{:S(2)}, u32[]{:S(2)}) collective-permute-start(f32[168,128]{1,0:T(8,128)S(1)} %shard_map.47.a), channel_id=1, source_target_pairs={{0,1},{1,2},{2,3},{3,0},{4,5},{5,6},{6,7},{7,4},{8,9},{9,10},{10,1... | collective-permute-start | bytes 258056 | tf_op jit(solution)/shard_map/ppermute | solution.py:258
  62.6 2.1 %collective-permute-done.14.b = f32[168,128]{1,0:T(8,128)S(1)} collective-permute-done((f32[168,128]{1,0:T(8,128)S(1)}, f32[168,128]{1,0:T(8,128)S(1)}, u32[]{:S(2)}, u32[]{:S(2)}) %collective-permute-start.14) | collective-permute-done | bytes 86048 | tf_op jit(solution)/shard_map/ppermute | solution.py:258
  64.7 1.4 %collective-permute-done.15.c = f32[168,128]{1,0:T(8,128)S(1)} collective-permute-done((f32[168,128]{1,0:T(8,128)S(1)}, f32[168,128]{1,0:T(8,128)S(1)}, u32[]{:S(2)}, u32[]{:S(2)}) %collective-permute-start.15) | collective-permute-done | bytes 86048 | tf_op jit(solution)/shard_map/ppermute | solution.py:258
  66.7 3.2 %shard_map.48 = (f32[4,264,128]{2,1,0:T(8,128)S(1)}, f32[32,640]{1,0:T(8,128)S(1)}, f32[32,128]{1,0:T(8,128)S(1)}) custom-call(f32[168,128]{1,0:T(8,128)S(1)} %shard_map.47.a, f32[168,128]{1,0:T(8,128)S(1)} %collective-permute-done.14.b, f32[168,128]{1,0:T(8,128)S(1)} %collective-permute-done.15.c, f32[168,128]{1,0:T(8,128)S(1)} %collective-permute-done.16.d, ...), custom_call_target="tpu_custom_call" | custom-call | tf_op jit(solution)/shard_map/pallas_call | solution.py:192
  70.0 2.4 %shard_map.49 = f32[3,264,128]{2,1,0:T(8,128)S(1)} custom-call(f32[32,640]{1,0:T(8,128)S(1)} %get-tuple-element.20.d_ref.refs_16_, bf16[8192,1280]{1,0:T(8,128)(2,1)S(1)} %get-tuple-element.14.pair_ref), custom_call_target="tpu_custom_call" | custom-call | tf_op jit(solution)/shard_map/pallas_call | solution.py:192
  72.7 1.7 %collective-permute-start.18 = (f32[264,128]{1,0:T(8,128)S(1)}, f32[264,128]{1,0:T(8,128)S(1)}, u32[]{:S(2)}, u32[]{:S(2)}) collective-permute-start(f32[264,128]{1,0:T(8,128)S(1)} %get-tuple-element.24), channel_id=1, source_target_pairs={{0,96},{4,28},{8,104},{12,4},{16,112},{20,12},{24,120},{28,20},{32... | collective-permute-start | bytes 405512 | tf_op jit(solution)/shard_map/ppermute | solution.py:258
  74.7 1.1 shard_map.50
  75.8 3.3 %collective-permute-done.20 = f32[264,128]{1,0:T(8,128)S(1)} collective-permute-done((f32[264,128]{1,0:T(8,128)S(1)}, f32[264,128]{1,0:T(8,128)S(1)}, u32[]{:S(2)}, u32[]{:S(2)}) %collective-permute-start.20) | collective-permute-done | bytes 135200 | tf_op jit(solution)/shard_map/ppermute | solution.py:258
  79.1 1.6 %collective-permute-done.19 = f32[264,128]{1,0:T(8,128)S(1)} collective-permute-done((f32[264,128]{1,0:T(8,128)S(1)}, f32[264,128]{1,0:T(8,128)S(1)}, u32[]{:S(2)}, u32[]{:S(2)}) %collective-permute-start.19) | collective-permute-done | bytes 135200 | tf_op jit(solution)/shard_map/ppermute | solution.py:258
  80.7 1.5 %collective-permute-start.21 = (f32[264,128]{1,0:T(8,128)S(1)}, f32[264,128]{1,0:T(8,128)S(1)}, u32[]{:S(2)}, u32[]{:S(2)}) collective-permute-start(f32[264,128]{1,0:T(8,128)S(1)} %fusion.2.a), channel_id=1, source_target_pairs={{0,16},{4,68},{8,24},{12,76},{16,0},{20,84},{24,8},{28,92},{32,48}... | collective-permute-start | bytes 405512 | tf_op jit(solution)/shard_map/ppermute | solution.py:258
  82.3 2.6 %collective-permute-start.22 = (f32[264,128]{1,0:T(8,128)S(1)}, f32[264,128]{1,0:T(8,128)S(1)}, u32[]{:S(2)}, u32[]{:S(2)}) collective-permute-start(f32[264,128]{1,0:T(8,128)S(1)} %fusion.2.a), channel_id=1, source_target_pairs={{0,8},{4,36},{8,16},{12,44},{16,24},{20,52},{24,0},{28,60},{32,40}... | collective-permute-start | bytes 405512 | tf_op jit(solution)/shard_map/ppermute | solution.py:258
  85.5 1.8 %collective-permute-done.21.b = f32[264,128]{1,0:T(8,128)S(1)} collective-permute-done((f32[264,128]{1,0:T(8,128)S(1)}, f32[264,128]{1,0:T(8,128)S(1)}, u32[]{:S(2)}, u32[]{:S(2)}) %collective-permute-start.21) | collective-permute-done | bytes 135200 | tf_op jit(solution)/shard_map/ppermute | solution.py:258
  87.3 1.4 %collective-permute-done.22.c = f32[264,128]{1,0:T(8,128)S(1)} collective-permute-done((f32[264,128]{1,0:T(8,128)S(1)}, f32[264,128]{1,0:T(8,128)S(1)}, u32[]{:S(2)}, u32[]{:S(2)}) %collective-permute-start.22) | collective-permute-done | bytes 135200 | tf_op jit(solution)/shard_map/ppermute | solution.py:258
  88.8 1.1 %collective-permute-done.23.d = f32[264,128]{1,0:T(8,128)S(1)} collective-permute-done((f32[264,128]{1,0:T(8,128)S(1)}, f32[264,128]{1,0:T(8,128)S(1)}, u32[]{:S(2)}, u32[]{:S(2)}) %collective-permute-start.23) | collective-permute-done | bytes 135200 | tf_op jit(solution)/shard_map/ppermute | solution.py:258
  90.6 1.4 %collective-permute-start.25 = (f32[256,128]{1,0:T(8,128)S(1)}, f32[256,128]{1,0:T(8,128)S(1)}, u32[]{:S(2)}, u32[]{:S(2)}) collective-permute-start(f32[256,128]{1,0:T(8,128)S(1)} %get-tuple-element.23.a.refs_10_), channel_id=1, source_target_pairs={{0,32},{4,12},{8,40},{12,20},{16,48},{20,28},{24,56},{28,4},{32,64... | collective-permute-start | bytes 393224 | tf_op jit(solution)/shard_map/ppermute | solution.py:258
  92.0 1.8 %collective-permute-start.26 = (f32[256,128]{1,0:T(8,128)S(1)}, f32[256,128]{1,0:T(8,128)S(1)}, u32[]{:S(2)}, u32[]{:S(2)}) collective-permute-start(f32[256,128]{1,0:T(8,128)S(1)} %get-tuple-element.23.a.refs_10_), channel_id=1, source_target_pairs={{0,96},{4,28},{8,104},{12,4},{16,112},{20,12},{24,120},{28,20},{32... | collective-permute-start | bytes 393224 | tf_op jit(solution)/shard_map/ppermute | solution.py:258
  93.8 2.9 %collective-permute-done.24.b.refs_11_ = f32[256,128]{1,0:T(8,128)S(1)} collective-permute-done((f32[256,128]{1,0:T(8,128)S(1)}, f32[256,128]{1,0:T(8,128)S(1)}, u32[]{:S(2)}, u32[]{:S(2)}) %collective-permute-start.24) | collective-permute-done | bytes 131104 | tf_op jit(solution)/shard_map/ppermute | solution.py:258
  96.7 1.3 %collective-permute-done.25.c.refs_12_ = f32[256,128]{1,0:T(8,128)S(1)} collective-permute-done((f32[256,128]{1,0:T(8,128)S(1)}, f32[256,128]{1,0:T(8,128)S(1)}, u32[]{:S(2)}, u32[]{:S(2)}) %collective-permute-start.25) | collective-permute-done | bytes 131104 | tf_op jit(solution)/shard_map/ppermute | solution.py:258
  98.8 1.2 %collective-permute-done.27 = f32[32,128]{1,0:T(8,128)S(1)} collective-permute-done((f32[32,128]{1,0:T(8,128)S(1)}, f32[32,128]{1,0:T(8,128)S(1)}, u32[]{:S(2)}, u32[]{:S(2)}) %collective-permute-start.27) | collective-permute-done | bytes 16416 | tf_op jit(solution)/shard_map/ppermute | solution.py:375
  100.1 0.9 collective-permute-start.30
  101.0 2.6 %collective-permute-start.28 = (f32[32,128]{1,0:T(8,128)S(1)}, f32[32,128]{1,0:T(8,128)S(1)}, u32[]{:S(2)}, u32[]{:S(2)}) collective-permute-start(f32[32,128]{1,0:T(8,128)S(1)} %add.90), channel_id=1, source_target_pairs={{0,1},{1,2},{2,3},{3,0},{4,5},{5,6},{6,7},{7,4},{8,9},{9,10},{10,1... | collective-permute-start | bytes 49160 | tf_op jit(solution)/shard_map/ppermute | solution.py:258
  103.6 0.6 collective-permute-start.29
  104.2 1.1 collective-permute-done.30
  106.0 1.4 %collective-permute-done.29 = f32[32,128]{1,0:T(8,128)S(1)} collective-permute-done((f32[32,128]{1,0:T(8,128)S(1)}, f32[32,128]{1,0:T(8,128)S(1)}, u32[]{:S(2)}, u32[]{:S(2)}) %collective-permute-start.29) | collective-permute-done | bytes 16416 | tf_op jit(solution)/shard_map/ppermute | solution.py:258
  107.4 1.4 %shard_map.53 = (f32[32,640]{1,0:T(8,128)}, f32[32,8192]{1,0:T(8,128)}) custom-call(f32[32,8192]{1,0:T(8,128)S(1)} %copy-done, f32[32,128]{1,0:T(8,128)S(1)} %get-tuple-element.19.refs_1_, f32[32,128]{1,0:T(8,128)S(1)} %get-tuple-element.18.gamma_ref.gamma0_ref.refs_2_, f32[32,128]{1,0:T(8,128)S(1)} %get-tuple-element.22.refs_3_, ...), custom_call_target="tpu_custom_call" | custom-call | tf_op jit(solution)/shard_map/pallas_call | solution.py:379
  (39 shorter events, 6.6 us)
Async XLA Ops:
  9.7 6.6 %collective-permute-start = (f32[32,640]{1,0:T(8,128)S(1)}, f32[32,640]{1,0:T(8,128)S(1)}, u32[]{:S(2)}, u32[]{:S(2)}) collective-permute-start(f32[32,640]{1,0:T(8,128)S(1)} %get-tuple-element.13.a), channel_id=1, source_target_pairs={{0,2},{1,3},{2,0},{3,1},{4,6},{5,7},{6,4},{7,5},{8,10},{9,11},{10,... | collective-permute-start | bytes 245768 | tf_op jit(solution)/shard_map/ppermute | solution.py:258
  13.1 5.7 %collective-permute-start.1 = (f32[32,640]{1,0:T(8,128)S(1)}, f32[32,640]{1,0:T(8,128)S(1)}, u32[]{:S(2)}, u32[]{:S(2)}) collective-permute-start(f32[32,640]{1,0:T(8,128)S(1)} %get-tuple-element.13.a), channel_id=1, source_target_pairs={{0,1},{1,2},{2,3},{3,0},{4,5},{5,6},{6,7},{7,4},{8,9},{9,10},{10,1... | collective-permute-start | bytes 245768 | tf_op jit(solution)/shard_map/ppermute | solution.py:258
  13.8 5.0 %collective-permute-start.2 = (f32[32,640]{1,0:T(8,128)S(1)}, f32[32,640]{1,0:T(8,128)S(1)}, u32[]{:S(2)}, u32[]{:S(2)}) collective-permute-start(f32[32,640]{1,0:T(8,128)S(1)} %get-tuple-element.13.a), channel_id=1, source_target_pairs={{0,3},{1,0},{2,1},{3,2},{4,7},{5,4},{6,5},{7,6},{8,11},{9,8},{10,9... | collective-permute-start | bytes 245768 | tf_op jit(solution)/shard_map/ppermute | solution.py:258
  21.8 2.5 %collective-permute-start.3 = (f32[4,264,128]{2,1,0:T(8,128)S(1)}, f32[4,264,128]{2,1,0:T(8,128)S(1)}, u32[]{:S(2)}, u32[]{:S(2)}) collective-permute-start(f32[4,264,128]{2,1,0:T(8,128)S(1)} %get-tuple-element.16), channel_id=1, source_target_pairs={{0,4},{4,0},{8,12},{12,8},{16,20},{20,16},{24,28},{28,24},{32,36},... | collective-permute-start | bytes 1622024 | tf_op jit(solution)/shard_map/ppermute | solution.py:279
  24.4 7.0 %collective-permute-start.6 = (f32[264,128]{1,0:T(8,128)S(1)}, f32[264,128]{1,0:T(8,128)S(1)}, u32[]{:S(2)}, u32[]{:S(2)}) collective-permute-start(f32[264,128]{1,0:T(8,128)S(1)} %get-tuple-element.28), channel_id=1, source_target_pairs={{0,64},{4,20},{8,72},{12,28},{16,80},{20,4},{24,88},{28,12},{32,96... | collective-permute-start | bytes 405512 | tf_op jit(solution)/shard_map/ppermute | solution.py:258
  28.4 5.5 %collective-permute-start.4 = (f32[264,128]{1,0:T(8,128)S(1)}, f32[264,128]{1,0:T(8,128)S(1)}, u32[]{:S(2)}, u32[]{:S(2)}) collective-permute-start(f32[264,128]{1,0:T(8,128)S(1)} %get-tuple-element.27), channel_id=1, source_target_pairs={{0,96},{4,28},{8,104},{12,4},{16,112},{20,12},{24,120},{28,20},{32... | collective-permute-start | bytes 405512 | tf_op jit(solution)/shard_map/ppermute | solution.py:258
  29.1 6.2 %collective-permute-start.5 = (f32[264,128]{1,0:T(8,128)S(1)}, f32[264,128]{1,0:T(8,128)S(1)}, u32[]{:S(2)}, u32[]{:S(2)}) collective-permute-start(f32[264,128]{1,0:T(8,128)S(1)} %get-tuple-element.29.after_ref), channel_id=1, source_target_pairs={{0,32},{4,12},{8,40},{12,20},{16,48},{20,28},{24,56},{28,4},{32,64... | collective-permute-start | bytes 405512 | tf_op jit(solution)/shard_map/ppermute | solution.py:258
  35.3 6.6 %collective-permute-start.7 = (f32[264,128]{1,0:T(8,128)S(1)}, f32[264,128]{1,0:T(8,128)S(1)}, u32[]{:S(2)}, u32[]{:S(2)}) collective-permute-start(f32[264,128]{1,0:T(8,128)S(1)} %fusion.8.a), channel_id=1, source_target_pairs={{0,16},{4,68},{8,24},{12,76},{16,0},{20,84},{24,8},{28,92},{32,48}... | collective-permute-start | bytes 405512 | tf_op jit(solution)/shard_map/ppermute | solution.py:258
  38.5 6.2 %collective-permute-start.8 = (f32[264,128]{1,0:T(8,128)S(1)}, f32[264,128]{1,0:T(8,128)S(1)}, u32[]{:S(2)}, u32[]{:S(2)}) collective-permute-start(f32[264,128]{1,0:T(8,128)S(1)} %fusion.8.a), channel_id=1, source_target_pairs={{0,8},{4,36},{8,16},{12,44},{16,24},{20,52},{24,0},{28,60},{32,40}... | collective-permute-start | bytes 405512 | tf_op jit(solution)/shard_map/ppermute | solution.py:258
  39.1 5.6 %collective-permute-start.9 = (f32[264,128]{1,0:T(8,128)S(1)}, f32[264,128]{1,0:T(8,128)S(1)}, u32[]{:S(2)}, u32[]{:S(2)}) collective-permute-start(f32[264,128]{1,0:T(8,128)S(1)} %fusion.8.a), channel_id=1, source_target_pairs={{0,24},{4,100},{8,0},{12,108},{16,8},{20,116},{24,16},{28,124},{32... | collective-permute-start | bytes 405512 | tf_op jit(solution)/shard_map/ppermute | solution.py:258
  44.8 6.5 %collective-permute-start.12 = (f32[256,128]{1,0:T(8,128)S(1)}, f32[256,128]{1,0:T(8,128)S(1)}, u32[]{:S(2)}, u32[]{:S(2)}) collective-permute-start(f32[256,128]{1,0:T(8,128)S(1)} %get-tuple-element.17.a.before_ref.refs_5_), channel_id=1, source_target_pairs={{0,64},{4,20},{8,72},{12,28},{16,80},{20,4},{24,88},{28,12},{32,96... | collective-permute-start | bytes 393224 | tf_op jit(solution)/shard_map/ppermute | solution.py:258
  46.0 5.3 %collective-permute-start.11 = (f32[256,128]{1,0:T(8,128)S(1)}, f32[256,128]{1,0:T(8,128)S(1)}, u32[]{:S(2)}, u32[]{:S(2)}) collective-permute-start(f32[256,128]{1,0:T(8,128)S(1)} %get-tuple-element.17.a.before_ref.refs_5_), channel_id=1, source_target_pairs={{0,96},{4,28},{8,104},{12,4},{16,112},{20,12},{24,120},{28,20},{32... | collective-permute-start | bytes 393224 | tf_op jit(solution)/shard_map/ppermute | solution.py:258
  47.6 6.2 %collective-permute-start.10 = (f32[256,128]{1,0:T(8,128)S(1)}, f32[256,128]{1,0:T(8,128)S(1)}, u32[]{:S(2)}, u32[]{:S(2)}) collective-permute-start(f32[256,128]{1,0:T(8,128)S(1)} %get-tuple-element.17.a.before_ref.refs_5_), channel_id=1, source_target_pairs={{0,32},{4,12},{8,40},{12,20},{16,48},{20,28},{24,56},{28,4},{32,64... | collective-permute-start | bytes 393224 | tf_op jit(solution)/shard_map/ppermute | solution.py:258
  53.8 2.2 %collective-permute-start.13 = (f32[4,256,128]{2,1,0:T(8,128)S(1)}, f32[4,256,128]{2,1,0:T(8,128)S(1)}, u32[]{:S(2)}, u32[]{:S(2)}) collective-permute-start(f32[4,256,128]{2,1,0:T(8,128)S(1)} %pad_maximum_fusion), channel_id=1, source_target_pairs={{0,4},{4,0},{8,12},{12,8},{16,20},{20,16},{24,28},{28,24},{32,36},... | collective-permute-start | bytes 1572872 | tf_op jit(solution)/shard_map/ppermute | solution.py:356
  57.8 6.9 %collective-permute-start.14 = (f32[168,128]{1,0:T(8,128)S(1)}, f32[168,128]{1,0:T(8,128)S(1)}, u32[]{:S(2)}, u32[]{:S(2)}) collective-permute-start(f32[168,128]{1,0:T(8,128)S(1)} %shard_map.47.a), channel_id=1, source_target_pairs={{0,2},{1,3},{2,0},{3,1},{4,6},{5,7},{6,4},{7,5},{8,10},{9,11},{10,... | collective-permute-start | bytes 258056 | tf_op jit(solution)/shard_map/ppermute | solution.py:258
  59.4 6.8 %collective-permute-start.15 = (f32[168,128]{1,0:T(8,128)S(1)}, f32[168,128]{1,0:T(8,128)S(1)}, u32[]{:S(2)}, u32[]{:S(2)}) collective-permute-start(f32[168,128]{1,0:T(8,128)S(1)} %shard_map.47.a), channel_id=1, source_target_pairs={{0,1},{1,2},{2,3},{3,0},{4,5},{5,6},{6,7},{7,4},{8,9},{9,10},{10,1... | collective-permute-start | bytes 258056 | tf_op jit(solution)/shard_map/ppermute | solution.py:258
  62.0 4.7 %collective-permute-start.16 = (f32[168,128]{1,0:T(8,128)S(1)}, f32[168,128]{1,0:T(8,128)S(1)}, u32[]{:S(2)}, u32[]{:S(2)}) collective-permute-start(f32[168,128]{1,0:T(8,128)S(1)} %shard_map.47.a), channel_id=1, source_target_pairs={{0,3},{1,0},{2,1},{3,2},{4,7},{5,4},{6,5},{7,6},{8,11},{9,8},{10,9... | collective-permute-start | bytes 258056 | tf_op jit(solution)/shard_map/ppermute | solution.py:258
  69.9 2.5 %collective-permute-start.17 = (f32[4,264,128]{2,1,0:T(8,128)S(1)}, f32[4,264,128]{2,1,0:T(8,128)S(1)}, u32[]{:S(2)}, u32[]{:S(2)}) collective-permute-start(f32[4,264,128]{2,1,0:T(8,128)S(1)} %get-tuple-element.21), channel_id=1, source_target_pairs={{0,4},{4,0},{8,12},{12,8},{16,20},{20,16},{24,28},{28,24},{32,36},... | collective-permute-start | bytes 1622024 | tf_op jit(solution)/shard_map/ppermute | solution.py:279
  70.0 37.4 %copy-start = (f32[32,8192]{1,0:T(8,128)S(1)}, f32[32,8192]{1,0:T(8,128)}, u32[]{:S(2)}) copy-start(f32[32,8192]{1,0:T(8,128)} %refs_0_.1) | copy-start | bytes 3145732
  72.5 6.6 %collective-permute-start.20 = (f32[264,128]{1,0:T(8,128)S(1)}, f32[264,128]{1,0:T(8,128)S(1)}, u32[]{:S(2)}, u32[]{:S(2)}) collective-permute-start(f32[264,128]{1,0:T(8,128)S(1)} %get-tuple-element.25), channel_id=1, source_target_pairs={{0,64},{4,20},{8,72},{12,28},{16,80},{20,4},{24,88},{28,12},{32,96... | collective-permute-start | bytes 405512 | tf_op jit(solution)/shard_map/ppermute | solution.py:258
  72.7 6.4 %collective-permute-start.18 = (f32[264,128]{1,0:T(8,128)S(1)}, f32[264,128]{1,0:T(8,128)S(1)}, u32[]{:S(2)}, u32[]{:S(2)}) collective-permute-start(f32[264,128]{1,0:T(8,128)S(1)} %get-tuple-element.24), channel_id=1, source_target_pairs={{0,96},{4,28},{8,104},{12,4},{16,112},{20,12},{24,120},{28,20},{32... | collective-permute-start | bytes 405512 | tf_op jit(solution)/shard_map/ppermute | solution.py:258
  74.5 6.2 %collective-permute-start.19 = (f32[264,128]{1,0:T(8,128)S(1)}, f32[264,128]{1,0:T(8,128)S(1)}, u32[]{:S(2)}, u32[]{:S(2)}) collective-permute-start(f32[264,128]{1,0:T(8,128)S(1)} %get-tuple-element.26.after_ref), channel_id=1, source_target_pairs={{0,32},{4,12},{8,40},{12,20},{16,48},{20,28},{24,56},{28,4},{32,64... | collective-permute-start | bytes 405512 | tf_op jit(solution)/shard_map/ppermute | solution.py:258
  80.7 6.6 %collective-permute-start.21 = (f32[264,128]{1,0:T(8,128)S(1)}, f32[264,128]{1,0:T(8,128)S(1)}, u32[]{:S(2)}, u32[]{:S(2)}) collective-permute-start(f32[264,128]{1,0:T(8,128)S(1)} %fusion.2.a), channel_id=1, source_target_pairs={{0,16},{4,68},{8,24},{12,76},{16,0},{20,84},{24,8},{28,92},{32,48}... | collective-permute-start | bytes 405512 | tf_op jit(solution)/shard_map/ppermute | solution.py:258
  82.3 6.5 %collective-permute-start.22 = (f32[264,128]{1,0:T(8,128)S(1)}, f32[264,128]{1,0:T(8,128)S(1)}, u32[]{:S(2)}, u32[]{:S(2)}) collective-permute-start(f32[264,128]{1,0:T(8,128)S(1)} %fusion.2.a), channel_id=1, source_target_pairs={{0,8},{4,36},{8,16},{12,44},{16,24},{20,52},{24,0},{28,60},{32,40}... | collective-permute-start | bytes 405512 | tf_op jit(solution)/shard_map/ppermute | solution.py:258
  84.9 5.0 %collective-permute-start.23 = (f32[264,128]{1,0:T(8,128)S(1)}, f32[264,128]{1,0:T(8,128)S(1)}, u32[]{:S(2)}, u32[]{:S(2)}) collective-permute-start(f32[264,128]{1,0:T(8,128)S(1)} %fusion.2.a), channel_id=1, source_target_pairs={{0,24},{4,100},{8,0},{12,108},{16,8},{20,116},{24,16},{28,124},{32... | collective-permute-start | bytes 405512 | tf_op jit(solution)/shard_map/ppermute | solution.py:258
  90.1 6.7 %collective-permute-start.24 = (f32[256,128]{1,0:T(8,128)S(1)}, f32[256,128]{1,0:T(8,128)S(1)}, u32[]{:S(2)}, u32[]{:S(2)}) collective-permute-start(f32[256,128]{1,0:T(8,128)S(1)} %get-tuple-element.23.a.refs_10_), channel_id=1, source_target_pairs={{0,64},{4,20},{8,72},{12,28},{16,80},{20,4},{24,88},{28,12},{32,96... | collective-permute-start | bytes 393224 | tf_op jit(solution)/shard_map/ppermute | solution.py:258
  90.6 7.4 %collective-permute-start.25 = (f32[256,128]{1,0:T(8,128)S(1)}, f32[256,128]{1,0:T(8,128)S(1)}, u32[]{:S(2)}, u32[]{:S(2)}) collective-permute-start(f32[256,128]{1,0:T(8,128)S(1)} %get-tuple-element.23.a.refs_10_), channel_id=1, source_target_pairs={{0,32},{4,12},{8,40},{12,20},{16,48},{20,28},{24,56},{28,4},{32,64... | collective-permute-start | bytes 393224 | tf_op jit(solution)/shard_map/ppermute | solution.py:258
  92.0 6.0 %collective-permute-start.26 = (f32[256,128]{1,0:T(8,128)S(1)}, f32[256,128]{1,0:T(8,128)S(1)}, u32[]{:S(2)}, u32[]{:S(2)}) collective-permute-start(f32[256,128]{1,0:T(8,128)S(1)} %get-tuple-element.23.a.refs_10_), channel_id=1, source_target_pairs={{0,96},{4,28},{8,104},{12,4},{16,112},{20,12},{24,120},{28,20},{32... | collective-permute-start | bytes 393224 | tf_op jit(solution)/shard_map/ppermute | solution.py:258
  98.1 9.3 %collective-permute-start.31 = (f32[4,256,128]{2,1,0:T(8,128)S(1)}, f32[4,256,128]{2,1,0:T(8,128)S(1)}, u32[]{:S(2)}, u32[]{:S(2)}) collective-permute-start(f32[4,256,128]{2,1,0:T(8,128)S(1)} %pad_maximum_fusion.1), channel_id=1, source_target_pairs={{0,4},{4,0},{8,12},{12,8},{16,20},{20,16},{24,28},{28,24},{32,36},... | collective-permute-start | bytes 1572872 | tf_op jit(solution)/shard_map/ppermute | solution.py:377
  98.3 1.8 %collective-permute-start.27 = (f32[32,128]{1,0:T(8,128)S(1)}, f32[32,128]{1,0:T(8,128)S(1)}, u32[]{:S(2)}, u32[]{:S(2)}) collective-permute-start(f32[32,128]{1,0:T(8,128)S(1)} %shard_map.52), channel_id=1, source_target_pairs={{0,4},{4,0},{8,12},{12,8},{16,20},{20,16},{24,28},{28,24},{32,36},... | collective-permute-start | bytes 49160 | tf_op jit(solution)/shard_map/ppermute | solution.py:375
  100.1 5.2 %collective-permute-start.30 = (f32[32,128]{1,0:T(8,128)S(1)}, f32[32,128]{1,0:T(8,128)S(1)}, u32[]{:S(2)}, u32[]{:S(2)}) collective-permute-start(f32[32,128]{1,0:T(8,128)S(1)} %add.90), channel_id=1, source_target_pairs={{0,2},{1,3},{2,0},{3,1},{4,6},{5,7},{6,4},{7,5},{8,10},{9,11},{10,... | collective-permute-start | bytes 49160 | tf_op jit(solution)/shard_map/ppermute | solution.py:258
  101.0 4.9 %collective-permute-start.28 = (f32[32,128]{1,0:T(8,128)S(1)}, f32[32,128]{1,0:T(8,128)S(1)}, u32[]{:S(2)}, u32[]{:S(2)}) collective-permute-start(f32[32,128]{1,0:T(8,128)S(1)} %add.90), channel_id=1, source_target_pairs={{0,1},{1,2},{2,3},{3,0},{4,5},{5,6},{6,7},{7,4},{8,9},{9,10},{10,1... | collective-permute-start | bytes 49160 | tf_op jit(solution)/shard_map/ppermute | solution.py:258
  103.6 3.7 %collective-permute-start.29 = (f32[32,128]{1,0:T(8,128)S(1)}, f32[32,128]{1,0:T(8,128)S(1)}, u32[]{:S(2)}, u32[]{:S(2)}) collective-permute-start(f32[32,128]{1,0:T(8,128)S(1)} %add.90), channel_id=1, source_target_pairs={{0,3},{1,0},{2,1},{3,2},{4,7},{5,4},{6,5},{7,6},{8,11},{9,8},{10,9... | collective-permute-start | bytes 49160 | tf_op jit(solution)/shard_map/ppermute | solution.py:258

commit v2 on v1

--- a/solution.py
+++ b/solution.py
@@ -132,7 +132,7 @@
             pltpu.SemaphoreType.DMA,
             pltpu.SemaphoreType.DMA((depth,)),
         ],
-        compiler_params=params(16),
+        compiler_params=params(11),
     )(far(residual), far(matrix))
 
 
@@ -144,7 +144,7 @@
     w_ref[n2 // 2 :, :] = w_ref[: n2 // 2, :]
     norm = jnp.sum(d * d, axis=1, keepdims=True)
     for slot, out in zip(slots, outs):
-        q = lax.rem(start + slot, PIECES)
+        q = start ^ slot
         for r in range(0, piece, chunk):
             at = pl.multiple_of((half * PIECES + q) * piece + r, chunk)
             o = jnp.dot(
@@ -156,20 +156,64 @@
 
 
 AWAY = (1, 2, 3)
+FLIP = (1, 2, 3)
+
+
+def flip_kernel(chunk, pair_ref, flipped_ref):
+    piece = flipped_ref.shape[1] // len(FLIP)
+    half, start = place(1)
+    for i, slot in enumerate(FLIP):
+        q = start ^ slot
+        for r in range(0, piece, chunk):
+            at = pl.multiple_of((half * PIECES + q) * piece + r, chunk)
+            to = i * piece + r
+            flipped_ref[:, to : to + chunk] = pair_ref[pl.ds(at, chunk), :].T
+
+
+def flip(pair, chunk=512):
+    rows, n2 = pair.shape
+    return pl.pallas_call(
+        functools.partial(flip_kernel, chunk),
+        in_specs=[VMEM],
+        out_specs=VMEM,
+        out_shape=pltpu.VMEM((n2, rows // (2 * PIECES) * len(FLIP)), BF),
+        compiler_params=params(4),
+        cost_estimate=pl.CostEstimate(
+            flops=0, bytes_accessed=2 * rows * n2, transcendentals=0
+        ),
+    )(pin(pair))
+
+
+def rows_flipped(d, flipped_ref, outs, parts=3, chunk=512):
+    piece = flipped_ref.shape[1] // len(FLIP)
+    vectors = jnp.concatenate(split(d, parts), axis=0)
+    vectors = jnp.concatenate([vectors, vectors], axis=1)
+    norm = jnp.sum(d * d, axis=1, keepdims=True)
+    for i, out in enumerate(outs):
+        for r in range(0, piece, chunk):
+            at = i * piece + r
+            o = jnp.dot(
+                vectors, flipped_ref[:, at : at + chunk], preferred_element_type=F32
+            )
+            o = sum(o[MEMBERS * j : MEMBERS * (j + 1)] for j in range(parts))
+            put(out, o, r // LANES)
+        put_sums(out, norm)
 
 
 def each(ref):
     return [ref.at[i] for i in range(ref.shape[0])]
 
 
-def send_first_kernel(order, a, b, c, d, pair_ref, out_ref, g_ref, w_ref):
+def send_first_kernel(order, a, b, c, d, flipped_ref, pair_ref, out_ref, g_ref, w_ref):
     g = sum_of_ring(order, (a, b, c, d))
     g_ref[...] = g
-    rows_body(range(PIECES), *place(1), g, pair_ref, each(out_ref), w_ref)
+    rest = [k for k in range(PIECES) if k not in FLIP]
+    rows_flipped(g, flipped_ref, [out_ref.at[k] for k in FLIP])
+    rows_body(rest, *place(1), g, pair_ref, [out_ref.at[k] for k in rest], w_ref)
 
 
 def send_second_kernel(
-    order, a, b, c, d, g0_ref, gamma_ref, pair_ref, out_ref, g_ref, alpha_ref, w_ref
+    order, a, b, c, d, g0_ref, gamma_ref, flipped_ref, pair_ref, out_ref, g_ref, alpha_ref, w_ref
 ):
     w = sum_of_ring(order, (a, b, c, d))
     g0 = g0_ref[...]
@@ -177,7 +221,9 @@
     alpha_ref[...] = wide(alpha)
     g = g0 - alpha * strips(w, g0.shape[1])
     g_ref[...] = g
-    rows_body(range(PIECES), *place(1), g, pair_ref, each(out_ref), w_ref)
+    rest = [k for k in range(PIECES) if k not in FLIP]
+    rows_flipped(g, flipped_ref, [out_ref.at[k] for k in FLIP])
+    rows_body(rest, *place(1), g, pair_ref, [out_ref.at[k] for k in rest], w_ref)
 
 
 def keep_kernel(d_ref, pair_ref, out_ref, w_ref):
@@ -195,7 +241,7 @@
         out_specs=[VMEM] * len(shapes),
         out_shape=[pltpu.VMEM(s, F32) for s in shapes],
         scratch_shapes=[pltpu.VMEM((pair.shape[1], 3 * MEMBERS), BF)],
-        compiler_params=params(8),
+        compiler_params=params(4),
     )(*map(pin, operands), pin(pair))
 
 
@@ -204,7 +250,7 @@
     acc = jnp.zeros((MEMBERS * parts, pair_ref.shape[1]), F32)
     norm = jnp.zeros((MEMBERS, 1), F32)
     for i, p in enumerate(pieces):
-        q = lax.rem(start - order[i] + PIECES, PIECES)
+        q = start ^ order[i]
         at = pl.multiple_of((half * PIECES + q) * piece, piece)
         vectors = jnp.concatenate(split(p, parts), axis=0)
         acc += jnp.dot(vectors, pair_ref[pl.ds(at, piece), :], preferred_element_type=F32)
@@ -234,7 +280,7 @@
         in_specs=[VMEM] * len(operands),
         out_specs=[VMEM] * len(shapes),
         out_shape=[pltpu.VMEM(s, F32) for s in shapes],
-        compiler_params=params(8),
+        compiler_params=params(4),
     )(*map(pin, operands))
 
 
@@ -242,16 +288,16 @@
     def moved(f, k):
         z, x, core = f // 8, f // 2 % 4, f % 2
         if core == stage:
-            z = (z + k) % 4
+            z = z ^ k
         else:
-            x = (x + k) % 4
+            x = x ^ k
         return z * 8 + x * 2 + core
 
     return [[(f, moved(f, k)) for f in range(32)] for k in (1, 2, 3)]
 
 
 CORE = [(f, f ^ 1) for f in range(32)]
-CONF = [[(c, (c + k) % 4) for c in range(4)] for k in (1, 2, 3)]
+CONF = [[(c, c ^ k) for c in range(4)] for k in (1, 2, 3)]
 
 
 def three(xs, axis, perms):
@@ -281,7 +327,7 @@
     away = [keep[i - 1] + got[i] for i in AWAY]
     (near,) = by_rows(near_kernel, [d, away[0]], pair, [shape])
     b, c, d = three(away, "feat", ring(0))
-    piece = (d + b) + (c + (near + got[0]))
+    piece = (b + c) + (d + (near + got[0]))
     return listed(order, [piece] + three([piece] * 3, "feat", ring(1)))
 
 
@@ -326,14 +372,14 @@
     for far_half, ps, images in ((0, p_own, i_own), (1, each(p_other), each(i_other))):
         half, start = place(far_half)
         for k in range(PIECES):
-            q = lax.rem(start - k + PIECES, PIECES)
+            q = start ^ k
             at = pl.ds(pl.multiple_of((half * PIECES + q) * piece, piece), piece)
             p = strips(ps[p_order.index(k)], piece)
             image = strips(images[i_order.index(k)], piece)
             res_ref[:, at] = r0_ref[:, at] - a0 * p - a1 * image
 
 
-ORDERS = (SECOND, SECOND, LAST, SECOND, SECOND, SECOND)
+ORDERS = (LAST, LAST, LAST, LAST, LAST, LAST)
 
 
 def body(matrix, targets):
@@ -342,12 +388,13 @@
     column = (MEMBERS, LANES)
 
     pair, part = first(targets, matrix)
+    flipped = flip(pair)
     order = ORDERS[0]
     parts = listed(order, [part] + three([part] * 3, "conf", CONF))
 
     all_pieces = (PIECES, size + TAIL, LANES)
     send, g0 = by_rows(
-        functools.partial(send_first_kernel, order), parts, pair, [all_pieces, (MEMBERS, n)])
+        functools.partial(send_first_kernel, order), parts + [flipped], pair, [all_pieces, (MEMBERS, n)])
     order = ORDERS[1]
     summands = reduce_pieces(order, g0, send, pair)
     p, gamma0 = on_core(
@@ -362,7 +409,7 @@
     parts = listed(order, [w] + three([w] * 3, "conf", CONF))
 
     send, g1, alpha0 = by_rows(
-        functools.partial(send_second_kernel, order), parts + [g0, gamma0], pair, [all_pieces, (MEMBERS, n), column]
+        functools.partial(send_second_kernel, order), parts + [g0, gamma0, flipped], pair, [all_pieces, (MEMBERS, n), column]
     )
     order = ORDERS[4]
     summands = reduce_pieces(order, g1, send, pair)
@@ -384,7 +431,7 @@
             jax.ShapeDtypeStruct((MEMBERS, n), F32),
             jax.ShapeDtypeStruct((MEMBERS, rows), F32),
         ],
-        compiler_params=params(8),
+        compiler_params=params(4),
     )(
         targets,
         alpha0,

time: 109 us -> 103 us (0.945)
  starting transfers between devices: 42.9 us -> 36 us
    ppermute x27, starting transfers between devices: 41.8 us -> 34.9 us  [three(): return [lax.ppermute(x, axis, perm) for x, perm in zip(xs, perms)]]
    pallas_call x0 -> x1, Pallas kernels: none -> 2.26 us  [flip(): pl.pallas_call(functools.partial(flip_kernel, chunk), in_specs=[VMEM], ou...]
    pallas_call x6, Pallas kernels: 13.3 us -> 11.5 us  [by_rows(): pl.pallas_call(kernel, in_specs=[VMEM] * (len(operands) + 1), out_specs=[...]
  transfers between devices with their start and end apart: 32 -> 32, of which waited for: 22 -> 20; matrix products, arithmetic and copies ran while one was open for 0% -> 0% of each run, Pallas kernels for 8% -> 11%
where the time goes in v2:
time: 103 us
  waiting for transfers between devices  37.9 us (37%)
  starting transfers between devices  36 us (35%)
  Pallas kernels  28.3 us (27%)
    ppermute x27, waiting for transfers between devices, three(): return [lax.ppermute(x, axis, perm) for x, perm in zip(xs, perms)]  36.6 us
    ppermute x27, starting transfers between devices, three(): return [lax.ppermute(x, axis, perm) for x, perm in zip(xs, perms)]  34.9 us
    pallas_call x6, Pallas kernels, by_rows(): pl.pallas_call(kernel, in_specs=[VMEM] * (len(operands) + 1), out_specs=[...  11.5 us
    pallas_call x1, Pallas kernels, first(): pl.pallas_call(functools.partial(first_kernel, blocks, depth, chunk, part...  9.09 us
    pallas_call x5, Pallas kernels, on_core(): pl.pallas_call(kernel, in_specs=[VMEM] * len(operands), out_specs=[VMEM]...  4.02 us
    pallas_call x1, Pallas kernels, flip(): pl.pallas_call(functools.partial(flip_kernel, chunk), in_specs=[VMEM], ou...  2.26 us
  transfers between devices with their start and end apart: 32, of which 20 were waited for; matrix products, arithmetic and copies ran while one was open for 0% of the time, Pallas kernels for 11%

profile of v2, /device:TPU:0, one launch (start us, length us, event | category | flops | bytes accessed | tf_op | source)
XLA Modules:
  0.0 103.3 jit_solution(10967709853158089854)
XLA Ops:
  0.6 9.1 %shard_map.41 = (bf16[8192,1280]{1,0:T(8,128)(2,1)S(1)}, f32[32,640]{1,0:T(8,128)S(1)}) custom-call(f32[32,8192]{1,0:T(8,128)} %refs_0_.1, f32[8192,640]{1,0:T(8,128)} %m_hbm.1), custom_call_target="tpu_custom_call" | custom-call | tf_op jit(solution)/shard_map/pallas_call | solution.py:123
  9.7 3.4 %collective-permute-start.2 = (f32[32,640]{1,0:T(8,128)S(1)}, f32[32,640]{1,0:T(8,128)S(1)}, u32[]{:S(2)}, u32[]{:S(2)}) collective-permute-start(f32[32,640]{1,0:T(8,128)S(1)} %get-tuple-element.13.a), channel_id=1, source_target_pairs={{0,2},{1,3},{2,0},{3,1},{4,6},{5,7},{6,4},{7,5},{8,10},{9,11},{10,... | collective-permute-start | bytes 245768 | tf_op jit(solution)/shard_map/ppermute | solution.py:304
  13.1 1.1 %collective-permute-start.1 = (f32[32,640]{1,0:T(8,128)S(1)}, f32[32,640]{1,0:T(8,128)S(1)}, u32[]{:S(2)}, u32[]{:S(2)}) collective-permute-start(f32[32,640]{1,0:T(8,128)S(1)} %get-tuple-element.13.a), channel_id=1, source_target_pairs={{0,3},{1,2},{2,1},{3,0},{4,7},{5,6},{6,5},{7,4},{8,11},{9,10},{10,... | collective-permute-start | bytes 245768 | tf_op jit(solution)/shard_map/ppermute | solution.py:304
  14.1 2.3 %shard_map.42.flipped_ref = bf16[1280,3072]{1,0:T(8,128)(2,1)S(1)} custom-call(bf16[8192,1280]{1,0:T(8,128)(2,1)S(1)} %get-tuple-element.14.pair_ref), custom_call_target="tpu_custom_call" | custom-call | bytes 20971520 | tf_op jit(solution)/shard_map/pallas_call | solution.py:175
  16.4 2.3 %collective-permute-done.1.c = f32[32,640]{1,0:T(8,128)S(1)} collective-permute-done((f32[32,640]{1,0:T(8,128)S(1)}, f32[32,640]{1,0:T(8,128)S(1)}, u32[]{:S(2)}, u32[]{:S(2)}) %collective-permute-start.1) | collective-permute-done | bytes 81952 | tf_op jit(solution)/shard_map/ppermute | solution.py:304
  18.7 2.2 %shard_map.43 = (f32[4,264,128]{2,1,0:T(8,128)S(1)}, f32[32,640]{1,0:T(8,128)S(1)}) custom-call(f32[32,640]{1,0:T(8,128)S(1)} %get-tuple-element.13.a, f32[32,640]{1,0:T(8,128)S(1)} %collective-permute-done.b, f32[32,640]{1,0:T(8,128)S(1)} %collective-permute-done.1.c, f32[32,640]{1,0:T(8,128)S(1)} %collective-permute-done.2.d, ...), custom_call_target="tpu_custom_call" | custom-call | tf_op jit(solution)/shard_map/pallas_call | solution.py:238
  21.1 2.4 %shard_map.44 = f32[3,264,128]{2,1,0:T(8,128)S(1)} custom-call(f32[32,640]{1,0:T(8,128)S(1)} %get-tuple-element.15.d_ref.g0_ref.refs_15_, bf16[8192,1280]{1,0:T(8,128)(2,1)S(1)} %get-tuple-element.14.pair_ref), custom_call_target="tpu_custom_call" | custom-call | tf_op jit(solution)/shard_map/pallas_call | solution.py:238
  23.5 4.0 %collective-permute-start.5 = (f32[264,128]{1,0:T(8,128)S(1)}, f32[264,128]{1,0:T(8,128)S(1)}, u32[]{:S(2)}, u32[]{:S(2)}) collective-permute-start(f32[264,128]{1,0:T(8,128)S(1)} %get-tuple-element.27), channel_id=1, source_target_pairs={{0,64},{4,20},{8,72},{12,28},{16,80},{20,4},{24,88},{28,12},{32,96... | collective-permute-start | bytes 405512 | tf_op jit(solution)/shard_map/ppermute | solution.py:304
  27.5 0.7 collective-permute-start.6
  28.5 1.1 %shard_map.45 = f32[264,128]{1,0:T(8,128)S(1)} custom-call(f32[32,640]{1,0:T(8,128)S(1)} %get-tuple-element.15.d_ref.g0_ref.refs_15_, f32[264,128]{1,0:T(8,128)S(1)} %get-tuple-element.29.after_ref, bf16[8192,1280]{1,0:T(8,128)(2,1)S(1)} %get-tuple-element.14.pair_ref), custom_call_target="tpu_custom_call" | custom-call | tf_op jit(solution)/shard_map/pallas_call | solution.py:238
  29.6 0.9 collective-permute-done.5
  30.5 3.2 %collective-permute-done.6 = f32[264,128]{1,0:T(8,128)S(1)} collective-permute-done((f32[264,128]{1,0:T(8,128)S(1)}, f32[264,128]{1,0:T(8,128)S(1)}, u32[]{:S(2)}, u32[]{:S(2)}) %collective-permute-start.6) | collective-permute-done | bytes 135200 | tf_op jit(solution)/shard_map/ppermute | solution.py:304
  33.8 3.1 %collective-permute-start.9 = (f32[264,128]{1,0:T(8,128)S(1)}, f32[264,128]{1,0:T(8,128)S(1)}, u32[]{:S(2)}, u32[]{:S(2)}) collective-permute-start(f32[264,128]{1,0:T(8,128)S(1)} %fusion.8.a), channel_id=1, source_target_pairs={{0,16},{4,68},{8,24},{12,76},{16,0},{20,84},{24,8},{28,92},{32,48}... | collective-permute-start | bytes 405512 | tf_op jit(solution)/shard_map/ppermute | solution.py:304
  36.9 1.1 %collective-permute-start.8 = (f32[264,128]{1,0:T(8,128)S(1)}, f32[264,128]{1,0:T(8,128)S(1)}, u32[]{:S(2)}, u32[]{:S(2)}) collective-permute-start(f32[264,128]{1,0:T(8,128)S(1)} %fusion.8.a), channel_id=1, source_target_pairs={{0,24},{4,100},{8,16},{12,108},{16,8},{20,116},{24,0},{28,124},{32... | collective-permute-start | bytes 405512 | tf_op jit(solution)/shard_map/ppermute | solution.py:304
  38.0 2.4 %collective-permute-done.9.d = f32[264,128]{1,0:T(8,128)S(1)} collective-permute-done((f32[264,128]{1,0:T(8,128)S(1)}, f32[264,128]{1,0:T(8,128)S(1)}, u32[]{:S(2)}, u32[]{:S(2)}) %collective-permute-start.9) | collective-permute-done | bytes 135200 | tf_op jit(solution)/shard_map/ppermute | solution.py:304
  40.4 2.7 %collective-permute-done.8.c = f32[264,128]{1,0:T(8,128)S(1)} collective-permute-done((f32[264,128]{1,0:T(8,128)S(1)}, f32[264,128]{1,0:T(8,128)S(1)}, u32[]{:S(2)}, u32[]{:S(2)}) %collective-permute-start.8) | collective-permute-done | bytes 135200 | tf_op jit(solution)/shard_map/ppermute | solution.py:304
  43.3 1.9 %collective-permute-start.12 = (f32[256,128]{1,0:T(8,128)S(1)}, f32[256,128]{1,0:T(8,128)S(1)}, u32[]{:S(2)}, u32[]{:S(2)}) collective-permute-start(f32[256,128]{1,0:T(8,128)S(1)} %get-tuple-element.17.a.before_ref.refs_5_), channel_id=1, source_target_pairs={{0,64},{4,20},{8,72},{12,28},{16,80},{20,4},{24,88},{28,12},{32,96... | collective-permute-start | bytes 393224 | tf_op jit(solution)/shard_map/ppermute | solution.py:304
  45.1 1.1 %collective-permute-start.11 = (f32[256,128]{1,0:T(8,128)S(1)}, f32[256,128]{1,0:T(8,128)S(1)}, u32[]{:S(2)}, u32[]{:S(2)}) collective-permute-start(f32[256,128]{1,0:T(8,128)S(1)} %get-tuple-element.17.a.before_ref.refs_5_), channel_id=1, source_target_pairs={{0,96},{4,28},{8,104},{12,20},{16,112},{20,12},{24,120},{28,4},{32... | collective-permute-start | bytes 393224 | tf_op jit(solution)/shard_map/ppermute | solution.py:304
  46.8 3.0 %collective-permute-done.12.d.refs_8_ = f32[256,128]{1,0:T(8,128)S(1)} collective-permute-done((f32[256,128]{1,0:T(8,128)S(1)}, f32[256,128]{1,0:T(8,128)S(1)}, u32[]{:S(2)}, u32[]{:S(2)}) %collective-permute-start.12) | collective-permute-done | bytes 131104 | tf_op jit(solution)/shard_map/ppermute | solution.py:304
  49.8 1.6 %collective-permute-done.11.c.refs_7_ = f32[256,128]{1,0:T(8,128)S(1)} collective-permute-done((f32[256,128]{1,0:T(8,128)S(1)}, f32[256,128]{1,0:T(8,128)S(1)}, u32[]{:S(2)}, u32[]{:S(2)}) %collective-permute-start.11) | collective-permute-done | bytes 131104 | tf_op jit(solution)/shard_map/ppermute | solution.py:304
  51.6 1.8 %shard_map.47.before_ref = f32[168,128]{1,0:T(8,128)S(1)} custom-call(f32[256,128]{1,0:T(8,128)S(1)} %get-tuple-element.17.a.before_ref.refs_5_, f32[256,128]{1,0:T(8,128)S(1)} %collective-permute-done.10.b.refs_6_, f32[256,128]{1,0:T(8,128)S(1)} %collective-permute-done.11.c.refs_7_, f32[256,128]{1,0:T(8,128)S(1)} %collective-permute-done.12.d.refs_8_, ...), custom_call_target="tpu_custom_call" | custom-call | tf_op jit(solution)/shard_map/pallas_call | solution.py:278
  53.5 1.8 %shard_map.48.a = f32[168,128]{1,0:T(8,128)S(1)} custom-call(f32[4,256,128]{2,1,0:T(8,128)S(1)} %collective-permute-done.13.p_ref.refs_9_, f32[168,128]{1,0:T(8,128)S(1)} %shard_map.47.before_ref, bf16[8192,1280]{1,0:T(8,128)(2,1)S(1)} %get-tuple-element.14.pair_ref), custom_call_target="tpu_custom_call" | custom-call | tf_op jit(solution)/shard_map/pallas_call | solution.py:278
  55.3 1.6 %collective-permute-start.16 = (f32[168,128]{1,0:T(8,128)S(1)}, f32[168,128]{1,0:T(8,128)S(1)}, u32[]{:S(2)}, u32[]{:S(2)}) collective-permute-start(f32[168,128]{1,0:T(8,128)S(1)} %shard_map.48.a), channel_id=1, source_target_pairs={{0,2},{1,3},{2,0},{3,1},{4,6},{5,7},{6,4},{7,5},{8,10},{9,11},{10,... | collective-permute-start | bytes 258056 | tf_op jit(solution)/shard_map/ppermute | solution.py:304
  56.9 1.4 %collective-permute-start.15 = (f32[168,128]{1,0:T(8,128)S(1)}, f32[168,128]{1,0:T(8,128)S(1)}, u32[]{:S(2)}, u32[]{:S(2)}) collective-permute-start(f32[168,128]{1,0:T(8,128)S(1)} %shard_map.48.a), channel_id=1, source_target_pairs={{0,3},{1,2},{2,1},{3,0},{4,7},{5,6},{6,5},{7,4},{8,11},{9,10},{10,... | collective-permute-start | bytes 258056 | tf_op jit(solution)/shard_map/ppermute | solution.py:304
  58.9 3.0 %collective-permute-done.16.d = f32[168,128]{1,0:T(8,128)S(1)} collective-permute-done((f32[168,128]{1,0:T(8,128)S(1)}, f32[168,128]{1,0:T(8,128)S(1)}, u32[]{:S(2)}, u32[]{:S(2)}) %collective-permute-start.16) | collective-permute-done | bytes 86048 | tf_op jit(solution)/shard_map/ppermute | solution.py:304
  61.9 1.7 %collective-permute-done.15.c = f32[168,128]{1,0:T(8,128)S(1)} collective-permute-done((f32[168,128]{1,0:T(8,128)S(1)}, f32[168,128]{1,0:T(8,128)S(1)}, u32[]{:S(2)}, u32[]{:S(2)}) %collective-permute-start.15) | collective-permute-done | bytes 86048 | tf_op jit(solution)/shard_map/ppermute | solution.py:304
  63.6 2.3 %shard_map.49 = (f32[4,264,128]{2,1,0:T(8,128)S(1)}, f32[32,640]{1,0:T(8,128)S(1)}, f32[32,128]{1,0:T(8,128)S(1)}) custom-call(f32[168,128]{1,0:T(8,128)S(1)} %shard_map.48.a, f32[168,128]{1,0:T(8,128)S(1)} %collective-permute-done.14.b, f32[168,128]{1,0:T(8,128)S(1)} %collective-permute-done.15.c, f32[168,128]{1,0:T(8,128)S(1)} %collective-permute-done.16.d, ...), custom_call_target="tpu_custom_call" | custom-call | tf_op jit(solution)/shard_map/pallas_call | solution.py:238
  66.1 2.4 %shard_map.50 = f32[3,264,128]{2,1,0:T(8,128)S(1)} custom-call(f32[32,640]{1,0:T(8,128)S(1)} %get-tuple-element.20.d_ref.refs_16_, bf16[8192,1280]{1,0:T(8,128)(2,1)S(1)} %get-tuple-element.14.pair_ref), custom_call_target="tpu_custom_call" | custom-call | tf_op jit(solution)/shard_map/pallas_call | solution.py:238
  68.6 1.9 %collective-permute-start.19 = (f32[264,128]{1,0:T(8,128)S(1)}, f32[264,128]{1,0:T(8,128)S(1)}, u32[]{:S(2)}, u32[]{:S(2)}) collective-permute-start(f32[264,128]{1,0:T(8,128)S(1)} %get-tuple-element.24), channel_id=1, source_target_pairs={{0,64},{4,20},{8,72},{12,28},{16,80},{20,4},{24,88},{28,12},{32,96... | collective-permute-start | bytes 405512 | tf_op jit(solution)/shard_map/ppermute | solution.py:304
  70.6 1.2 %collective-permute-start.20 = (f32[264,128]{1,0:T(8,128)S(1)}, f32[264,128]{1,0:T(8,128)S(1)}, u32[]{:S(2)}, u32[]{:S(2)}) collective-permute-start(f32[264,128]{1,0:T(8,128)S(1)} %get-tuple-element.25), channel_id=1, source_target_pairs={{0,96},{4,28},{8,104},{12,20},{16,112},{20,12},{24,120},{28,4},{32... | collective-permute-start | bytes 405512 | tf_op jit(solution)/shard_map/ppermute | solution.py:304
  72.2 1.1 %shard_map.51 = f32[264,128]{1,0:T(8,128)S(1)} custom-call(f32[32,640]{1,0:T(8,128)S(1)} %get-tuple-element.20.d_ref.refs_16_, f32[264,128]{1,0:T(8,128)S(1)} %get-tuple-element.26.after_ref, bf16[8192,1280]{1,0:T(8,128)(2,1)S(1)} %get-tuple-element.14.pair_ref), custom_call_target="tpu_custom_call" | custom-call | tf_op jit(solution)/shard_map/pallas_call | solution.py:238
  73.2 2.0 %collective-permute-done.19 = f32[264,128]{1,0:T(8,128)S(1)} collective-permute-done((f32[264,128]{1,0:T(8,128)S(1)}, f32[264,128]{1,0:T(8,128)S(1)}, u32[]{:S(2)}, u32[]{:S(2)}) %collective-permute-start.19) | collective-permute-done | bytes 135200 | tf_op jit(solution)/shard_map/ppermute | solution.py:304
  75.2 1.6 %collective-permute-done.20 = f32[264,128]{1,0:T(8,128)S(1)} collective-permute-done((f32[264,128]{1,0:T(8,128)S(1)}, f32[264,128]{1,0:T(8,128)S(1)}, u32[]{:S(2)}, u32[]{:S(2)}) %collective-permute-start.20) | collective-permute-done | bytes 135200 | tf_op jit(solution)/shard_map/ppermute | solution.py:304
  76.8 1.5 %collective-permute-start.23 = (f32[264,128]{1,0:T(8,128)S(1)}, f32[264,128]{1,0:T(8,128)S(1)}, u32[]{:S(2)}, u32[]{:S(2)}) collective-permute-start(f32[264,128]{1,0:T(8,128)S(1)} %fusion.2.a), channel_id=1, source_target_pairs={{0,16},{4,68},{8,24},{12,76},{16,0},{20,84},{24,8},{28,92},{32,48}... | collective-permute-start | bytes 405512 | tf_op jit(solution)/shard_map/ppermute | solution.py:304
  78.4 1.5 %collective-permute-start.22 = (f32[264,128]{1,0:T(8,128)S(1)}, f32[264,128]{1,0:T(8,128)S(1)}, u32[]{:S(2)}, u32[]{:S(2)}) collective-permute-start(f32[264,128]{1,0:T(8,128)S(1)} %fusion.2.a), channel_id=1, source_target_pairs={{0,24},{4,100},{8,16},{12,108},{16,8},{20,116},{24,0},{28,124},{32... | collective-permute-start | bytes 405512 | tf_op jit(solution)/shard_map/ppermute | solution.py:304
  80.4 3.1 %collective-permute-done.23.d = f32[264,128]{1,0:T(8,128)S(1)} collective-permute-done((f32[264,128]{1,0:T(8,128)S(1)}, f32[264,128]{1,0:T(8,128)S(1)}, u32[]{:S(2)}, u32[]{:S(2)}) %collective-permute-start.23) | collective-permute-done | bytes 135200 | tf_op jit(solution)/shard_map/ppermute | solution.py:304
  83.4 1.4 %collective-permute-done.22.c = f32[264,128]{1,0:T(8,128)S(1)} collective-permute-done((f32[264,128]{1,0:T(8,128)S(1)}, f32[264,128]{1,0:T(8,128)S(1)}, u32[]{:S(2)}, u32[]{:S(2)}) %collective-permute-start.22) | collective-permute-done | bytes 135200 | tf_op jit(solution)/shard_map/ppermute | solution.py:304
  85.0 1.9 %collective-permute-start.26 = (f32[256,128]{1,0:T(8,128)S(1)}, f32[256,128]{1,0:T(8,128)S(1)}, u32[]{:S(2)}, u32[]{:S(2)}) collective-permute-start(f32[256,128]{1,0:T(8,128)S(1)} %get-tuple-element.23.a.refs_10_), channel_id=1, source_target_pairs={{0,64},{4,20},{8,72},{12,28},{16,80},{20,4},{24,88},{28,12},{32,96... | collective-permute-start | bytes 393224 | tf_op jit(solution)/shard_map/ppermute | solution.py:304
  87.0 1.2 %collective-permute-start.25 = (f32[256,128]{1,0:T(8,128)S(1)}, f32[256,128]{1,0:T(8,128)S(1)}, u32[]{:S(2)}, u32[]{:S(2)}) collective-permute-start(f32[256,128]{1,0:T(8,128)S(1)} %get-tuple-element.23.a.refs_10_), channel_id=1, source_target_pairs={{0,96},{4,28},{8,104},{12,20},{16,112},{20,12},{24,120},{28,4},{32... | collective-permute-start | bytes 393224 | tf_op jit(solution)/shard_map/ppermute | solution.py:304
  88.6 3.0 %collective-permute-done.26.d.refs_13_ = f32[256,128]{1,0:T(8,128)S(1)} collective-permute-done((f32[256,128]{1,0:T(8,128)S(1)}, f32[256,128]{1,0:T(8,128)S(1)}, u32[]{:S(2)}, u32[]{:S(2)}) %collective-permute-start.26) | collective-permute-done | bytes 131104 | tf_op jit(solution)/shard_map/ppermute | solution.py:304
  91.6 1.6 %collective-permute-done.25.c.refs_12_ = f32[256,128]{1,0:T(8,128)S(1)} collective-permute-done((f32[256,128]{1,0:T(8,128)S(1)}, f32[256,128]{1,0:T(8,128)S(1)}, u32[]{:S(2)}, u32[]{:S(2)}) %collective-permute-start.25) | collective-permute-done | bytes 131104 | tf_op jit(solution)/shard_map/ppermute | solution.py:304
  93.4 0.6 collective-permute-start.27
  94.0 1.2 %collective-permute-done.27 = f32[32,128]{1,0:T(8,128)S(1)} collective-permute-done((f32[32,128]{1,0:T(8,128)S(1)}, f32[32,128]{1,0:T(8,128)S(1)}, u32[]{:S(2)}, u32[]{:S(2)}) %collective-permute-start.27) | collective-permute-done | bytes 16416 | tf_op jit(solution)/shard_map/ppermute | solution.py:422
  95.2 1.5 %collective-permute-start.30 = (f32[32,128]{1,0:T(8,128)S(1)}, f32[32,128]{1,0:T(8,128)S(1)}, u32[]{:S(2)}, u32[]{:S(2)}) collective-permute-start(f32[32,128]{1,0:T(8,128)S(1)} %add.90), channel_id=1, source_target_pairs={{0,2},{1,3},{2,0},{3,1},{4,6},{5,7},{6,4},{7,5},{8,10},{9,11},{10,... | collective-permute-start | bytes 49160 | tf_op jit(solution)/shard_map/ppermute | solution.py:304
  96.7 1.4 %collective-permute-start.29 = (f32[32,128]{1,0:T(8,128)S(1)}, f32[32,128]{1,0:T(8,128)S(1)}, u32[]{:S(2)}, u32[]{:S(2)}) collective-permute-start(f32[32,128]{1,0:T(8,128)S(1)} %add.90), channel_id=1, source_target_pairs={{0,3},{1,2},{2,1},{3,0},{4,7},{5,6},{6,5},{7,4},{8,11},{9,10},{10,... | collective-permute-start | bytes 49160 | tf_op jit(solution)/shard_map/ppermute | solution.py:304
  98.7 1.8 %collective-permute-done.30 = f32[32,128]{1,0:T(8,128)S(1)} collective-permute-done((f32[32,128]{1,0:T(8,128)S(1)}, f32[32,128]{1,0:T(8,128)S(1)}, u32[]{:S(2)}, u32[]{:S(2)}) %collective-permute-start.30) | collective-permute-done | bytes 16416 | tf_op jit(solution)/shard_map/ppermute | solution.py:304
  100.5 1.2 %collective-permute-done.29 = f32[32,128]{1,0:T(8,128)S(1)} collective-permute-done((f32[32,128]{1,0:T(8,128)S(1)}, f32[32,128]{1,0:T(8,128)S(1)}, u32[]{:S(2)}, u32[]{:S(2)}) %collective-permute-start.29) | collective-permute-done | bytes 16416 | tf_op jit(solution)/shard_map/ppermute | solution.py:304
  102.0 1.4 %shard_map.54 = (f32[32,640]{1,0:T(8,128)}, f32[32,8192]{1,0:T(8,128)}) custom-call(f32[32,8192]{1,0:T(8,128)S(1)} %copy-done, f32[32,128]{1,0:T(8,128)S(1)} %get-tuple-element.19.refs_1_, f32[32,128]{1,0:T(8,128)S(1)} %get-tuple-element.18.gamma_ref.gamma0_ref.refs_2_, f32[32,128]{1,0:T(8,128)S(1)} %get-tuple-element.22.refs_3_, ...), custom_call_target="tpu_custom_call" | custom-call | tf_op jit(solution)/shard_map/pallas_call | solution.py:426
  (40 shorter events, 4.9 us)
Async XLA Ops:
  9.7 6.7 %collective-permute-start.2 = (f32[32,640]{1,0:T(8,128)S(1)}, f32[32,640]{1,0:T(8,128)S(1)}, u32[]{:S(2)}, u32[]{:S(2)}) collective-permute-start(f32[32,640]{1,0:T(8,128)S(1)} %get-tuple-element.13.a), channel_id=1, source_target_pairs={{0,2},{1,3},{2,0},{3,1},{4,6},{5,7},{6,4},{7,5},{8,10},{9,11},{10,... | collective-permute-start | bytes 245768 | tf_op jit(solution)/shard_map/ppermute | solution.py:304
  13.1 5.7 %collective-permute-start.1 = (f32[32,640]{1,0:T(8,128)S(1)}, f32[32,640]{1,0:T(8,128)S(1)}, u32[]{:S(2)}, u32[]{:S(2)}) collective-permute-start(f32[32,640]{1,0:T(8,128)S(1)} %get-tuple-element.13.a), channel_id=1, source_target_pairs={{0,3},{1,2},{2,1},{3,0},{4,7},{5,6},{6,5},{7,4},{8,11},{9,10},{10,... | collective-permute-start | bytes 245768 | tf_op jit(solution)/shard_map/ppermute | solution.py:304
  14.1 4.6 %collective-permute-start = (f32[32,640]{1,0:T(8,128)S(1)}, f32[32,640]{1,0:T(8,128)S(1)}, u32[]{:S(2)}, u32[]{:S(2)}) collective-permute-start(f32[32,640]{1,0:T(8,128)S(1)} %get-tuple-element.13.a), channel_id=1, source_target_pairs={{0,1},{1,0},{2,3},{3,2},{4,5},{5,4},{6,7},{7,6},{8,9},{9,8},{10,11... | collective-permute-start | bytes 245768 | tf_op jit(solution)/shard_map/ppermute | solution.py:304
  21.0 2.5 %collective-permute-start.3 = (f32[4,264,128]{2,1,0:T(8,128)S(1)}, f32[4,264,128]{2,1,0:T(8,128)S(1)}, u32[]{:S(2)}, u32[]{:S(2)}) collective-permute-start(f32[4,264,128]{2,1,0:T(8,128)S(1)} %get-tuple-element.16), channel_id=1, source_target_pairs={{0,4},{4,0},{8,12},{12,8},{16,20},{20,16},{24,28},{28,24},{32,36},... | collective-permute-start | bytes 1622024 | tf_op jit(solution)/shard_map/ppermute | solution.py:325
  23.5 6.9 %collective-permute-start.5 = (f32[264,128]{1,0:T(8,128)S(1)}, f32[264,128]{1,0:T(8,128)S(1)}, u32[]{:S(2)}, u32[]{:S(2)}) collective-permute-start(f32[264,128]{1,0:T(8,128)S(1)} %get-tuple-element.27), channel_id=1, source_target_pairs={{0,64},{4,20},{8,72},{12,28},{16,80},{20,4},{24,88},{28,12},{32,96... | collective-permute-start | bytes 405512 | tf_op jit(solution)/shard_map/ppermute | solution.py:304
  27.5 6.2 %collective-permute-start.6 = (f32[264,128]{1,0:T(8,128)S(1)}, f32[264,128]{1,0:T(8,128)S(1)}, u32[]{:S(2)}, u32[]{:S(2)}) collective-permute-start(f32[264,128]{1,0:T(8,128)S(1)} %get-tuple-element.28), channel_id=1, source_target_pairs={{0,96},{4,28},{8,104},{12,20},{16,112},{20,12},{24,120},{28,4},{32... | collective-permute-start | bytes 405512 | tf_op jit(solution)/shard_map/ppermute | solution.py:304
  28.2 5.5 %collective-permute-start.4 = (f32[264,128]{1,0:T(8,128)S(1)}, f32[264,128]{1,0:T(8,128)S(1)}, u32[]{:S(2)}, u32[]{:S(2)}) collective-permute-start(f32[264,128]{1,0:T(8,128)S(1)} %get-tuple-element.29.after_ref), channel_id=1, source_target_pairs={{0,32},{4,12},{8,40},{12,4},{16,48},{20,28},{24,56},{28,20},{32,0}... | collective-permute-start | bytes 405512 | tf_op jit(solution)/shard_map/ppermute | solution.py:304
  33.8 6.6 %collective-permute-start.9 = (f32[264,128]{1,0:T(8,128)S(1)}, f32[264,128]{1,0:T(8,128)S(1)}, u32[]{:S(2)}, u32[]{:S(2)}) collective-permute-start(f32[264,128]{1,0:T(8,128)S(1)} %fusion.8.a), channel_id=1, source_target_pairs={{0,16},{4,68},{8,24},{12,76},{16,0},{20,84},{24,8},{28,92},{32,48}... | collective-permute-start | bytes 405512 | tf_op jit(solution)/shard_map/ppermute | solution.py:304
  36.9 6.2 %collective-permute-start.8 = (f32[264,128]{1,0:T(8,128)S(1)}, f32[264,128]{1,0:T(8,128)S(1)}, u32[]{:S(2)}, u32[]{:S(2)}) collective-permute-start(f32[264,128]{1,0:T(8,128)S(1)} %fusion.8.a), channel_id=1, source_target_pairs={{0,24},{4,100},{8,16},{12,108},{16,8},{20,116},{24,0},{28,124},{32... | collective-permute-start | bytes 405512 | tf_op jit(solution)/shard_map/ppermute | solution.py:304
  38.0 5.1 %collective-permute-start.7 = (f32[264,128]{1,0:T(8,128)S(1)}, f32[264,128]{1,0:T(8,128)S(1)}, u32[]{:S(2)}, u32[]{:S(2)}) collective-permute-start(f32[264,128]{1,0:T(8,128)S(1)} %fusion.8.a), channel_id=1, source_target_pairs={{0,8},{4,36},{8,0},{12,44},{16,24},{20,52},{24,16},{28,60},{32,40}... | collective-permute-start | bytes 405512 | tf_op jit(solution)/shard_map/ppermute | solution.py:304
  43.3 6.5 %collective-permute-start.12 = (f32[256,128]{1,0:T(8,128)S(1)}, f32[256,128]{1,0:T(8,128)S(1)}, u32[]{:S(2)}, u32[]{:S(2)}) collective-permute-start(f32[256,128]{1,0:T(8,128)S(1)} %get-tuple-element.17.a.before_ref.refs_5_), channel_id=1, source_target_pairs={{0,64},{4,20},{8,72},{12,28},{16,80},{20,4},{24,88},{28,12},{32,96... | collective-permute-start | bytes 393224 | tf_op jit(solution)/shard_map/ppermute | solution.py:304
  45.1 6.2 %collective-permute-start.11 = (f32[256,128]{1,0:T(8,128)S(1)}, f32[256,128]{1,0:T(8,128)S(1)}, u32[]{:S(2)}, u32[]{:S(2)}) collective-permute-start(f32[256,128]{1,0:T(8,128)S(1)} %get-tuple-element.17.a.before_ref.refs_5_), channel_id=1, source_target_pairs={{0,96},{4,28},{8,104},{12,20},{16,112},{20,12},{24,120},{28,4},{32... | collective-permute-start | bytes 393224 | tf_op jit(solution)/shard_map/ppermute | solution.py:304
  46.2 5.1 %collective-permute-start.10 = (f32[256,128]{1,0:T(8,128)S(1)}, f32[256,128]{1,0:T(8,128)S(1)}, u32[]{:S(2)}, u32[]{:S(2)}) collective-permute-start(f32[256,128]{1,0:T(8,128)S(1)} %get-tuple-element.17.a.before_ref.refs_5_), channel_id=1, source_target_pairs={{0,32},{4,12},{8,40},{12,4},{16,48},{20,28},{24,56},{28,20},{32,0}... | collective-permute-start | bytes 393224 | tf_op jit(solution)/shard_map/ppermute | solution.py:304
  51.4 2.2 %collective-permute-start.13 = (f32[4,256,128]{2,1,0:T(8,128)S(1)}, f32[4,256,128]{2,1,0:T(8,128)S(1)}, u32[]{:S(2)}, u32[]{:S(2)}) collective-permute-start(f32[4,256,128]{2,1,0:T(8,128)S(1)} %pad_maximum_fusion), channel_id=1, source_target_pairs={{0,4},{4,0},{8,12},{12,8},{16,20},{20,16},{24,28},{28,24},{32,36},... | collective-permute-start | bytes 1572872 | tf_op jit(solution)/shard_map/ppermute | solution.py:403
  55.3 6.6 %collective-permute-start.16 = (f32[168,128]{1,0:T(8,128)S(1)}, f32[168,128]{1,0:T(8,128)S(1)}, u32[]{:S(2)}, u32[]{:S(2)}) collective-permute-start(f32[168,128]{1,0:T(8,128)S(1)} %shard_map.48.a), channel_id=1, source_target_pairs={{0,2},{1,3},{2,0},{3,1},{4,6},{5,7},{6,4},{7,5},{8,10},{9,11},{10,... | collective-permute-start | bytes 258056 | tf_op jit(solution)/shard_map/ppermute | solution.py:304
  56.9 6.7 %collective-permute-start.15 = (f32[168,128]{1,0:T(8,128)S(1)}, f32[168,128]{1,0:T(8,128)S(1)}, u32[]{:S(2)}, u32[]{:S(2)}) collective-permute-start(f32[168,128]{1,0:T(8,128)S(1)} %shard_map.48.a), channel_id=1, source_target_pairs={{0,3},{1,2},{2,1},{3,0},{4,7},{5,6},{6,5},{7,4},{8,11},{9,10},{10,... | collective-permute-start | bytes 258056 | tf_op jit(solution)/shard_map/ppermute | solution.py:304
  58.4 5.3 %collective-permute-start.14 = (f32[168,128]{1,0:T(8,128)S(1)}, f32[168,128]{1,0:T(8,128)S(1)}, u32[]{:S(2)}, u32[]{:S(2)}) collective-permute-start(f32[168,128]{1,0:T(8,128)S(1)} %shard_map.48.a), channel_id=1, source_target_pairs={{0,1},{1,0},{2,3},{3,2},{4,5},{5,4},{6,7},{7,6},{8,9},{9,8},{10,11... | collective-permute-start | bytes 258056 | tf_op jit(solution)/shard_map/ppermute | solution.py:304
  66.0 2.5 %collective-permute-start.17 = (f32[4,264,128]{2,1,0:T(8,128)S(1)}, f32[4,264,128]{2,1,0:T(8,128)S(1)}, u32[]{:S(2)}, u32[]{:S(2)}) collective-permute-start(f32[4,264,128]{2,1,0:T(8,128)S(1)} %get-tuple-element.21), channel_id=1, source_target_pairs={{0,4},{4,0},{8,12},{12,8},{16,20},{20,16},{24,28},{28,24},{32,36},... | collective-permute-start | bytes 1622024 | tf_op jit(solution)/shard_map/ppermute | solution.py:325
  66.1 35.8 %copy-start = (f32[32,8192]{1,0:T(8,128)S(1)}, f32[32,8192]{1,0:T(8,128)}, u32[]{:S(2)}) copy-start(f32[32,8192]{1,0:T(8,128)} %refs_0_.1) | copy-start | bytes 3145732
  68.6 6.6 %collective-permute-start.19 = (f32[264,128]{1,0:T(8,128)S(1)}, f32[264,128]{1,0:T(8,128)S(1)}, u32[]{:S(2)}, u32[]{:S(2)}) collective-permute-start(f32[264,128]{1,0:T(8,128)S(1)} %get-tuple-element.24), channel_id=1, source_target_pairs={{0,64},{4,20},{8,72},{12,28},{16,80},{20,4},{24,88},{28,12},{32,96... | collective-permute-start | bytes 405512 | tf_op jit(solution)/shard_map/ppermute | solution.py:304
  70.6 6.2 %collective-permute-start.20 = (f32[264,128]{1,0:T(8,128)S(1)}, f32[264,128]{1,0:T(8,128)S(1)}, u32[]{:S(2)}, u32[]{:S(2)}) collective-permute-start(f32[264,128]{1,0:T(8,128)S(1)} %get-tuple-element.25), channel_id=1, source_target_pairs={{0,96},{4,28},{8,104},{12,20},{16,112},{20,12},{24,120},{28,4},{32... | collective-permute-start | bytes 405512 | tf_op jit(solution)/shard_map/ppermute | solution.py:304
  71.8 5.0 %collective-permute-start.18 = (f32[264,128]{1,0:T(8,128)S(1)}, f32[264,128]{1,0:T(8,128)S(1)}, u32[]{:S(2)}, u32[]{:S(2)}) collective-permute-start(f32[264,128]{1,0:T(8,128)S(1)} %get-tuple-element.26.after_ref), channel_id=1, source_target_pairs={{0,32},{4,12},{8,40},{12,4},{16,48},{20,28},{24,56},{28,20},{32,0}... | collective-permute-start | bytes 405512 | tf_op jit(solution)/shard_map/ppermute | solution.py:304
  76.8 6.6 %collective-permute-start.23 = (f32[264,128]{1,0:T(8,128)S(1)}, f32[264,128]{1,0:T(8,128)S(1)}, u32[]{:S(2)}, u32[]{:S(2)}) collective-permute-start(f32[264,128]{1,0:T(8,128)S(1)} %fusion.2.a), channel_id=1, source_target_pairs={{0,16},{4,68},{8,24},{12,76},{16,0},{20,84},{24,8},{28,92},{32,48}... | collective-permute-start | bytes 405512 | tf_op jit(solution)/shard_map/ppermute | solution.py:304
  78.4 6.5 %collective-permute-start.22 = (f32[264,128]{1,0:T(8,128)S(1)}, f32[264,128]{1,0:T(8,128)S(1)}, u32[]{:S(2)}, u32[]{:S(2)}) collective-permute-start(f32[264,128]{1,0:T(8,128)S(1)} %fusion.2.a), channel_id=1, source_target_pairs={{0,24},{4,100},{8,16},{12,108},{16,8},{20,116},{24,0},{28,124},{32... | collective-permute-start | bytes 405512 | tf_op jit(solution)/shard_map/ppermute | solution.py:304
  79.9 5.0 %collective-permute-start.21 = (f32[264,128]{1,0:T(8,128)S(1)}, f32[264,128]{1,0:T(8,128)S(1)}, u32[]{:S(2)}, u32[]{:S(2)}) collective-permute-start(f32[264,128]{1,0:T(8,128)S(1)} %fusion.2.a), channel_id=1, source_target_pairs={{0,8},{4,36},{8,0},{12,44},{16,24},{20,52},{24,16},{28,60},{32,40}... | collective-permute-start | bytes 405512 | tf_op jit(solution)/shard_map/ppermute | solution.py:304
  85.0 6.6 %collective-permute-start.26 = (f32[256,128]{1,0:T(8,128)S(1)}, f32[256,128]{1,0:T(8,128)S(1)}, u32[]{:S(2)}, u32[]{:S(2)}) collective-permute-start(f32[256,128]{1,0:T(8,128)S(1)} %get-tuple-element.23.a.refs_10_), channel_id=1, source_target_pairs={{0,64},{4,20},{8,72},{12,28},{16,80},{20,4},{24,88},{28,12},{32,96... | collective-permute-start | bytes 393224 | tf_op jit(solution)/shard_map/ppermute | solution.py:304
  87.0 6.2 %collective-permute-start.25 = (f32[256,128]{1,0:T(8,128)S(1)}, f32[256,128]{1,0:T(8,128)S(1)}, u32[]{:S(2)}, u32[]{:S(2)}) collective-permute-start(f32[256,128]{1,0:T(8,128)S(1)} %get-tuple-element.23.a.refs_10_), channel_id=1, source_target_pairs={{0,96},{4,28},{8,104},{12,20},{16,112},{20,12},{24,120},{28,4},{32... | collective-permute-start | bytes 393224 | tf_op jit(solution)/shard_map/ppermute | solution.py:304
  88.2 5.0 %collective-permute-start.24 = (f32[256,128]{1,0:T(8,128)S(1)}, f32[256,128]{1,0:T(8,128)S(1)}, u32[]{:S(2)}, u32[]{:S(2)}) collective-permute-start(f32[256,128]{1,0:T(8,128)S(1)} %get-tuple-element.23.a.refs_10_), channel_id=1, source_target_pairs={{0,32},{4,12},{8,40},{12,4},{16,48},{20,28},{24,56},{28,20},{32,0}... | collective-permute-start | bytes 393224 | tf_op jit(solution)/shard_map/ppermute | solution.py:304
  93.2 8.7 %collective-permute-start.31 = (f32[4,256,128]{2,1,0:T(8,128)S(1)}, f32[4,256,128]{2,1,0:T(8,128)S(1)}, u32[]{:S(2)}, u32[]{:S(2)}) collective-permute-start(f32[4,256,128]{2,1,0:T(8,128)S(1)} %pad_maximum_fusion.1), channel_id=1, source_target_pairs={{0,4},{4,0},{8,12},{12,8},{16,20},{20,16},{24,28},{28,24},{32,36},... | collective-permute-start | bytes 1572872 | tf_op jit(solution)/shard_map/ppermute | solution.py:424
  93.4 1.8 %collective-permute-start.27 = (f32[32,128]{1,0:T(8,128)S(1)}, f32[32,128]{1,0:T(8,128)S(1)}, u32[]{:S(2)}, u32[]{:S(2)}) collective-permute-start(f32[32,128]{1,0:T(8,128)S(1)} %shard_map.53), channel_id=1, source_target_pairs={{0,4},{4,0},{8,12},{12,8},{16,20},{20,16},{24,28},{28,24},{32,36},... | collective-permute-start | bytes 49160 | tf_op jit(solution)/shard_map/ppermute | solution.py:422
  95.2 5.2 %collective-permute-start.30 = (f32[32,128]{1,0:T(8,128)S(1)}, f32[32,128]{1,0:T(8,128)S(1)}, u32[]{:S(2)}, u32[]{:S(2)}) collective-permute-start(f32[32,128]{1,0:T(8,128)S(1)} %add.90), channel_id=1, source_target_pairs={{0,2},{1,3},{2,0},{3,1},{4,6},{5,7},{6,4},{7,5},{8,10},{9,11},{10,... | collective-permute-start | bytes 49160 | tf_op jit(solution)/shard_map/ppermute | solution.py:304
  96.7 4.9 %collective-permute-start.29 = (f32[32,128]{1,0:T(8,128)S(1)}, f32[32,128]{1,0:T(8,128)S(1)}, u32[]{:S(2)}, u32[]{:S(2)}) collective-permute-start(f32[32,128]{1,0:T(8,128)S(1)} %add.90), channel_id=1, source_target_pairs={{0,3},{1,2},{2,1},{3,0},{4,7},{5,6},{6,5},{7,4},{8,11},{9,10},{10,... | collective-permute-start | bytes 49160 | tf_op jit(solution)/shard_map/ppermute | solution.py:304
  98.2 3.7 %collective-permute-start.28 = (f32[32,128]{1,0:T(8,128)S(1)}, f32[32,128]{1,0:T(8,128)S(1)}, u32[]{:S(2)}, u32[]{:S(2)}) collective-permute-start(f32[32,128]{1,0:T(8,128)S(1)} %add.90), channel_id=1, source_target_pairs={{0,1},{1,0},{2,3},{3,2},{4,5},{5,4},{6,7},{7,6},{8,9},{9,8},{10,11... | collective-permute-start | bytes 49160 | tf_op jit(solution)/shard_map/ppermute | solution.py:304

commit v3 on v2

--- a/solution.py
+++ b/solution.py
@@ -118,7 +118,7 @@
     g_ref[...] = fold(acc_ref[...], parts)
 
 
-def first(residual, matrix, blocks=8, depth=3, chunk=512, parts=3):
+def first(residual, matrix, blocks=8, depth=4, chunk=512, parts=3):
     rows, n = matrix.shape
     return pl.pallas_call(
         functools.partial(first_kernel, blocks, depth, chunk, parts),
@@ -132,7 +132,7 @@
             pltpu.SemaphoreType.DMA,
             pltpu.SemaphoreType.DMA((depth,)),
         ],
-        compiler_params=params(11),
+        compiler_params=params(14),
     )(far(residual), far(matrix))
 
 
@@ -258,12 +258,19 @@
     return fold(acc, parts), norm
 
 
-def cols_own_kernel(order, a, b, c, d, pair_ref, w_ref):
+def cols_near_kernel(p_ref, pair_ref, w_ref):
     piece = pair_ref.shape[0] // (2 * PIECES)
-    pieces = [strips(p, piece) for p in (a, b, c, d)]
-    w, norm = cols_body(*place(0), order, pieces, pair_ref)
+    w, norm = cols_body(*place(0), (0,), [strips(p_ref, piece)], pair_ref)
     put(w_ref, w)
     put_sums(w_ref, norm)
+
+
+def cols_own_kernel(order, b, c, d, before_ref, pair_ref, w_ref):
+    piece = pair_ref.shape[0] // (2 * PIECES)
+    pieces = [strips(p, piece) for p in (b, c, d)]
+    w, norm = cols_body(*place(0), order[1:], pieces, pair_ref)
+    put(w_ref, w + strips(before_ref, w.shape[1]))
+    put_sums(w_ref, norm + sums_of(before_ref))
 
 
 def cols_other_kernel(order, p_ref, before_ref, pair_ref, w_ref):
@@ -349,13 +356,20 @@
 
 
 def curve_kernel(a, b, c, d, curve_ref):
-    norm = sum(jnp.sum(strips(p, p.shape[0] * LANES // MEMBERS) ** 2, axis=1, keepdims=True) for p in (a, b, c, d))
-    curve_ref[...] = wide(norm)
-
-
-def gather_pieces(order, piece):
+    width = a.shape[0] * LANES // MEMBERS
+    squares = [jnp.square(strips(p, width)) for p in (a, b, c, d)]
+    put_sums(curve_ref, jnp.sum(sum(squares), axis=1, keepdims=True))
+
+
+def stack_kernel(a, b, c, d, after_ref, out_ref):
+    for i, x in enumerate((a, b, c, d)):
+        out_ref[i] = x[...]
+
+
+def gather_pieces(order, piece, after):
     own = listed(order, [piece] + three([piece] * 3, "feat", ring(0)))
-    return own, jnp.stack(own)
+    (stacked,) = on_core(stack_kernel, own + [after], [(PIECES, *piece.shape)])
+    return own, stacked
 
 
 def finish_kernel(p_order, i_order, *refs):
@@ -364,7 +378,7 @@
     g0_ref, g1_ref, sol_ref, res_ref = refs[15:]
     gamma1 = gamma1_ref[:, :1]
     a0 = alpha0_ref[:, :1]
-    a1 = gamma1 / curve_ref[:, :1]
+    a1 = gamma1 / sums_of(curve_ref[...])
     b0 = gamma1 / gamma0_ref[:, :1]
     g0 = g0_ref[...]
     sol_ref[...] = a0 * g0 + a1 * (g1_ref[...] + b0 * g0)
@@ -399,11 +413,12 @@
     summands = reduce_pieces(order, g0, send, pair)
     p, gamma0 = on_core(
         functools.partial(piece_kernel, order), summands, [(size, LANES), column])
-    p_own, stacked = gather_pieces(ORDERS[2], p)
+    packed = [(MEMBERS * n // LANES + TAIL, LANES)]
+    (w,) = on_core(cols_near_kernel, [p, pair], packed)
+    p_own, stacked = gather_pieces(ORDERS[2], p, w)
     p_other = lax.ppermute(stacked, "feat", CORE)
 
-    packed = [(MEMBERS * n // LANES + TAIL, LANES)]
-    (w,) = on_core(functools.partial(cols_own_kernel, ORDERS[2]), p_own + [pair], packed)
+    (w,) = on_core(functools.partial(cols_own_kernel, ORDERS[2]), p_own[1:] + [w, pair], packed)
     (w,) = on_core(functools.partial(cols_other_kernel, ORDERS[2]), [p_other, w, pair], packed)
     order = ORDERS[3]
     parts = listed(order, [w] + three([w] * 3, "conf", CONF))
@@ -416,9 +431,9 @@
     image, gamma1 = on_core(
         functools.partial(image_kernel, order), summands + [p, gamma0], [(size, LANES), column]
     )
-    i_own, stacked = gather_pieces(ORDERS[5], image)
-
-    (curve,) = on_core(curve_kernel, i_own, [column])
+    i_own, stacked = gather_pieces(ORDERS[5], image, gamma1)
+
+    (curve,) = on_core(curve_kernel, i_own, [(TAIL, LANES)])
     curve = curve + lax.ppermute(curve, "feat", CORE)
     curve = total(curve, three([curve] * 3, "conf", CONF))
     i_other = lax.ppermute(stacked, "feat", CORE)

time: 103 us -> 103 us (level)
    pallas_call x5 -> x8, Pallas kernels: 4.02 us -> 4.17 us  [on_core(): pl.pallas_call(kernel, in_specs=[VMEM] * len(operands), out_specs=[VMEM]...]
where the time goes in v3:
time: 103 us
  waiting for transfers between devices  37.4 us (36%)
  starting transfers between devices  35.9 us (35%)
  Pallas kernels  28.3 us (27%)
    ppermute x27, waiting for transfers between devices, three(): return [lax.ppermute(x, axis, perm) for x, perm in zip(xs, perms)]  35.6 us
    ppermute x27, starting transfers between devices, three(): return [lax.ppermute(x, axis, perm) for x, perm in zip(xs, perms)]  34.9 us
    pallas_call x6, Pallas kernels, by_rows(): pl.pallas_call(kernel, in_specs=[VMEM] * (len(operands) + 1), out_specs=[...  11.5 us
    pallas_call x1, Pallas kernels, first(): pl.pallas_call(functools.partial(first_kernel, blocks, depth, chunk, part...  8.97 us
    pallas_call x8, Pallas kernels, on_core(): pl.pallas_call(kernel, in_specs=[VMEM] * len(operands), out_specs=[VMEM]...  4.17 us
    pallas_call x1, Pallas kernels, flip(): pl.pallas_call(functools.partial(flip_kernel, chunk), in_specs=[VMEM], ou...  2.26 us
  transfers between devices with their start and end apart: 32, of which 20 were waited for; matrix products, arithmetic and copies ran while one was open for 0% of the time, Pallas kernels for 11%

profile of v3, /device:TPU:0, one launch (start us, length us, event | category | flops | bytes accessed | tf_op | source)
XLA Modules:
  0.0 102.7 jit_solution(14750573934539009822)
XLA Ops:
  0.6 9.0 %shard_map.41 = (bf16[8192,1280]{1,0:T(8,128)(2,1)S(1)}, f32[32,640]{1,0:T(8,128)S(1)}) custom-call(f32[32,8192]{1,0:T(8,128)} %refs_0_.1, f32[8192,640]{1,0:T(8,128)} %m_hbm.1), custom_call_target="tpu_custom_call" | custom-call | tf_op jit(solution)/shard_map/pallas_call | solution.py:123
  9.6 3.4 %collective-permute-start.2 = (f32[32,640]{1,0:T(8,128)S(1)}, f32[32,640]{1,0:T(8,128)S(1)}, u32[]{:S(2)}, u32[]{:S(2)}) collective-permute-start(f32[32,640]{1,0:T(8,128)S(1)} %get-tuple-element.13.a), channel_id=1, source_target_pairs={{0,2},{1,3},{2,0},{3,1},{4,6},{5,7},{6,4},{7,5},{8,10},{9,11},{10,... | collective-permute-start | bytes 245768 | tf_op jit(solution)/shard_map/ppermute | solution.py:311
  13.0 1.1 %collective-permute-start.1 = (f32[32,640]{1,0:T(8,128)S(1)}, f32[32,640]{1,0:T(8,128)S(1)}, u32[]{:S(2)}, u32[]{:S(2)}) collective-permute-start(f32[32,640]{1,0:T(8,128)S(1)} %get-tuple-element.13.a), channel_id=1, source_target_pairs={{0,3},{1,2},{2,1},{3,0},{4,7},{5,6},{6,5},{7,4},{8,11},{9,10},{10,... | collective-permute-start | bytes 245768 | tf_op jit(solution)/shard_map/ppermute | solution.py:311
  14.0 2.3 %shard_map.42.flipped_ref = bf16[1280,3072]{1,0:T(8,128)(2,1)S(1)} custom-call(bf16[8192,1280]{1,0:T(8,128)(2,1)S(1)} %get-tuple-element.14.pair_ref), custom_call_target="tpu_custom_call" | custom-call | bytes 20971520 | tf_op jit(solution)/shard_map/pallas_call | solution.py:175
  16.3 2.3 %collective-permute-done.1.c = f32[32,640]{1,0:T(8,128)S(1)} collective-permute-done((f32[32,640]{1,0:T(8,128)S(1)}, f32[32,640]{1,0:T(8,128)S(1)}, u32[]{:S(2)}, u32[]{:S(2)}) %collective-permute-start.1) | collective-permute-done | bytes 81952 | tf_op jit(solution)/shard_map/ppermute | solution.py:311
  18.6 2.2 %shard_map.43 = (f32[4,264,128]{2,1,0:T(8,128)S(1)}, f32[32,640]{1,0:T(8,128)S(1)}) custom-call(f32[32,640]{1,0:T(8,128)S(1)} %get-tuple-element.13.a, f32[32,640]{1,0:T(8,128)S(1)} %collective-permute-done.b, f32[32,640]{1,0:T(8,128)S(1)} %collective-permute-done.1.c, f32[32,640]{1,0:T(8,128)S(1)} %collective-permute-done.2.d, ...), custom_call_target="tpu_custom_call" | custom-call | tf_op jit(solution)/shard_map/pallas_call | solution.py:238
  21.0 2.4 %shard_map.44 = f32[3,264,128]{2,1,0:T(8,128)S(1)} custom-call(f32[32,640]{1,0:T(8,128)S(1)} %get-tuple-element.15.d_ref.g0_ref.refs_15_, bf16[8192,1280]{1,0:T(8,128)(2,1)S(1)} %get-tuple-element.14.pair_ref), custom_call_target="tpu_custom_call" | custom-call | tf_op jit(solution)/shard_map/pallas_call | solution.py:238
  23.4 3.9 %collective-permute-start.5 = (f32[264,128]{1,0:T(8,128)S(1)}, f32[264,128]{1,0:T(8,128)S(1)}, u32[]{:S(2)}, u32[]{:S(2)}) collective-permute-start(f32[264,128]{1,0:T(8,128)S(1)} %get-tuple-element.27), channel_id=1, source_target_pairs={{0,64},{4,20},{8,72},{12,28},{16,80},{20,4},{24,88},{28,12},{32,96... | collective-permute-start | bytes 405512 | tf_op jit(solution)/shard_map/ppermute | solution.py:311
  27.4 0.7 collective-permute-start.6
  28.4 1.1 %shard_map.45 = f32[264,128]{1,0:T(8,128)S(1)} custom-call(f32[32,640]{1,0:T(8,128)S(1)} %get-tuple-element.15.d_ref.g0_ref.refs_15_, f32[264,128]{1,0:T(8,128)S(1)} %get-tuple-element.29.after_ref, bf16[8192,1280]{1,0:T(8,128)(2,1)S(1)} %get-tuple-element.14.pair_ref), custom_call_target="tpu_custom_call" | custom-call | tf_op jit(solution)/shard_map/pallas_call | solution.py:238
  29.5 0.9 collective-permute-done.5
  30.4 3.2 %collective-permute-done.6 = f32[264,128]{1,0:T(8,128)S(1)} collective-permute-done((f32[264,128]{1,0:T(8,128)S(1)}, f32[264,128]{1,0:T(8,128)S(1)}, u32[]{:S(2)}, u32[]{:S(2)}) %collective-permute-start.6) | collective-permute-done | bytes 135200 | tf_op jit(solution)/shard_map/ppermute | solution.py:311
  33.7 3.1 %collective-permute-start.9 = (f32[264,128]{1,0:T(8,128)S(1)}, f32[264,128]{1,0:T(8,128)S(1)}, u32[]{:S(2)}, u32[]{:S(2)}) collective-permute-start(f32[264,128]{1,0:T(8,128)S(1)} %fusion.8.a), channel_id=1, source_target_pairs={{0,16},{4,68},{8,24},{12,76},{16,0},{20,84},{24,8},{28,92},{32,48}... | collective-permute-start | bytes 405512 | tf_op jit(solution)/shard_map/ppermute | solution.py:311
  36.8 1.1 %collective-permute-start.8 = (f32[264,128]{1,0:T(8,128)S(1)}, f32[264,128]{1,0:T(8,128)S(1)}, u32[]{:S(2)}, u32[]{:S(2)}) collective-permute-start(f32[264,128]{1,0:T(8,128)S(1)} %fusion.8.a), channel_id=1, source_target_pairs={{0,24},{4,100},{8,16},{12,108},{16,8},{20,116},{24,0},{28,124},{32... | collective-permute-start | bytes 405512 | tf_op jit(solution)/shard_map/ppermute | solution.py:311
  37.9 2.3 %collective-permute-done.9.d = f32[264,128]{1,0:T(8,128)S(1)} collective-permute-done((f32[264,128]{1,0:T(8,128)S(1)}, f32[264,128]{1,0:T(8,128)S(1)}, u32[]{:S(2)}, u32[]{:S(2)}) %collective-permute-start.9) | collective-permute-done | bytes 135200 | tf_op jit(solution)/shard_map/ppermute | solution.py:311
  40.3 2.7 %collective-permute-done.8.c = f32[264,128]{1,0:T(8,128)S(1)} collective-permute-done((f32[264,128]{1,0:T(8,128)S(1)}, f32[264,128]{1,0:T(8,128)S(1)}, u32[]{:S(2)}, u32[]{:S(2)}) %collective-permute-start.8) | collective-permute-done | bytes 135200 | tf_op jit(solution)/shard_map/ppermute | solution.py:311
  43.1 1.9 %collective-permute-start.12 = (f32[256,128]{1,0:T(8,128)S(1)}, f32[256,128]{1,0:T(8,128)S(1)}, u32[]{:S(2)}, u32[]{:S(2)}) collective-permute-start(f32[256,128]{1,0:T(8,128)S(1)} %get-tuple-element.17.p_ref.a.before_ref.refs_5_), channel_id=1, source_target_pairs={{0,64},{4,20},{8,72},{12,28},{16,80},{20,4},{24,88},{28,12},{32,96... | collective-permute-start | bytes 393224 | tf_op jit(solution)/shard_map/ppermute | solution.py:311
  45.0 1.1 %collective-permute-start.11 = (f32[256,128]{1,0:T(8,128)S(1)}, f32[256,128]{1,0:T(8,128)S(1)}, u32[]{:S(2)}, u32[]{:S(2)}) collective-permute-start(f32[256,128]{1,0:T(8,128)S(1)} %get-tuple-element.17.p_ref.a.before_ref.refs_5_), channel_id=1, source_target_pairs={{0,96},{4,28},{8,104},{12,20},{16,112},{20,12},{24,120},{28,4},{32... | collective-permute-start | bytes 393224 | tf_op jit(solution)/shard_map/ppermute | solution.py:311
  47.2 2.4 %collective-permute-done.12.d.refs_8_ = f32[256,128]{1,0:T(8,128)S(1)} collective-permute-done((f32[256,128]{1,0:T(8,128)S(1)}, f32[256,128]{1,0:T(8,128)S(1)}, u32[]{:S(2)}, u32[]{:S(2)}) %collective-permute-start.12) | collective-permute-done | bytes 131104 | tf_op jit(solution)/shard_map/ppermute | solution.py:311
  49.6 1.6 %collective-permute-done.11.c.refs_7_ = f32[256,128]{1,0:T(8,128)S(1)} collective-permute-done((f32[256,128]{1,0:T(8,128)S(1)}, f32[256,128]{1,0:T(8,128)S(1)}, u32[]{:S(2)}, u32[]{:S(2)}) %collective-permute-start.11) | collective-permute-done | bytes 131104 | tf_op jit(solution)/shard_map/ppermute | solution.py:311
  51.5 1.4 %shard_map.49.before_ref = f32[168,128]{1,0:T(8,128)S(1)} custom-call(f32[256,128]{1,0:T(8,128)S(1)} %collective-permute-done.10.b.refs_6_, f32[256,128]{1,0:T(8,128)S(1)} %collective-permute-done.11.c.refs_7_, f32[256,128]{1,0:T(8,128)S(1)} %collective-permute-done.12.d.refs_8_, f32[168,128]{1,0:T(8,128)S(1)} %shard_map.47.after_ref.before_ref, ...), custom_call_target="tpu_custom_call" | custom-call | tf_op jit(solution)/shard_map/pallas_call | solution.py:285
  53.4 1.8 %shard_map.50.a = f32[168,128]{1,0:T(8,128)S(1)} custom-call(f32[4,256,128]{2,1,0:T(8,128)S(1)} %collective-permute-done.13.p_ref.refs_9_, f32[168,128]{1,0:T(8,128)S(1)} %shard_map.49.before_ref, bf16[8192,1280]{1,0:T(8,128)(2,1)S(1)} %get-tuple-element.14.pair_ref), custom_call_target="tpu_custom_call" | custom-call | tf_op jit(solution)/shard_map/pallas_call | solution.py:285
  55.2 1.6 %collective-permute-start.16 = (f32[168,128]{1,0:T(8,128)S(1)}, f32[168,128]{1,0:T(8,128)S(1)}, u32[]{:S(2)}, u32[]{:S(2)}) collective-permute-start(f32[168,128]{1,0:T(8,128)S(1)} %shard_map.50.a), channel_id=1, source_target_pairs={{0,2},{1,3},{2,0},{3,1},{4,6},{5,7},{6,4},{7,5},{8,10},{9,11},{10,... | collective-permute-start | bytes 258056 | tf_op jit(solution)/shard_map/ppermute | solution.py:311
  56.8 1.4 %collective-permute-start.15 = (f32[168,128]{1,0:T(8,128)S(1)}, f32[168,128]{1,0:T(8,128)S(1)}, u32[]{:S(2)}, u32[]{:S(2)}) collective-permute-start(f32[168,128]{1,0:T(8,128)S(1)} %shard_map.50.a), channel_id=1, source_target_pairs={{0,3},{1,2},{2,1},{3,0},{4,7},{5,6},{6,5},{7,4},{8,11},{9,10},{10,... | collective-permute-start | bytes 258056 | tf_op jit(solution)/shard_map/ppermute | solution.py:311
  58.8 2.7 %collective-permute-done.16.d = f32[168,128]{1,0:T(8,128)S(1)} collective-permute-done((f32[168,128]{1,0:T(8,128)S(1)}, f32[168,128]{1,0:T(8,128)S(1)}, u32[]{:S(2)}, u32[]{:S(2)}) %collective-permute-start.16) | collective-permute-done | bytes 86048 | tf_op jit(solution)/shard_map/ppermute | solution.py:311
  61.4 1.7 %collective-permute-done.15.c = f32[168,128]{1,0:T(8,128)S(1)} collective-permute-done((f32[168,128]{1,0:T(8,128)S(1)}, f32[168,128]{1,0:T(8,128)S(1)}, u32[]{:S(2)}, u32[]{:S(2)}) %collective-permute-start.15) | collective-permute-done | bytes 86048 | tf_op jit(solution)/shard_map/ppermute | solution.py:311
  63.2 2.3 %shard_map.51 = (f32[4,264,128]{2,1,0:T(8,128)S(1)}, f32[32,640]{1,0:T(8,128)S(1)}, f32[32,128]{1,0:T(8,128)S(1)}) custom-call(f32[168,128]{1,0:T(8,128)S(1)} %shard_map.50.a, f32[168,128]{1,0:T(8,128)S(1)} %collective-permute-done.14.b, f32[168,128]{1,0:T(8,128)S(1)} %collective-permute-done.15.c, f32[168,128]{1,0:T(8,128)S(1)} %collective-permute-done.16.d, ...), custom_call_target="tpu_custom_call" | custom-call | tf_op jit(solution)/shard_map/pallas_call | solution.py:238
  65.7 2.4 %shard_map.52 = f32[3,264,128]{2,1,0:T(8,128)S(1)} custom-call(f32[32,640]{1,0:T(8,128)S(1)} %get-tuple-element.20.d_ref.refs_16_, bf16[8192,1280]{1,0:T(8,128)(2,1)S(1)} %get-tuple-element.14.pair_ref), custom_call_target="tpu_custom_call" | custom-call | tf_op jit(solution)/shard_map/pallas_call | solution.py:238
  68.1 1.9 %collective-permute-start.19 = (f32[264,128]{1,0:T(8,128)S(1)}, f32[264,128]{1,0:T(8,128)S(1)}, u32[]{:S(2)}, u32[]{:S(2)}) collective-permute-start(f32[264,128]{1,0:T(8,128)S(1)} %get-tuple-element.24), channel_id=1, source_target_pairs={{0,64},{4,20},{8,72},{12,28},{16,80},{20,4},{24,88},{28,12},{32,96... | collective-permute-start | bytes 405512 | tf_op jit(solution)/shard_map/ppermute | solution.py:311
  70.1 1.2 %collective-permute-start.20 = (f32[264,128]{1,0:T(8,128)S(1)}, f32[264,128]{1,0:T(8,128)S(1)}, u32[]{:S(2)}, u32[]{:S(2)}) collective-permute-start(f32[264,128]{1,0:T(8,128)S(1)} %get-tuple-element.25), channel_id=1, source_target_pairs={{0,96},{4,28},{8,104},{12,20},{16,112},{20,12},{24,120},{28,4},{32... | collective-permute-start | bytes 405512 | tf_op jit(solution)/shard_map/ppermute | solution.py:311
  71.7 1.1 %shard_map.53 = f32[264,128]{1,0:T(8,128)S(1)} custom-call(f32[32,640]{1,0:T(8,128)S(1)} %get-tuple-element.20.d_ref.refs_16_, f32[264,128]{1,0:T(8,128)S(1)} %get-tuple-element.26.after_ref, bf16[8192,1280]{1,0:T(8,128)(2,1)S(1)} %get-tuple-element.14.pair_ref), custom_call_target="tpu_custom_call" | custom-call | tf_op jit(solution)/shard_map/pallas_call | solution.py:238
  72.8 2.0 %collective-permute-done.19 = f32[264,128]{1,0:T(8,128)S(1)} collective-permute-done((f32[264,128]{1,0:T(8,128)S(1)}, f32[264,128]{1,0:T(8,128)S(1)}, u32[]{:S(2)}, u32[]{:S(2)}) %collective-permute-start.19) | collective-permute-done | bytes 135200 | tf_op jit(solution)/shard_map/ppermute | solution.py:311
  74.7 1.6 %collective-permute-done.20 = f32[264,128]{1,0:T(8,128)S(1)} collective-permute-done((f32[264,128]{1,0:T(8,128)S(1)}, f32[264,128]{1,0:T(8,128)S(1)}, u32[]{:S(2)}, u32[]{:S(2)}) %collective-permute-start.20) | collective-permute-done | bytes 135200 | tf_op jit(solution)/shard_map/ppermute | solution.py:311
  76.3 1.5 %collective-permute-start.23 = (f32[264,128]{1,0:T(8,128)S(1)}, f32[264,128]{1,0:T(8,128)S(1)}, u32[]{:S(2)}, u32[]{:S(2)}) collective-permute-start(f32[264,128]{1,0:T(8,128)S(1)} %fusion.2.a), channel_id=1, source_target_pairs={{0,16},{4,68},{8,24},{12,76},{16,0},{20,84},{24,8},{28,92},{32,48}... | collective-permute-start | bytes 405512 | tf_op jit(solution)/shard_map/ppermute | solution.py:311
  77.9 1.5 %collective-permute-start.22 = (f32[264,128]{1,0:T(8,128)S(1)}, f32[264,128]{1,0:T(8,128)S(1)}, u32[]{:S(2)}, u32[]{:S(2)}) collective-permute-start(f32[264,128]{1,0:T(8,128)S(1)} %fusion.2.a), channel_id=1, source_target_pairs={{0,24},{4,100},{8,16},{12,108},{16,8},{20,116},{24,0},{28,124},{32... | collective-permute-start | bytes 405512 | tf_op jit(solution)/shard_map/ppermute | solution.py:311
  79.4 0.5 collective-permute-start.21
  79.9 3.1 %collective-permute-done.23.d = f32[264,128]{1,0:T(8,128)S(1)} collective-permute-done((f32[264,128]{1,0:T(8,128)S(1)}, f32[264,128]{1,0:T(8,128)S(1)}, u32[]{:S(2)}, u32[]{:S(2)}) %collective-permute-start.23) | collective-permute-done | bytes 135200 | tf_op jit(solution)/shard_map/ppermute | solution.py:311
  83.0 1.4 %collective-permute-done.22.c = f32[264,128]{1,0:T(8,128)S(1)} collective-permute-done((f32[264,128]{1,0:T(8,128)S(1)}, f32[264,128]{1,0:T(8,128)S(1)}, u32[]{:S(2)}, u32[]{:S(2)}) %collective-permute-start.22) | collective-permute-done | bytes 135200 | tf_op jit(solution)/shard_map/ppermute | solution.py:311
  84.6 1.9 %collective-permute-start.26 = (f32[256,128]{1,0:T(8,128)S(1)}, f32[256,128]{1,0:T(8,128)S(1)}, u32[]{:S(2)}, u32[]{:S(2)}) collective-permute-start(f32[256,128]{1,0:T(8,128)S(1)} %get-tuple-element.23.a.refs_10_), channel_id=1, source_target_pairs={{0,64},{4,20},{8,72},{12,28},{16,80},{20,4},{24,88},{28,12},{32,96... | collective-permute-start | bytes 393224 | tf_op jit(solution)/shard_map/ppermute | solution.py:311
  86.5 1.2 %collective-permute-start.25 = (f32[256,128]{1,0:T(8,128)S(1)}, f32[256,128]{1,0:T(8,128)S(1)}, u32[]{:S(2)}, u32[]{:S(2)}) collective-permute-start(f32[256,128]{1,0:T(8,128)S(1)} %get-tuple-element.23.a.refs_10_), channel_id=1, source_target_pairs={{0,96},{4,28},{8,104},{12,20},{16,112},{20,12},{24,120},{28,4},{32... | collective-permute-start | bytes 393224 | tf_op jit(solution)/shard_map/ppermute | solution.py:311
  88.1 3.0 %collective-permute-done.26.d.refs_13_ = f32[256,128]{1,0:T(8,128)S(1)} collective-permute-done((f32[256,128]{1,0:T(8,128)S(1)}, f32[256,128]{1,0:T(8,128)S(1)}, u32[]{:S(2)}, u32[]{:S(2)}) %collective-permute-start.26) | collective-permute-done | bytes 131104 | tf_op jit(solution)/shard_map/ppermute | solution.py:311
  91.1 1.6 %collective-permute-done.25.c.refs_12_ = f32[256,128]{1,0:T(8,128)S(1)} collective-permute-done((f32[256,128]{1,0:T(8,128)S(1)}, f32[256,128]{1,0:T(8,128)S(1)}, u32[]{:S(2)}, u32[]{:S(2)}) %collective-permute-start.25) | collective-permute-done | bytes 131104 | tf_op jit(solution)/shard_map/ppermute | solution.py:311
  93.4 1.3 %collective-permute-done.27 = f32[8,128]{1,0:T(8,128)S(1)} collective-permute-done((f32[8,128]{1,0:T(8,128)S(1)}, f32[8,128]{1,0:T(8,128)S(1)}, u32[]{:S(2)}, u32[]{:S(2)}) %collective-permute-start.27) | collective-permute-done | bytes 4128 | tf_op jit(solution)/shard_map/ppermute | solution.py:437
  94.7 1.5 %collective-permute-start.30 = (f32[8,128]{1,0:T(8,128)S(1)}, f32[8,128]{1,0:T(8,128)S(1)}, u32[]{:S(2)}, u32[]{:S(2)}) collective-permute-start(f32[8,128]{1,0:T(8,128)S(1)} %add.90), channel_id=1, source_target_pairs={{0,2},{1,3},{2,0},{3,1},{4,6},{5,7},{6,4},{7,5},{8,10},{9,11},{10,... | collective-permute-start | bytes 12296 | tf_op jit(solution)/shard_map/ppermute | solution.py:311
  96.3 1.4 %collective-permute-start.29 = (f32[8,128]{1,0:T(8,128)S(1)}, f32[8,128]{1,0:T(8,128)S(1)}, u32[]{:S(2)}, u32[]{:S(2)}) collective-permute-start(f32[8,128]{1,0:T(8,128)S(1)} %add.90), channel_id=1, source_target_pairs={{0,3},{1,2},{2,1},{3,0},{4,7},{5,6},{6,5},{7,4},{8,11},{9,10},{10,... | collective-permute-start | bytes 12296 | tf_op jit(solution)/shard_map/ppermute | solution.py:311
  98.2 1.6 %collective-permute-done.30 = f32[8,128]{1,0:T(8,128)S(1)} collective-permute-done((f32[8,128]{1,0:T(8,128)S(1)}, f32[8,128]{1,0:T(8,128)S(1)}, u32[]{:S(2)}, u32[]{:S(2)}) %collective-permute-start.30) | collective-permute-done | bytes 4128 | tf_op jit(solution)/shard_map/ppermute | solution.py:311
  99.8 1.2 %collective-permute-done.29 = f32[8,128]{1,0:T(8,128)S(1)} collective-permute-done((f32[8,128]{1,0:T(8,128)S(1)}, f32[8,128]{1,0:T(8,128)S(1)}, u32[]{:S(2)}, u32[]{:S(2)}) %collective-permute-start.29) | collective-permute-done | bytes 4128 | tf_op jit(solution)/shard_map/ppermute | solution.py:311
  101.3 1.4 %shard_map.57 = (f32[32,640]{1,0:T(8,128)}, f32[32,8192]{1,0:T(8,128)}) custom-call(f32[32,8192]{1,0:T(8,128)S(1)} %copy-done, f32[32,128]{1,0:T(8,128)S(1)} %get-tuple-element.19.refs_1_, f32[32,128]{1,0:T(8,128)S(1)} %get-tuple-element.18.gamma_ref.gamma0_ref.refs_2_, f32[32,128]{1,0:T(8,128)S(1)} %get-tuple-element.22.after_ref.refs_3_, ...), custom_call_target="tpu_custom_call" | custom-call | tf_op jit(solution)/shard_map/pallas_call | solution.py:441
  (41 shorter events, 5.7 us)
Async XLA Ops:
  9.6 6.7 %collective-permute-start.2 = (f32[32,640]{1,0:T(8,128)S(1)}, f32[32,640]{1,0:T(8,128)S(1)}, u32[]{:S(2)}, u32[]{:S(2)}) collective-permute-start(f32[32,640]{1,0:T(8,128)S(1)} %get-tuple-element.13.a), channel_id=1, source_target_pairs={{0,2},{1,3},{2,0},{3,1},{4,6},{5,7},{6,4},{7,5},{8,10},{9,11},{10,... | collective-permute-start | bytes 245768 | tf_op jit(solution)/shard_map/ppermute | solution.py:311
  13.0 5.7 %collective-permute-start.1 = (f32[32,640]{1,0:T(8,128)S(1)}, f32[32,640]{1,0:T(8,128)S(1)}, u32[]{:S(2)}, u32[]{:S(2)}) collective-permute-start(f32[32,640]{1,0:T(8,128)S(1)} %get-tuple-element.13.a), channel_id=1, source_target_pairs={{0,3},{1,2},{2,1},{3,0},{4,7},{5,6},{6,5},{7,4},{8,11},{9,10},{10,... | collective-permute-start | bytes 245768 | tf_op jit(solution)/shard_map/ppermute | solution.py:311
  14.0 4.6 %collective-permute-start = (f32[32,640]{1,0:T(8,128)S(1)}, f32[32,640]{1,0:T(8,128)S(1)}, u32[]{:S(2)}, u32[]{:S(2)}) collective-permute-start(f32[32,640]{1,0:T(8,128)S(1)} %get-tuple-element.13.a), channel_id=1, source_target_pairs={{0,1},{1,0},{2,3},{3,2},{4,5},{5,4},{6,7},{7,6},{8,9},{9,8},{10,11... | collective-permute-start | bytes 245768 | tf_op jit(solution)/shard_map/ppermute | solution.py:311
  20.9 2.5 %collective-permute-start.3 = (f32[4,264,128]{2,1,0:T(8,128)S(1)}, f32[4,264,128]{2,1,0:T(8,128)S(1)}, u32[]{:S(2)}, u32[]{:S(2)}) collective-permute-start(f32[4,264,128]{2,1,0:T(8,128)S(1)} %get-tuple-element.16), channel_id=1, source_target_pairs={{0,4},{4,0},{8,12},{12,8},{16,20},{20,16},{24,28},{28,24},{32,36},... | collective-permute-start | bytes 1622024 | tf_op jit(solution)/shard_map/ppermute | solution.py:332
  23.4 6.9 %collective-permute-start.5 = (f32[264,128]{1,0:T(8,128)S(1)}, f32[264,128]{1,0:T(8,128)S(1)}, u32[]{:S(2)}, u32[]{:S(2)}) collective-permute-start(f32[264,128]{1,0:T(8,128)S(1)} %get-tuple-element.27), channel_id=1, source_target_pairs={{0,64},{4,20},{8,72},{12,28},{16,80},{20,4},{24,88},{28,12},{32,96... | collective-permute-start | bytes 405512 | tf_op jit(solution)/shard_map/ppermute | solution.py:311
  27.4 6.2 %collective-permute-start.6 = (f32[264,128]{1,0:T(8,128)S(1)}, f32[264,128]{1,0:T(8,128)S(1)}, u32[]{:S(2)}, u32[]{:S(2)}) collective-permute-start(f32[264,128]{1,0:T(8,128)S(1)} %get-tuple-element.28), channel_id=1, source_target_pairs={{0,96},{4,28},{8,104},{12,20},{16,112},{20,12},{24,120},{28,4},{32... | collective-permute-start | bytes 405512 | tf_op jit(solution)/shard_map/ppermute | solution.py:311
  28.1 5.5 %collective-permute-start.4 = (f32[264,128]{1,0:T(8,128)S(1)}, f32[264,128]{1,0:T(8,128)S(1)}, u32[]{:S(2)}, u32[]{:S(2)}) collective-permute-start(f32[264,128]{1,0:T(8,128)S(1)} %get-tuple-element.29.after_ref), channel_id=1, source_target_pairs={{0,32},{4,12},{8,40},{12,4},{16,48},{20,28},{24,56},{28,20},{32,0}... | collective-permute-start | bytes 405512 | tf_op jit(solution)/shard_map/ppermute | solution.py:311
  33.7 6.6 %collective-permute-start.9 = (f32[264,128]{1,0:T(8,128)S(1)}, f32[264,128]{1,0:T(8,128)S(1)}, u32[]{:S(2)}, u32[]{:S(2)}) collective-permute-start(f32[264,128]{1,0:T(8,128)S(1)} %fusion.8.a), channel_id=1, source_target_pairs={{0,16},{4,68},{8,24},{12,76},{16,0},{20,84},{24,8},{28,92},{32,48}... | collective-permute-start | bytes 405512 | tf_op jit(solution)/shard_map/ppermute | solution.py:311
  36.8 6.2 %collective-permute-start.8 = (f32[264,128]{1,0:T(8,128)S(1)}, f32[264,128]{1,0:T(8,128)S(1)}, u32[]{:S(2)}, u32[]{:S(2)}) collective-permute-start(f32[264,128]{1,0:T(8,128)S(1)} %fusion.8.a), channel_id=1, source_target_pairs={{0,24},{4,100},{8,16},{12,108},{16,8},{20,116},{24,0},{28,124},{32... | collective-permute-start | bytes 405512 | tf_op jit(solution)/shard_map/ppermute | solution.py:311
  37.9 5.1 %collective-permute-start.7 = (f32[264,128]{1,0:T(8,128)S(1)}, f32[264,128]{1,0:T(8,128)S(1)}, u32[]{:S(2)}, u32[]{:S(2)}) collective-permute-start(f32[264,128]{1,0:T(8,128)S(1)} %fusion.8.a), channel_id=1, source_target_pairs={{0,8},{4,36},{8,0},{12,44},{16,24},{20,52},{24,16},{28,60},{32,40}... | collective-permute-start | bytes 405512 | tf_op jit(solution)/shard_map/ppermute | solution.py:311
  43.1 6.5 %collective-permute-start.12 = (f32[256,128]{1,0:T(8,128)S(1)}, f32[256,128]{1,0:T(8,128)S(1)}, u32[]{:S(2)}, u32[]{:S(2)}) collective-permute-start(f32[256,128]{1,0:T(8,128)S(1)} %get-tuple-element.17.p_ref.a.before_ref.refs_5_), channel_id=1, source_target_pairs={{0,64},{4,20},{8,72},{12,28},{16,80},{20,4},{24,88},{28,12},{32,96... | collective-permute-start | bytes 393224 | tf_op jit(solution)/shard_map/ppermute | solution.py:311
  45.0 6.2 %collective-permute-start.11 = (f32[256,128]{1,0:T(8,128)S(1)}, f32[256,128]{1,0:T(8,128)S(1)}, u32[]{:S(2)}, u32[]{:S(2)}) collective-permute-start(f32[256,128]{1,0:T(8,128)S(1)} %get-tuple-element.17.p_ref.a.before_ref.refs_5_), channel_id=1, source_target_pairs={{0,96},{4,28},{8,104},{12,20},{16,112},{20,12},{24,120},{28,4},{32... | collective-permute-start | bytes 393224 | tf_op jit(solution)/shard_map/ppermute | solution.py:311
  46.1 5.1 %collective-permute-start.10 = (f32[256,128]{1,0:T(8,128)S(1)}, f32[256,128]{1,0:T(8,128)S(1)}, u32[]{:S(2)}, u32[]{:S(2)}) collective-permute-start(f32[256,128]{1,0:T(8,128)S(1)} %get-tuple-element.17.p_ref.a.before_ref.refs_5_), channel_id=1, source_target_pairs={{0,32},{4,12},{8,40},{12,4},{16,48},{20,28},{24,56},{28,20},{32,0}... | collective-permute-start | bytes 393224 | tf_op jit(solution)/shard_map/ppermute | solution.py:311
  51.2 2.2 %collective-permute-start.13 = (f32[4,256,128]{2,1,0:T(8,128)S(1)}, f32[4,256,128]{2,1,0:T(8,128)S(1)}, u32[]{:S(2)}, u32[]{:S(2)}) collective-permute-start(f32[4,256,128]{2,1,0:T(8,128)S(1)} %shard_map.48), channel_id=1, source_target_pairs={{0,4},{4,0},{8,12},{12,8},{16,20},{20,16},{24,28},{28,24},{32,36},... | collective-permute-start | bytes 1572872 | tf_op jit(solution)/shard_map/ppermute | solution.py:419
  55.2 6.3 %collective-permute-start.16 = (f32[168,128]{1,0:T(8,128)S(1)}, f32[168,128]{1,0:T(8,128)S(1)}, u32[]{:S(2)}, u32[]{:S(2)}) collective-permute-start(f32[168,128]{1,0:T(8,128)S(1)} %shard_map.50.a), channel_id=1, source_target_pairs={{0,2},{1,3},{2,0},{3,1},{4,6},{5,7},{6,4},{7,5},{8,10},{9,11},{10,... | collective-permute-start | bytes 258056 | tf_op jit(solution)/shard_map/ppermute | solution.py:311
  56.8 6.4 %collective-permute-start.15 = (f32[168,128]{1,0:T(8,128)S(1)}, f32[168,128]{1,0:T(8,128)S(1)}, u32[]{:S(2)}, u32[]{:S(2)}) collective-permute-start(f32[168,128]{1,0:T(8,128)S(1)} %shard_map.50.a), channel_id=1, source_target_pairs={{0,3},{1,2},{2,1},{3,0},{4,7},{5,6},{6,5},{7,4},{8,11},{9,10},{10,... | collective-permute-start | bytes 258056 | tf_op jit(solution)/shard_map/ppermute | solution.py:311
  58.2 5.0 %collective-permute-start.14 = (f32[168,128]{1,0:T(8,128)S(1)}, f32[168,128]{1,0:T(8,128)S(1)}, u32[]{:S(2)}, u32[]{:S(2)}) collective-permute-start(f32[168,128]{1,0:T(8,128)S(1)} %shard_map.50.a), channel_id=1, source_target_pairs={{0,1},{1,0},{2,3},{3,2},{4,5},{5,4},{6,7},{7,6},{8,9},{9,8},{10,11... | collective-permute-start | bytes 258056 | tf_op jit(solution)/shard_map/ppermute | solution.py:311
  65.6 2.5 %collective-permute-start.17 = (f32[4,264,128]{2,1,0:T(8,128)S(1)}, f32[4,264,128]{2,1,0:T(8,128)S(1)}, u32[]{:S(2)}, u32[]{:S(2)}) collective-permute-start(f32[4,264,128]{2,1,0:T(8,128)S(1)} %get-tuple-element.21), channel_id=1, source_target_pairs={{0,4},{4,0},{8,12},{12,8},{16,20},{20,16},{24,28},{28,24},{32,36},... | collective-permute-start | bytes 1622024 | tf_op jit(solution)/shard_map/ppermute | solution.py:332
  65.6 35.7 %copy-start = (f32[32,8192]{1,0:T(8,128)S(1)}, f32[32,8192]{1,0:T(8,128)}, u32[]{:S(2)}) copy-start(f32[32,8192]{1,0:T(8,128)} %refs_0_.1) | copy-start | bytes 3145732
  68.1 6.6 %collective-permute-start.19 = (f32[264,128]{1,0:T(8,128)S(1)}, f32[264,128]{1,0:T(8,128)S(1)}, u32[]{:S(2)}, u32[]{:S(2)}) collective-permute-start(f32[264,128]{1,0:T(8,128)S(1)} %get-tuple-element.24), channel_id=1, source_target_pairs={{0,64},{4,20},{8,72},{12,28},{16,80},{20,4},{24,88},{28,12},{32,96... | collective-permute-start | bytes 405512 | tf_op jit(solution)/shard_map/ppermute | solution.py:311
  70.1 6.2 %collective-permute-start.20 = (f32[264,128]{1,0:T(8,128)S(1)}, f32[264,128]{1,0:T(8,128)S(1)}, u32[]{:S(2)}, u32[]{:S(2)}) collective-permute-start(f32[264,128]{1,0:T(8,128)S(1)} %get-tuple-element.25), channel_id=1, source_target_pairs={{0,96},{4,28},{8,104},{12,20},{16,112},{20,12},{24,120},{28,4},{32... | collective-permute-start | bytes 405512 | tf_op jit(solution)/shard_map/ppermute | solution.py:311
  71.3 5.0 %collective-permute-start.18 = (f32[264,128]{1,0:T(8,128)S(1)}, f32[264,128]{1,0:T(8,128)S(1)}, u32[]{:S(2)}, u32[]{:S(2)}) collective-permute-start(f32[264,128]{1,0:T(8,128)S(1)} %get-tuple-element.26.after_ref), channel_id=1, source_target_pairs={{0,32},{4,12},{8,40},{12,4},{16,48},{20,28},{24,56},{28,20},{32,0}... | collective-permute-start | bytes 405512 | tf_op jit(solution)/shard_map/ppermute | solution.py:311
  76.3 6.6 %collective-permute-start.23 = (f32[264,128]{1,0:T(8,128)S(1)}, f32[264,128]{1,0:T(8,128)S(1)}, u32[]{:S(2)}, u32[]{:S(2)}) collective-permute-start(f32[264,128]{1,0:T(8,128)S(1)} %fusion.2.a), channel_id=1, source_target_pairs={{0,16},{4,68},{8,24},{12,76},{16,0},{20,84},{24,8},{28,92},{32,48}... | collective-permute-start | bytes 405512 | tf_op jit(solution)/shard_map/ppermute | solution.py:311
  77.9 6.5 %collective-permute-start.22 = (f32[264,128]{1,0:T(8,128)S(1)}, f32[264,128]{1,0:T(8,128)S(1)}, u32[]{:S(2)}, u32[]{:S(2)}) collective-permute-start(f32[264,128]{1,0:T(8,128)S(1)} %fusion.2.a), channel_id=1, source_target_pairs={{0,24},{4,100},{8,16},{12,108},{16,8},{20,116},{24,0},{28,124},{32... | collective-permute-start | bytes 405512 | tf_op jit(solution)/shard_map/ppermute | solution.py:311
  79.4 5.0 %collective-permute-start.21 = (f32[264,128]{1,0:T(8,128)S(1)}, f32[264,128]{1,0:T(8,128)S(1)}, u32[]{:S(2)}, u32[]{:S(2)}) collective-permute-start(f32[264,128]{1,0:T(8,128)S(1)} %fusion.2.a), channel_id=1, source_target_pairs={{0,8},{4,36},{8,0},{12,44},{16,24},{20,52},{24,16},{28,60},{32,40}... | collective-permute-start | bytes 405512 | tf_op jit(solution)/shard_map/ppermute | solution.py:311
  84.6 6.6 %collective-permute-start.26 = (f32[256,128]{1,0:T(8,128)S(1)}, f32[256,128]{1,0:T(8,128)S(1)}, u32[]{:S(2)}, u32[]{:S(2)}) collective-permute-start(f32[256,128]{1,0:T(8,128)S(1)} %get-tuple-element.23.a.refs_10_), channel_id=1, source_target_pairs={{0,64},{4,20},{8,72},{12,28},{16,80},{20,4},{24,88},{28,12},{32,96... | collective-permute-start | bytes 393224 | tf_op jit(solution)/shard_map/ppermute | solution.py:311
  86.5 6.2 %collective-permute-start.25 = (f32[256,128]{1,0:T(8,128)S(1)}, f32[256,128]{1,0:T(8,128)S(1)}, u32[]{:S(2)}, u32[]{:S(2)}) collective-permute-start(f32[256,128]{1,0:T(8,128)S(1)} %get-tuple-element.23.a.refs_10_), channel_id=1, source_target_pairs={{0,96},{4,28},{8,104},{12,20},{16,112},{20,12},{24,120},{28,4},{32... | collective-permute-start | bytes 393224 | tf_op jit(solution)/shard_map/ppermute | solution.py:311
  87.7 5.0 %collective-permute-start.24 = (f32[256,128]{1,0:T(8,128)S(1)}, f32[256,128]{1,0:T(8,128)S(1)}, u32[]{:S(2)}, u32[]{:S(2)}) collective-permute-start(f32[256,128]{1,0:T(8,128)S(1)} %get-tuple-element.23.a.refs_10_), channel_id=1, source_target_pairs={{0,32},{4,12},{8,40},{12,4},{16,48},{20,28},{24,56},{28,20},{32,0}... | collective-permute-start | bytes 393224 | tf_op jit(solution)/shard_map/ppermute | solution.py:311
  92.7 8.6 %collective-permute-start.31 = (f32[4,256,128]{2,1,0:T(8,128)S(1)}, f32[4,256,128]{2,1,0:T(8,128)S(1)}, u32[]{:S(2)}, u32[]{:S(2)}) collective-permute-start(f32[4,256,128]{2,1,0:T(8,128)S(1)} %shard_map.56), channel_id=1, source_target_pairs={{0,4},{4,0},{8,12},{12,8},{16,20},{20,16},{24,28},{28,24},{32,36},... | collective-permute-start | bytes 1572872 | tf_op jit(solution)/shard_map/ppermute | solution.py:439
  92.9 1.8 %collective-permute-start.27 = (f32[8,128]{1,0:T(8,128)S(1)}, f32[8,128]{1,0:T(8,128)S(1)}, u32[]{:S(2)}, u32[]{:S(2)}) collective-permute-start(f32[8,128]{1,0:T(8,128)S(1)} %shard_map.55), channel_id=1, source_target_pairs={{0,4},{4,0},{8,12},{12,8},{16,20},{20,16},{24,28},{28,24},{32,36},... | collective-permute-start | bytes 12296 | tf_op jit(solution)/shard_map/ppermute | solution.py:437
  94.7 5.1 %collective-permute-start.30 = (f32[8,128]{1,0:T(8,128)S(1)}, f32[8,128]{1,0:T(8,128)S(1)}, u32[]{:S(2)}, u32[]{:S(2)}) collective-permute-start(f32[8,128]{1,0:T(8,128)S(1)} %add.90), channel_id=1, source_target_pairs={{0,2},{1,3},{2,0},{3,1},{4,6},{5,7},{6,4},{7,5},{8,10},{9,11},{10,... | collective-permute-start | bytes 12296 | tf_op jit(solution)/shard_map/ppermute | solution.py:311
  96.3 4.8 %collective-permute-start.29 = (f32[8,128]{1,0:T(8,128)S(1)}, f32[8,128]{1,0:T(8,128)S(1)}, u32[]{:S(2)}, u32[]{:S(2)}) collective-permute-start(f32[8,128]{1,0:T(8,128)S(1)} %add.90), channel_id=1, source_target_pairs={{0,3},{1,2},{2,1},{3,0},{4,7},{5,6},{6,5},{7,4},{8,11},{9,10},{10,... | collective-permute-start | bytes 12296 | tf_op jit(solution)/shard_map/ppermute | solution.py:311
  97.7 3.6 %collective-permute-start.28 = (f32[8,128]{1,0:T(8,128)S(1)}, f32[8,128]{1,0:T(8,128)S(1)}, u32[]{:S(2)}, u32[]{:S(2)}) collective-permute-start(f32[8,128]{1,0:T(8,128)S(1)} %add.90), channel_id=1, source_target_pairs={{0,1},{1,0},{2,3},{3,2},{4,5},{5,4},{6,7},{7,6},{8,9},{9,8},{10,11... | collective-permute-start | bytes 12296 | tf_op jit(solution)/shard_map/ppermute | solution.py:311
